TPU v7x, 128 devices: a whole 4x4x4 slice. The times are simulated.
128 devices in a mesh: ctx: 8 (over x, z_lo), fsdp: 16 (over y, z_hi, core).
Axes of the slice: x: 4, y: 4, z: 4 (z_hi: 2, z_lo: 2; z = z_hi * 2 + z_lo), core: 2. Of those that a mesh axis runs over, the one named last changes fastest.
Arguments:
- hidden: bfloat16 [16, 2048, 8192], P('fsdp', 'ctx'), may hold values from -6 to 6
- queries: bfloat16 [16, 2048, 4096], P('fsdp', 'ctx'), may hold values from -300 to 300
- conv_input: bfloat16 [16, 2048, 8192], P('fsdp', 'ctx'), may hold values from -6 to 6
- norm_gain: float32 [8192], replicated, may hold values from 0.1 to 1.9
- kv_weight: bfloat16 [8192, 1024], P('fsdp'), may hold values from -0.0625 to 0.0625
- conv_weight: float32 [4, 8192], replicated, may hold values from -3 to 3
- conv_bias: float32 [8192], replicated, may hold values from -3 to 3
- starts: int32 [16, 8], P('fsdp'), may hold values from 0 to 2047, as said below
- segment_ids: int32 [16, 2048], P('fsdp', 'ctx'), may hold values from 0 to 7, as said below
Outputs:
- attended: bfloat16 [16, 2048, 4096], P('fsdp', 'ctx')
- conv_out: bfloat16 [16, 2048, 8192], P('fsdp', 'ctx')
Inputs may be any that keep to these rules, and one draw needn't show every extreme that they name: Each row lists its 8 episode starts in increasing order, the first one 0 and the last one 2048 - 1; one episode of each row holds at least 1024 positions. `segment_ids`: in each row the ids start at 0 and rise by one at each of the row's starts.
All inputs are finite; a program needn't handle non-finite values.
Results may differ from a plain program's by a relative error of at most 0.011.
Values may be sent and summed in bfloat16 or wider, within the bound.
No kernel may reach another device: no remote copies, remote signals or barrier semaphores. Data moves between devices by JAX's collectives and lax.ppermute only.
A program may use at most 128 MiB of HBM per device.

v0:
```python
import math

import jax
import jax.numpy as jnp
from jax import lax
from jax.sharding import PartitionSpec as P

HEAD = 128
TAPS = 4


def passed_along(x, axis, by):
    devices = lax.axis_size(axis)
    pairs = [(i, i + by) for i in range(devices) if 0 <= i + by < devices]
    return lax.ppermute(x, axis, pairs)


def body(
    hidden, queries, conv_input, norm_gain, kv_weight, conv_weight, conv_bias, starts, segment_ids
):
    shard_len = hidden.shape[1]
    cycle_index = lax.axis_index("ctx")
    features = hidden[0].astype(jnp.float32)
    normed = (
        features
        * lax.rsqrt(jnp.mean(features * features, axis=-1, keepdims=True) + 1e-06)
        * norm_gain
    ).astype(jnp.bfloat16)
    kv_width = kv_weight.shape[1]
    kv_total = jnp.dot(
        normed,
        lax.all_gather(kv_weight, "fsdp", axis=0, tiled=True),
        preferred_element_type=jnp.float32,
    )
    key_value = kv_total.astype(jnp.bfloat16)
    local_seg = segment_ids[0]
    episode_list = starts[0]
    positions = cycle_index * shard_len + jnp.arange(shard_len, dtype=jnp.int32)
    episode_start = jnp.max(
        jnp.where(episode_list[None, :] <= positions[:, None], episode_list[None, :], 0), axis=1
    )
    signal = conv_input[0]
    tail_rows = passed_along(signal[shard_len - (TAPS - 1) :], "ctx", 1)
    extended = jnp.concatenate([tail_rows, signal], axis=0)
    mixing = jnp.zeros(signal.shape, jnp.float32) + conv_bias[None, :]
    for tap in range(TAPS):
        source = positions - (TAPS - 1) + tap
        valid = (source >= episode_start)[:, None]
        mixing = (
            mixing
            + jnp.where(valid, extended[tap : tap + shard_len].astype(jnp.float32), 0.0)
            * conv_weight[tap][None, :]
        )
    conv_out = jax.nn.silu(mixing).astype(jnp.bfloat16)
    kv_heads = kv_width // (2 * HEAD)
    per_group = queries.shape[2] // HEAD // kv_heads
    query_rows = queries[0]
    query_heads = query_rows.reshape(shard_len, kv_heads, per_group, HEAD)
    scale = 1.0 / math.sqrt(HEAD)
    last_query = jnp.max(positions)
    lowest_seg = jnp.min(local_seg)
    highest_seg = jnp.max(local_seg)

    def absorb(carry, key_block, value_block, key_seg, key_pos):
        running_max, running_total, summed = carry
        scores = (
            jnp.einsum("tkgd,skd->tkgs", query_heads, key_block, preferred_element_type=jnp.float32)
            * scale
        )
        allowed = (key_pos[None, :] <= positions[:, None]) & (
            key_seg[None, :] == local_seg[:, None]
        )
        allowed = allowed[:, None, None, :]
        scores = jnp.where(allowed, scores, -1e30)
        new_max = jnp.maximum(running_max, jnp.max(scores, axis=-1))
        weights = jnp.where(allowed, jnp.exp(scores - new_max[..., None]), 0.0)
        factor = jnp.exp(running_max - new_max)
        new_total = factor * running_total + jnp.sum(weights, axis=-1)
        product = jnp.einsum(
            "tkgs,skd->tkgd",
            weights.astype(jnp.bfloat16),
            value_block,
            preferred_element_type=jnp.float32,
        )
        return (new_max, new_total, factor[..., None] * summed + product)

    initial = (
        jnp.full((shard_len, kv_heads, per_group), -1e30, jnp.float32),
        jnp.zeros((shard_len, kv_heads, per_group), jnp.float32),
        jnp.zeros((shard_len, kv_heads, per_group, HEAD), jnp.float32),
    )
    kv_piece = lax.all_gather(key_value, "ctx", axis=0, tiled=True)
    seg_piece = lax.all_gather(local_seg, "ctx", axis=0, tiled=True)
    count_rows = kv_piece.shape[0]
    block_rows = math.gcd(count_rows, 512)
    key_pos = jnp.arange(count_rows, dtype=jnp.int32)
    key_heads = kv_piece[:, : kv_heads * HEAD].reshape(count_rows, kv_heads, HEAD)
    value_heads = kv_piece[:, kv_heads * HEAD :].reshape(count_rows, kv_heads, HEAD)

    def step(index, state):
        begin = index * block_rows

        def cut(array):
            return lax.dynamic_slice_in_dim(array, begin, block_rows, 0)

        block_pos = cut(key_pos)
        block_seg = cut(seg_piece)
        live = (
            (jnp.min(block_pos) <= last_query)
            & (jnp.max(block_seg) >= lowest_seg)
            & (jnp.min(block_seg) <= highest_seg)
        )
        return lax.cond(
            live,
            lambda inner: absorb(inner, cut(key_heads), cut(value_heads), block_seg, block_pos),
            lambda inner: inner,
            state,
        )

    final_max, final_total, final_sum = lax.fori_loop(0, count_rows // block_rows, step, initial)
    attended = (final_sum / final_total[..., None]).astype(jnp.bfloat16).reshape(shard_len, -1)
    return (attended[None], conv_out[None])


def solution(mesh):
    return jax.shard_map(
        body,
        mesh=mesh,
        in_specs=(
            P("fsdp", "ctx", None),
            P("fsdp", "ctx", None),
            P("fsdp", "ctx", None),
            P(),
            P("fsdp", None),
            P(),
            P(),
            P("fsdp", None),
            P("fsdp", "ctx"),
        ),
        out_specs=(P("fsdp", "ctx", None), P("fsdp", "ctx", None)),
        check_vma=False,
    )
```

profile of v0, /device:TPU:7, one launch (start us, length us, event | category | flops | bytes accessed | tf_op | source)
XLA Modules:
  0.0 330.0 jit_solution(3079206484951237510)
XLA Ops:
  7.2 0.0 all-gather.4.cloned.1.call-start
  7.2 0.7 all-gather.4.cloned.1.call-update
  7.9 0.0 all-gather.6.cloned.1.call-start
  7.9 3.1 fusion.20
  11.1 0.0 copy-start.4
  11.1 0.0 copy-start.1
  11.1 0.0 copy-start.2
  11.1 0.0 copy-start
  11.1 112.4 %all-gather.4.cloned.1.call-done = bf16[8192,1024]{1,0:T(8,128)(2,1)} async-done(((bf16[512,1024]{1,0:T(8,128)(2,1)}), bf16[8192,1024]{1,0:T(8,128)(2,1)}) %all-gather.4.cloned.1.call-update) | async-done | bytes 16777232 | tf_op jit(solution)/shard_map/all_gather | solution.py:32
  123.5 12.4 %fusion.31 = bf16[256,1024]{1,0:T(8,128)(2,1)} fusion(bf16[8192,1024]{1,0:T(8,128)(2,1)} %all-gather.4.cloned.1.call-done, bf16[1,256,8192]{2,1,0:T(8,128)(2,1)} %param.13, f32[8192]{0:T(1024)} %param.16, f32[256]{0:T(256)S(1)} %add_rsqrt_fusion), kind=kOutput, calls=%fused_computation.42 | convolution fusion | flops 4303618048 | bytes 21529600 | tf_op jit(solution)/shard_map/dot_general | solution.py:30
  135.9 0.0 copy-start.3
  135.9 0.0 all-gather.6.cloned.1.call-update
  135.9 0.9 slice_bitcast_fusion.1
  136.9 2.3 collective-permute-start
  139.2 0.0 copy-done.4
  139.2 0.1 select_reduce_fusion
  139.3 0.0 copy-done.1
  139.3 0.1 fusion.40
  139.4 0.0 copy-done.2
  139.4 0.6 fusion.37
  140.1 0.6 fusion.35
  140.7 0.0 copy-done
  140.7 2.4 copy.22
  143.1 3.0 copy.24
  146.2 12.4 %all-gather = s32[1,2048]{1,0:T(1,128)S(1)} all-gather(s32[1,256]{1,0:T(1,128)S(1)} %copy-done.2), channel_id=2, replica_groups=mesh['ctx'=8,'fsdp'=16] {'ctx'}, dimensions={1}, use_global_device_ids=true | all-gather | bytes 9216 | tf_op jit(solution)/shard_map/all_gather | solution.py:93
  158.5 0.0 collective-permute-done
  158.5 0.0 copy-done.3
  158.5 16.2 %fusion.30 = bf16[1,256,8192]{2,1,0:T(8,128)(2,1)} fusion(f32[8192]{0:T(1024)S(1)} %bitcast.65, bf16[256,8192]{1,0:T(8,128)(2,1)} %bitcast.61, pred[256]{0:T(512)(128)(4,1)S(1)} %get-tuple-element.409, f32[8192]{0:T(1024)S(1)} %bitcast.66, bf16[3,8192]{1,0:T(4,128)(2,1)S(1)} %collective-permute-done, pred[256]{0:T(512)(128)(4,1)S(1)} %get-tuple-element.410, ...), kind=kLoop, calls=%fused_computation.39 | loop fusion | flops 62914560 | bytes 8602624 | tf_op jit(solution)/shard_map/broadcast_in_dim | solution.py:122
  174.7 48.5 %all-gather.6.cloned.1.call-done = bf16[2048,1024]{1,0:T(8,128)(2,1)} async-done(((bf16[256,1024]{1,0:T(8,128)(2,1)}), bf16[2048,1024]{1,0:T(8,128)(2,1)}) %all-gather.6.cloned.1.call-update) | async-done | bytes 4194320 | tf_op jit(solution)/shard_map/all_gather | solution.py:92
  223.2 4.0 %fusion.39 = (bf16[2048,512]{1,0:T(8,128)(2,1)}, bf16[256,4,8,128]{3,2,1,0:T(8,128)(2,1)S(1)}) fusion(bf16[2048,1024]{1,0:T(8,128)(2,1)} %all-gather.6.cloned.1.call-done), kind=kLoop, calls=%fused_computation.55 | loop fusion | bytes 8388608 | tf_op jit(solution)/shard_map/slice | solution.py:98
  227.1 1.7 copy.34
  228.8 4.0 %copy.30 = bf16[2048,512]{0,1:T(8,128)(2,1)} copy(bf16[2048,512]{1,0:T(8,128)(2,1)} %get-tuple-element.402) | data formatting | bytes 4194304
  232.8 2.4 broadcast_in_dim.87
  235.3 82.3 %while.18 = (s32[]{:T(128)}, f32[256,4,8]{0,2,1:T(8,128)S(1)}, f32[256,4,8]{0,2,1:T(8,128)S(1)}, f32[256,4,8,128]{0,3,2,1:T(8,128)}, s32[2048]{0:T(1024)S(1)}, /...) while((s32[]{:T(128)}, f32[256,4,8]{0,2,1:T(8,128)S(1)}, ...), condition=%wide.region_12.13_spmd.clone, body=%wide.region_4.12_spmd.clone.sunk | while | flops 2204518144 | bytes 62932436 | solution.py:120
  235.3 0.8 fusion.44
  239.8 16.0 %conditional.3 = ((f32[256,4,8]{0,2,1:T(8,128)S(1)}, f32[256,4,8]{0,2,1:T(8,128)S(1)}, f32[256,4,8,128]{0,3,2,1:T(8,128)})) conditional(s32[]{:T(128)} %convert_element_type.78, (f32[256,4,8]{0,2,1:T(8,128)S(1)}, f32[256,4,8]{0,2,1:T(8,128)S(1)}, f32[256,4,8,128]{0,3,2,1:T(8,128)}) %tuple.66, (s32[512]{0:T(512)S(1)}, s32[]{:T(128)}, ...), branch_computations={%region_8.8_spmd, %region_9.11_spmd} | conditional | flops 2204516608 | bytes 62922828 | solution.py:113
  239.8 0.2 compare_and_fusion
  240.1 3.7 %fusion.2 = (f32[256,4,8]{0,2,1:T(8,128)S(1)}, f32[4,512,256,8]{2,1,3,0:T(8,128)S(1)}) fusion(pred[256,512]{0,1:T(8,128)(4,1)S(1)} %compare_and_fusion, bf16[256,4,8,128]{3,0,2,1:T(8,128)(2,1)S(1)} %get-tuple-element.254, bf16[2048,4,128]{2,0,1:T(8,128)(2,1)} %get-tuple-element.252, s32[]{:T(128)S(6)} %select_n.27), kind=kOutput, calls=%fused_computation.3 | convolution fusion | flops 1086316544 | bytes 19562500 | tf_op jit(solution)/shard_map/while/body/eval_jaxpr/cond/branch_1_fun/tkgd,skd->tkgs/dot_general | solution.py:67
  243.8 4.2 %fusion.4 = f32[256,4,8]{0,2,1:T(8,128)S(1)} fusion(f32[4,512,256,8]{2,1,3,0:T(8,128)S(1)} %get-tuple-element.399, f32[256,4,8]{0,2,1:T(8,128)S(1)} %max.2, pred[256,512]{0,1:T(8,128)(4,1)S(1)} %compare_and_fusion), kind=kLoop, calls=%fused_computation.5 | loop fusion | flops 20963328 | bytes 16973824 | tf_op jit(solution)/shard_map/while/body/eval_jaxpr/cond/branch_1_fun/reduce_sum | solution.py:78
  248.1 7.8 %bitcast_add_fusion = f32[256,4,8,128]{0,3,2,1:T(8,128)} fusion(f32[256,4,8,128]{0,3,2,1:T(8,128)} %get-tuple-element.256, f32[4,512,256,8]{2,1,3,0:T(8,128)S(1)} %get-tuple-element.399, f32[256,4,8]{0,2,1:T(8,128)S(1)} %max.2, pred[256,512]{0,1:T(8,128)(4,1)S(1)} %compare_and_fusion, f32[256,4,8]{0,2,1:T(8,128)S(1)} %get-tuple-element.394, ...), kind=kOutput, calls=%fused_computation.8 | convolution fusion | flops 1096810496 | bytes 25886724 | tf_op jit(solution)/shard_map/while/body/eval_jaxpr/cond/branch_1_fun/tkgs,skd->tkgd/dot_general | solution.py:79
  255.8 0.8 fusion.44
  260.4 16.0 %conditional.3 = ((f32[256,4,8]{0,2,1:T(8,128)S(1)}, f32[256,4,8]{0,2,1:T(8,128)S(1)}, f32[256,4,8,128]{0,3,2,1:T(8,128)})) conditional(s32[]{:T(128)} %convert_element_type.78, (f32[256,4,8]{0,2,1:T(8,128)S(1)}, f32[256,4,8]{0,2,1:T(8,128)S(1)}, f32[256,4,8,128]{0,3,2,1:T(8,128)}) %tuple.66, (s32[512]{0:T(512)S(1)}, s32[]{:T(128)}, ...), branch_computations={%region_8.8_spmd, %region_9.11_spmd} | conditional | flops 2204516608 | bytes 62922828 | solution.py:113
  260.4 0.2 compare_and_fusion
  260.6 3.7 %fusion.2 = (f32[256,4,8]{0,2,1:T(8,128)S(1)}, f32[4,512,256,8]{2,1,3,0:T(8,128)S(1)}) fusion(pred[256,512]{0,1:T(8,128)(4,1)S(1)} %compare_and_fusion, bf16[256,4,8,128]{3,0,2,1:T(8,128)(2,1)S(1)} %get-tuple-element.254, bf16[2048,4,128]{2,0,1:T(8,128)(2,1)} %get-tuple-element.252, s32[]{:T(128)S(6)} %select_n.27), kind=kOutput, calls=%fused_computation.3 | convolution fusion | flops 1086316544 | bytes 19562500 | tf_op jit(solution)/shard_map/while/body/eval_jaxpr/cond/branch_1_fun/tkgd,skd->tkgs/dot_general | solution.py:67
  264.4 4.2 %fusion.4 = f32[256,4,8]{0,2,1:T(8,128)S(1)} fusion(f32[4,512,256,8]{2,1,3,0:T(8,128)S(1)} %get-tuple-element.399, f32[256,4,8]{0,2,1:T(8,128)S(1)} %max.2, pred[256,512]{0,1:T(8,128)(4,1)S(1)} %compare_and_fusion), kind=kLoop, calls=%fused_computation.5 | loop fusion | flops 20963328 | bytes 16973824 | tf_op jit(solution)/shard_map/while/body/eval_jaxpr/cond/branch_1_fun/reduce_sum | solution.py:78
  268.6 7.8 %bitcast_add_fusion = f32[256,4,8,128]{0,3,2,1:T(8,128)} fusion(f32[256,4,8,128]{0,3,2,1:T(8,128)} %get-tuple-element.256, f32[4,512,256,8]{2,1,3,0:T(8,128)S(1)} %get-tuple-element.399, f32[256,4,8]{0,2,1:T(8,128)S(1)} %max.2, pred[256,512]{0,1:T(8,128)(4,1)S(1)} %compare_and_fusion, f32[256,4,8]{0,2,1:T(8,128)S(1)} %get-tuple-element.394, ...), kind=kOutput, calls=%fused_computation.8 | convolution fusion | flops 1096810496 | bytes 25886724 | tf_op jit(solution)/shard_map/while/body/eval_jaxpr/cond/branch_1_fun/tkgs,skd->tkgd/dot_general | solution.py:79
  276.4 0.8 fusion.44
  281.0 16.0 %conditional.3 = ((f32[256,4,8]{0,2,1:T(8,128)S(1)}, f32[256,4,8]{0,2,1:T(8,128)S(1)}, f32[256,4,8,128]{0,3,2,1:T(8,128)})) conditional(s32[]{:T(128)} %convert_element_type.78, (f32[256,4,8]{0,2,1:T(8,128)S(1)}, f32[256,4,8]{0,2,1:T(8,128)S(1)}, f32[256,4,8,128]{0,3,2,1:T(8,128)}) %tuple.66, (s32[512]{0:T(512)S(1)}, s32[]{:T(128)}, ...), branch_computations={%region_8.8_spmd, %region_9.11_spmd} | conditional | flops 2204516608 | bytes 62922828 | solution.py:113
  281.0 0.2 compare_and_fusion
  281.2 3.7 %fusion.2 = (f32[256,4,8]{0,2,1:T(8,128)S(1)}, f32[4,512,256,8]{2,1,3,0:T(8,128)S(1)}) fusion(pred[256,512]{0,1:T(8,128)(4,1)S(1)} %compare_and_fusion, bf16[256,4,8,128]{3,0,2,1:T(8,128)(2,1)S(1)} %get-tuple-element.254, bf16[2048,4,128]{2,0,1:T(8,128)(2,1)} %get-tuple-element.252, s32[]{:T(128)S(6)} %select_n.27), kind=kOutput, calls=%fused_computation.3 | convolution fusion | flops 1086316544 | bytes 19562500 | tf_op jit(solution)/shard_map/while/body/eval_jaxpr/cond/branch_1_fun/tkgd,skd->tkgs/dot_general | solution.py:67
  285.0 4.2 %fusion.4 = f32[256,4,8]{0,2,1:T(8,128)S(1)} fusion(f32[4,512,256,8]{2,1,3,0:T(8,128)S(1)} %get-tuple-element.399, f32[256,4,8]{0,2,1:T(8,128)S(1)} %max.2, pred[256,512]{0,1:T(8,128)(4,1)S(1)} %compare_and_fusion), kind=kLoop, calls=%fused_computation.5 | loop fusion | flops 20963328 | bytes 16973824 | tf_op jit(solution)/shard_map/while/body/eval_jaxpr/cond/branch_1_fun/reduce_sum | solution.py:78
  289.2 7.8 %bitcast_add_fusion = f32[256,4,8,128]{0,3,2,1:T(8,128)} fusion(f32[256,4,8,128]{0,3,2,1:T(8,128)} %get-tuple-element.256, f32[4,512,256,8]{2,1,3,0:T(8,128)S(1)} %get-tuple-element.399, f32[256,4,8]{0,2,1:T(8,128)S(1)} %max.2, pred[256,512]{0,1:T(8,128)(4,1)S(1)} %compare_and_fusion, f32[256,4,8]{0,2,1:T(8,128)S(1)} %get-tuple-element.394, ...), kind=kOutput, calls=%fused_computation.8 | convolution fusion | flops 1096810496 | bytes 25886724 | tf_op jit(solution)/shard_map/while/body/eval_jaxpr/cond/branch_1_fun/tkgs,skd->tkgd/dot_general | solution.py:79
  297.0 0.8 fusion.44
  301.6 16.0 %conditional.3 = ((f32[256,4,8]{0,2,1:T(8,128)S(1)}, f32[256,4,8]{0,2,1:T(8,128)S(1)}, f32[256,4,8,128]{0,3,2,1:T(8,128)})) conditional(s32[]{:T(128)} %convert_element_type.78, (f32[256,4,8]{0,2,1:T(8,128)S(1)}, f32[256,4,8]{0,2,1:T(8,128)S(1)}, f32[256,4,8,128]{0,3,2,1:T(8,128)}) %tuple.66, (s32[512]{0:T(512)S(1)}, s32[]{:T(128)}, ...), branch_computations={%region_8.8_spmd, %region_9.11_spmd} | conditional | flops 2204516608 | bytes 62922828 | solution.py:113
  301.6 0.2 compare_and_fusion
  301.8 3.7 %fusion.2 = (f32[256,4,8]{0,2,1:T(8,128)S(1)}, f32[4,512,256,8]{2,1,3,0:T(8,128)S(1)}) fusion(pred[256,512]{0,1:T(8,128)(4,1)S(1)} %compare_and_fusion, bf16[256,4,8,128]{3,0,2,1:T(8,128)(2,1)S(1)} %get-tuple-element.254, bf16[2048,4,128]{2,0,1:T(8,128)(2,1)} %get-tuple-element.252, s32[]{:T(128)S(6)} %select_n.27), kind=kOutput, calls=%fused_computation.3 | convolution fusion | flops 1086316544 | bytes 19562500 | tf_op jit(solution)/shard_map/while/body/eval_jaxpr/cond/branch_1_fun/tkgd,skd->tkgs/dot_general | solution.py:67
  305.6 4.2 %fusion.4 = f32[256,4,8]{0,2,1:T(8,128)S(1)} fusion(f32[4,512,256,8]{2,1,3,0:T(8,128)S(1)} %get-tuple-element.399, f32[256,4,8]{0,2,1:T(8,128)S(1)} %max.2, pred[256,512]{0,1:T(8,128)(4,1)S(1)} %compare_and_fusion), kind=kLoop, calls=%fused_computation.5 | loop fusion | flops 20963328 | bytes 16973824 | tf_op jit(solution)/shard_map/while/body/eval_jaxpr/cond/branch_1_fun/reduce_sum | solution.py:78
  309.8 7.8 %bitcast_add_fusion = f32[256,4,8,128]{0,3,2,1:T(8,128)} fusion(f32[256,4,8,128]{0,3,2,1:T(8,128)} %get-tuple-element.256, f32[4,512,256,8]{2,1,3,0:T(8,128)S(1)} %get-tuple-element.399, f32[256,4,8]{0,2,1:T(8,128)S(1)} %max.2, pred[256,512]{0,1:T(8,128)(4,1)S(1)} %compare_and_fusion, f32[256,4,8]{0,2,1:T(8,128)S(1)} %get-tuple-element.394, ...), kind=kOutput, calls=%fused_computation.8 | convolution fusion | flops 1096810496 | bytes 25886724 | tf_op jit(solution)/shard_map/while/body/eval_jaxpr/cond/branch_1_fun/tkgs,skd->tkgd/dot_general | solution.py:79
  317.6 2.7 divide_convert_fusion
  320.3 2.9 copy.31
  (26 shorter events, 0.2 us)
Async XLA Ops:
  7.2 116.3 %all-gather.4.cloned.1.call-start = ((), (), s32[]{:S(2)}) async-start(), calls=%async_computation | async-start | bytes 17825792 | tf_op jit(solution)/shard_map/all_gather | solution.py:32
  7.9 215.3 %all-gather.6.cloned.1.call-start = ((), (), s32[]{:S(2)}) async-start(), calls=%async_computation.1 | async-start | bytes 4718592 | tf_op jit(solution)/shard_map/all_gather | solution.py:92
  11.1 128.1 %copy-start.4 = (s32[1,8]{1,0:T(1,128)S(1)}, s32[1,8]{1,0:T(1,128)}, u32[]{:S(2)}) copy-start(s32[1,8]{1,0:T(1,128)} %param.20) | copy-start | bytes 100
  11.1 128.2 %copy-start.1 = (f32[4,8192]{1,0:T(4,128)S(1)}, f32[4,8192]{1,0:T(4,128)}, u32[]{:S(2)}) copy-start(f32[4,8192]{1,0:T(4,128)} %param.18) | copy-start | bytes 393220
  11.1 128.3 %copy-start.2 = (s32[1,256]{1,0:T(1,128)S(1)}, s32[1,256]{1,0:T(1,128)}, u32[]{:S(2)}) copy-start(s32[1,256]{1,0:T(1,128)} %param.21) | copy-start | bytes 3076
  11.1 129.6 %copy-start = (bf16[1,256,4096]{2,1,0:T(8,128)(2,1)S(1)}, bf16[1,256,4096]{2,1,0:T(8,128)(2,1)}, u32[]{:S(2)}) copy-start(bf16[1,256,4096]{2,1,0:T(8,128)(2,1)} %param.14) | copy-start | bytes 6291460
  135.9 22.6 %copy-start.3 = (f32[8192]{0:T(1024)S(1)}, f32[8192]{0:T(1024)}, u32[]{:S(2)}) copy-start(f32[8192]{0:T(1024)} %param.19) | copy-start | bytes 98308
  136.9 21.7 %collective-permute-start = (bf16[3,8192]{1,0:T(4,128)(2,1)S(1)}, bf16[3,8192]{1,0:T(4,128)(2,1)S(1)}, u32[]{:S(2)}, u32[]{:S(2)}) collective-permute-start(bf16[3,8192]{1,0:T(4,128)(2,1)S(1)} %slice_bitcast_fusion.1), channel_id=1, source_target_pairs={{0,16},{16,32},{32,48},{48,64},{64,80},{80,96},{96,112},{1,17},{17... | collective-permute-start | bytes 147464 | tf_op jit(solution)/shard_map/ppermute | solution.py:15
Sparse Core Ops, SparseCore 0:
  10.4 113.0 all-gather.3
  136.1 87.0 all-gather.5
where the time goes:
time: 331 us; the launch traced here: 330 us
  waiting for transfers between devices  162 us (49%)
  matrix products  58.5 us (18%)
  other arithmetic  44.2 us (13%)
  local copies, waits for them, and re-layouts  21.5 us (6%)
  loops' own time  15.4 us (5%)
  between operations  14.1 us (4%)
  blocking collectives  12.4 us (4%)
    all_gather x1, waiting for transfers between devices, body(): lax.all_gather(kv_weight, 'fsdp', axis=0, tiled=True)  112 us
    all_gather x1, waiting for transfers between devices, body(): kv_piece = lax.all_gather(key_value, 'ctx', axis=0, tiled=True)  48.5 us
    dot_general x4, matrix products, absorb(): jnp.einsum('tkgs,skd->tkgd', weights.astype(jnp.bfloat16), value_block, p...  31.1 us
    reduce_sum x4, other arithmetic, absorb(): new_total = factor * running_total + jnp.sum(weights, axis=-1)  16.8 us
    broadcast_in_dim x1, other arithmetic, body(): return (attended[None], conv_out[None])  16.2 us
    another operation x1, loops' own time, body(): lax.fori_loop(0, count_rows // block_rows, step, initial)  15.1 us
    dot_general x4, matrix products, absorb(): jnp.einsum('tkgd,skd->tkgs', query_heads, key_block, preferred_element_ty...  14.9 us
    dot_general x1, matrix products, body(): jnp.dot(normed, lax.all_gather(kv_weight, 'fsdp', axis=0, tiled=True), pr...  12.4 us
  transfers between devices with their start and end apart: 3, of which 2 were waited for; matrix products, arithmetic and copies ran while one was open for 8% of the time, Pallas kernels for 0%

commit v1 on v0

v1 whole, which is shorter than its diff:
```python
import functools
import math

import jax
import jax.numpy as jnp
import numpy as np
from jax import lax
from jax.experimental import pallas as pl
from jax.experimental.pallas import tpu as pltpu
from jax.sharding import PartitionSpec as P

HEAD = 128
TAPS = 4
EPISODES = 8
AXES = ("ctx", "fsdp")
CTX, FSDP = 8, 16
DEVICES = CTX * FSDP
MIB = 1 << 20


def place(i):
    c, f = divmod(i, FSDP)
    x, zl = divmod(c, 2)
    y, r = divmod(f, 4)
    zh, k = divmod(r, 2)
    return x, y, zh, zl, k


def device(x, y, zh, zl, k):
    return ((x % 4) * 2 + zl) * FSDP + ((y % 4) * 2 + zh) * 2 + k


def lead_core(x, zl):
    return (x + zl) % 2


def neighbour(x, y, zh, zl, way):
    return {
        "x+": (x + 1, y, zh, zl),
        "x-": (x - 1, y, zh, zl),
        "y+": (x, y + 1, zh, zl),
        "y-": (x, y - 1, zh, zl),
        "zlo": (x, y, zh, 1 - zl),
        "zhi": (x, y, 1 - zh, 1 - zl),
    }[way]


STEPS = (
    ((0, "y-", 0), (1, "zhi", 1)),
    ((0, "y+", 1),),
    ((0, "x-", 1), (1, "x+", 0)),
    ((0, "y-", 0), (1, "y+", 1)),
    ((0, "zhi", 0), (1, "zlo", 1)),
    ((0, "x-", 0), (1, "x+", 1)),
    ((0, "zlo", 1), (1, "y+", 0)),
    ((0, "y-", 0),),
)
SENT = ((0, 0), (0, 0), (1, 2), (1, 1), (1, 1), (4, 4), (5, 4), (5, 5))


def weight_plan():
    pairs, held = [], [[i % FSDP for i in range(DEVICES)]]
    for step, sent in zip(STEPS, SENT):
        now, got = [], [-1] * DEVICES
        for i in range(DEVICES):
            x, y, zh, zl, k = place(i)
            role = 0 if k == lead_core(x, zl) else 1
            for sender, way, receiver in step:
                if sender == role:
                    nx, ny, nzh, nzl = neighbour(x, y, zh, zl, way)
                    lead = lead_core(nx, nzl)
                    to = device(nx, ny, nzh, nzl, lead if receiver == 0 else 1 - lead)
                    now.append((i, to))
                    got[to] = held[sent[role]][i]
        pairs.append(now)
        held.append(got)
    slots = [
        [held[n][i] for n in (0, 1, 3, 4, 5, 6, 7)] + [max(held[2][i], held[8][i])]
        for i in range(DEVICES)
    ]
    return pairs, np.asarray(slots, np.int32)


WEIGHT_PAIRS, SLOTS = weight_plan()


def moved(way):
    return [
        (i, device(*neighbour(*place(i)[:4], way), place(i)[4])) for i in range(DEVICES)
    ]


SWAP = [(i, i ^ 1) for i in range(DEVICES)]


def send(x, pairs):
    return lax.ppermute(x, AXES, pairs)


def params(mib, **kw):
    return pltpu.CompilerParams(vmem_limit_bytes=mib * MIB, **kw)


def cost(flops, moved_bytes, trans=0):
    return pl.CostEstimate(
        flops=int(flops), bytes_accessed=int(moved_bytes), transcendentals=int(trans)
    )


def norm_kernel(slots, h_ref, g_ref, mine_ref, other_ref, *, width, chunk, count):
    rows = h_ref.shape[0]
    total = jnp.zeros((rows, chunk), jnp.float32)
    for c in range(width // chunk):
        f = h_ref[:, c * chunk : (c + 1) * chunk].astype(jnp.float32)
        total = total + f * f
    mean = jnp.sum(total, axis=-1, keepdims=True) * (1.0 / width)
    factor = lax.rsqrt(mean + 1e-06)
    for which, out in ((1, other_ref), (0, mine_ref)):
        for s in range(count):
            at = pl.multiple_of(slots[which, s] * chunk, chunk)
            f = h_ref[:, pl.ds(at, chunk)].astype(jnp.float32)
            out[s] = (f * factor * g_ref[:, pl.ds(at, chunk)]).astype(jnp.bfloat16)


def norm(slots, hidden, gain, chunk):
    rows, width = hidden.shape
    count = slots.shape[1]
    tile = 64
    shape = jax.ShapeDtypeStruct((count, rows, chunk), jnp.bfloat16)
    out_spec = pl.BlockSpec((count, tile, chunk), lambda i: (0, i, 0))
    return pl.pallas_call(
        functools.partial(norm_kernel, width=width, chunk=chunk, count=count),
        grid=(rows // tile,),
        in_specs=[
            pl.BlockSpec(memory_space=pltpu.SMEM),
            pl.BlockSpec((tile, width), lambda i: (i, 0)),
            pl.BlockSpec((1, width), lambda i: (0, 0)),
        ],
        out_specs=[out_spec, out_spec],
        out_shape=[shape, shape],
        compiler_params=params(24),
        cost_estimate=cost(rows * width * 6, rows * width * 4),
        name="norm",
    )(slots, hidden, gain)


def project_kernel(*refs, count, carried):
    xs, ws = refs[:count], refs[count : 2 * count]
    out = refs[-1]
    total = refs[2 * count][...] if carried else None
    for x, w in zip(xs, ws):
        part = jnp.dot(x[0], w[...], preferred_element_type=jnp.float32)
        total = part if total is None else total + part
    out[...] = total


def project(x, slots, weights, carried=None):
    _, rows, depth = x.shape
    columns = weights[0].shape[1]
    tile = 512
    count = len(slots)
    in_specs = [
        pl.BlockSpec((1, rows, depth), functools.partial(lambda s, i: (s, 0, 0), s)) for s in slots
    ]
    in_specs += [pl.BlockSpec((depth, tile), lambda i: (0, i))] * count
    out_spec = pl.BlockSpec((rows, tile), lambda i: (0, i))
    operands = [x] * count + list(weights)
    if carried is not None:
        in_specs.append(out_spec)
        operands.append(carried)
    return pl.pallas_call(
        functools.partial(project_kernel, count=count, carried=carried is not None),
        grid=(columns // tile,),
        in_specs=in_specs,
        out_specs=out_spec,
        out_shape=jax.ShapeDtypeStruct((rows, columns), jnp.float32),
        compiler_params=params(24),
        cost_estimate=cost(
            2 * count * rows * depth * columns, count * (rows + columns) * depth * 2 + rows * columns * 8
        ),
        name="project",
    )(*operands)


def conv_kernel(info, x_ref, halo_ref, w_ref, b_ref, o_ref, ext):
    rows, width = x_ref.shape
    back = TAPS - 1
    ext[pl.ds(8 - back, back), :] = halo_ref[...].astype(jnp.float32)
    ext[pl.ds(8, rows), :] = x_ref[...].astype(jnp.float32)
    step, lanes = 32, 256
    for r in range(0, rows, step):
        pos = info[0] + r + lax.broadcasted_iota(jnp.int32, (step, 1), 0)
        begin = jnp.zeros((step, 1), jnp.int32)
        for e in range(EPISODES):
            begin = jnp.where(info[1 + e] <= pos, jnp.maximum(begin, info[1 + e]), begin)
        depth = pos - begin
        for c in range(0, width, lanes):
            cols = slice(c, c + lanes)
            mixing = jnp.zeros((step, lanes), jnp.float32) + b_ref[:, cols]
            for tap in range(TAPS):
                behind = back - tap
                term = ext[pl.ds(8 + r - behind, step), cols]
                if behind:
                    term = jnp.where(depth >= behind, term, 0.0)
                mixing = mixing + term * w_ref[tap : tap + 1, cols]
            o_ref[pl.ds(r, step), cols] = (mixing / (1.0 + jnp.exp(-mixing))).astype(o_ref.dtype)


def conv(info, x, halo, weight, bias):
    rows, width = x.shape
    tile = 1024
    return pl.pallas_call(
        conv_kernel,
        grid=(width // tile,),
        in_specs=[
            pl.BlockSpec(memory_space=pltpu.SMEM),
            pl.BlockSpec((rows, tile), lambda i: (0, i)),
            pl.BlockSpec((TAPS - 1, tile), lambda i: (0, i)),
            pl.BlockSpec((TAPS, tile), lambda i: (0, i)),
            pl.BlockSpec((1, tile), lambda i: (0, i)),
        ],
        out_specs=pl.BlockSpec((rows, tile), lambda i: (0, i)),
        out_shape=jax.ShapeDtypeStruct((rows, width), x.dtype),
        scratch_shapes=[pltpu.VMEM((rows + 8, tile), jnp.float32)],
        compiler_params=params(24),
        cost_estimate=cost(rows * width * 40, rows * width * 4, rows * width * 2),
        name="conv",
    )(info, x, halo, weight, bias)


def attend_kernel(info, q_ref, *refs, count, per_group):
    ks, vs = refs[:count], refs[count : 2 * count]
    o_ref, m_ref, l_ref, a_ref, mask_ref = refs[2 * count :]
    rows = q_ref.shape[0]
    keys = ks[0].shape[0]
    factor = math.log2(math.e) / math.sqrt(HEAD)
    first = info[0]
    pos = first + lax.broadcasted_iota(jnp.int32, (rows, keys), 0)
    begin = jnp.zeros((rows, keys), jnp.int32)
    lowest = jnp.int32(0)
    for e in range(EPISODES):
        start = info[1 + e]
        begin = jnp.where(start <= pos, jnp.maximum(begin, start), begin)
        lowest = jnp.where(start <= first, jnp.maximum(lowest, start), lowest)
    offset = lax.broadcasted_iota(jnp.int32, (rows, keys), 1)

    def block(b, own):
        key_pos = info[1 + EPISODES + b] + offset
        allowed = key_pos >= begin
        if own:
            allowed = allowed & (key_pos <= pos)
        mask_ref[...] = jnp.where(allowed, 0.0, -1e30)
        for h in range(per_group):
            q = q_ref[:, h * HEAD : (h + 1) * HEAD]
            s = lax.dot_general(
                q, ks[b][...], (((1,), (1,)), ((), ())), preferred_element_type=jnp.float32
            )
            s = s + mask_ref[...]
            top = jnp.max(s, axis=1, keepdims=True)
            if own:
                new = jnp.broadcast_to(top, (rows, HEAD))
            else:
                old = m_ref[h]
                new = jnp.maximum(old, top)
            w = jnp.exp2((s - jnp.concatenate([new] * (keys // HEAD), axis=1)) * factor)
            part = w[:, :HEAD]
            for c in range(HEAD, keys, HEAD):
                part = part + w[:, c : c + HEAD]
            product = jnp.dot(
                w.astype(jnp.bfloat16), vs[b][...], preferred_element_type=jnp.float32
            )
            if own:
                l_ref[h] = part
                a_ref[h] = product
            else:
                shrink = jnp.exp2((old - new) * factor)
                l_ref[h] = l_ref[h] * shrink + part
                a_ref[h] = a_ref[h] * shrink + product
            m_ref[h] = new

    block(0, True)
    for b in range(1, count):
        base = info[1 + EPISODES + b]

        @pl.when((base < first) & (base + keys > lowest))
        def _():
            block(b, False)

    for h in range(per_group):
        total = jnp.sum(l_ref[h], axis=1, keepdims=True)
        o_ref[:, h * HEAD : (h + 1) * HEAD] = (a_ref[h] / total).astype(o_ref.dtype)


def attend(info, queries, blocks):
    rows, width = queries.shape
    keys, columns = blocks[0].shape
    kv_heads = columns // (2 * HEAD)
    group = width // kv_heads
    count = len(blocks)
    per_group = group // HEAD
    q_spec = pl.BlockSpec((rows, group), lambda g: (0, g))
    return pl.pallas_call(
        functools.partial(attend_kernel, count=count, per_group=per_group),
        grid=(kv_heads,),
        in_specs=[pl.BlockSpec(memory_space=pltpu.SMEM), q_spec]
        + [pl.BlockSpec((keys, HEAD), lambda g: (0, g))] * count
        + [pl.BlockSpec((keys, HEAD), lambda g: (0, kv_heads + g))] * count,
        out_specs=q_spec,
        out_shape=jax.ShapeDtypeStruct((rows, width), queries.dtype),
        scratch_shapes=[pltpu.VMEM((per_group, rows, HEAD), jnp.float32)] * 3
        + [pltpu.VMEM((rows, keys), jnp.float32)],
        compiler_params=params(32),
        cost_estimate=cost(
            4 * rows * width * keys * count, rows * width * 4 + count * keys * columns * 2,
            rows * keys * count * width // HEAD,
        ),
        name="attend",
    )(info, queries, *blocks, *blocks)


def body(
    hidden, queries, conv_input, norm_gain, kv_weight, conv_weight, conv_bias, starts, segment_ids
):
    del segment_ids
    rows = hidden.shape[1]
    ctx = lax.axis_index("ctx")
    me = ctx * FSDP + lax.axis_index("fsdp")
    x, zl = ctx // 2, ctx % 2
    leads = lax.axis_index("fsdp") % 2 == lead_core(x, zl)
    depth = kv_weight.shape[0]

    w1 = send(kv_weight, WEIGHT_PAIRS[0])
    w2 = send(kv_weight, WEIGHT_PAIRS[1])

    table = jnp.asarray(SLOTS)
    slots = jnp.stack([table[me], table[me ^ 1]])
    mine, other = norm(slots, hidden[0], norm_gain[None], depth)
    theirs = send(other, SWAP)

    w3 = send(jnp.where(leads, w1, w2), WEIGHT_PAIRS[2])
    w4 = send(w1, WEIGHT_PAIRS[3])
    w5 = send(w1, WEIGHT_PAIRS[4])

    first = ctx * rows
    info = jnp.concatenate([first[None], starts[0]])
    signal = conv_input[0]
    halo = lax.ppermute(
        signal[rows - (TAPS - 1) :], "ctx", [(i, i + 1) for i in range(CTX - 1)]
    )
    conv_out = conv(info, signal, halo, conv_weight, conv_bias[None])

    def both(slot_ids, weights, carried=(None, None)):
        return tuple(
            project(v, slot_ids, weights, c) for v, c in zip((theirs, mine), carried)
        )

    sums = both((0, 1), (kv_weight, w1))
    w6 = send(w4, WEIGHT_PAIRS[5])
    w7 = send(jnp.where(leads, w5, w4), WEIGHT_PAIRS[6])
    w8 = send(w5, WEIGHT_PAIRS[7])
    sums = both((2, 3, 4), (w3, w4, w5), sums)
    last = (w6, w7, jnp.where(leads, w8, w2))
    their_sum = project(theirs, (5, 6, 7), last, sums[0])
    back = send(their_sum, SWAP)
    my_sum = project(mine, (5, 6, 7), last, sums[1])
    kv = (my_sum + back).astype(jnp.bfloat16)

    up, down, pair = moved("x+"), moved("x-"), moved("zlo")
    from_left = send(kv, up)
    from_right = send(kv, down)
    from_pair = send(kv, pair)
    left_pair = send(from_pair, up)
    right_pair = send(from_pair, down)
    far = send(from_left, up)
    far_pair = send(right_pair, down)

    def base(dx, dz):
        return (((x + dx) % 4) * 2 + (zl + dz) % 2) * rows

    bases = [first, base(0, 1), base(-1, 0), base(1, 0), base(-1, 1), base(1, 1), base(2, 0), base(2, 1)]
    blocks = [kv, from_pair, from_left, from_right, left_pair, right_pair, far, far_pair]
    attended = attend(jnp.concatenate([info, jnp.stack(bases)]), queries[0], blocks)
    return attended[None], conv_out[None]


def solution(mesh):
    return jax.shard_map(
        body,
        mesh=mesh,
        in_specs=(
            P("fsdp", "ctx", None),
            P("fsdp", "ctx", None),
            P("fsdp", "ctx", None),
            P(),
            P("fsdp", None),
            P(),
            P(),
            P("fsdp", None),
            P("fsdp", "ctx"),
        ),
        out_specs=(P("fsdp", "ctx", None), P("fsdp", "ctx", None)),
        check_vma=False,
    )
```

time: 331 us -> 180 us (0.54)
  the two profiles are of different devices: /device:TPU:7 before, /device:TPU:95 now
where the time goes in v1:
time: 180 us; the launch traced here: 179 us
  waiting for transfers between devices  79 us (44%)
  Pallas kernels  65.1 us (36%)
  starting transfers between devices  23.4 us (13%)
  local copies, waits for them, and re-layouts  6.96 us (4%)
  other arithmetic  3.3 us (2%)
    ppermute x17, waiting for transfers between devices, send(): return lax.ppermute(x, AXES, pairs)  71.3 us
    pallas_call x1, Pallas kernels, attend(): pl.pallas_call(functools.partial(attend_kernel, count=count, per_group=pe...  38.5 us
    ppermute x17, starting transfers between devices, send(): return lax.ppermute(x, AXES, pairs)  20.3 us
    pallas_call x6, Pallas kernels, project(): pl.pallas_call(functools.partial(project_kernel, count=count, carried=car...  12.5 us
    pallas_call x1, Pallas kernels, conv(): pl.pallas_call(conv_kernel, grid=(width // tile,), in_specs=[pl.BlockSpec...  10.4 us
    ppermute x1, waiting for transfers between devices, body(): lax.ppermute(signal[rows - (TAPS - 1):], 'ctx', [(i, i + 1) for i in rang...  7.71 us
    unnamed x16, local copies, waits for them, and re-layouts  5.16 us
    pallas_call x1, Pallas kernels, norm(): pl.pallas_call(functools.partial(norm_kernel, width=width, chunk=chunk, c...  3.68 us
  transfers between devices with their start and end apart: 18, of which 9 were waited for; matrix products, arithmetic and copies ran while one was open for 3% of the time, Pallas kernels for 14%

profile of v1, /device:TPU:95, one launch (start us, length us, event | category | flops | bytes accessed | tf_op | source)
XLA Modules:
  0.0 178.7 jit_solution(13998432762993331783)
XLA Ops:
  0.6 0.5 collective-permute-start
  1.2 14.6 %collective-permute-done.refs_3_ = bf16[512,1024]{1,0:T(8,128)(2,1)S(1)} collective-permute-done((bf16[512,1024]{1,0:T(8,128)(2,1)}, bf16[512,1024]{1,0:T(8,128)(2,1)S(1)}, u32[]{:S(2)}, u32[]{:S(2)}) %collective-permute-start) | collective-permute-done | bytes 1048608 | tf_op jit(solution)/shard_map/ppermute | solution.py:97
  15.8 1.5 collective-permute-start.3
  17.3 3.5 %collective-permute-start.6 = (bf16[512,1024]{1,0:T(8,128)(2,1)}, bf16[512,1024]{1,0:T(8,128)(2,1)}, u32[]{:S(2)}, u32[]{:S(2)}) collective-permute-start(bf16[512,1024]{1,0:T(8,128)(2,1)} %refs_2_.3), channel_id=1, source_target_pairs={{0,5},{2,7},{4,9},{6,11},{8,13},{10,15},{12,1},{14,3},{17,20},{19,... | collective-permute-start | bytes 3145736 | tf_op jit(solution)/shard_map/ppermute | solution.py:97
  20.8 9.6 %collective-permute-done.3.refs_5_ = bf16[512,1024]{1,0:T(8,128)(2,1)} collective-permute-done((bf16[512,1024]{1,0:T(8,128)(2,1)S(1)}, bf16[512,1024]{1,0:T(8,128)(2,1)}, u32[]{:S(2)}, u32[]{:S(2)}) %collective-permute-start.3) | collective-permute-done | bytes 1048608 | tf_op jit(solution)/shard_map/ppermute | solution.py:97
  30.4 1.9 %collective-permute-start.5 = (bf16[512,1024]{1,0:T(8,128)(2,1)}, bf16[512,1024]{1,0:T(8,128)(2,1)}, u32[]{:S(2)}, u32[]{:S(2)}) collective-permute-start(bf16[512,1024]{1,0:T(8,128)(2,1)} %collective-permute-done.3.refs_5_), channel_id=1, source_target_pairs={{0,12},{2,14},{4,0},{6,2},{8,4},{10,6},{12,8},{14,10},{17,29},{19,... | collective-permute-start | bytes 3145736 | tf_op jit(solution)/shard_map/ppermute | solution.py:97
  32.3 0.1 collective-permute-start.1
  32.4 0.8 constant_dynamic-slice_fusion.1
  33.2 0.0 copy-start.2
  33.2 2.2 %copy-done.2 = bf16[1,256,8192]{2,1,0:T(8,128)(2,1)S(1)} copy-done((bf16[1,256,8192]{2,1,0:T(8,128)(2,1)S(1)}, bf16[1,256,8192]{2,1,0:T(8,128)(2,1)}, u32[]{:S(2)}) %copy-start.2) | copy-done | bytes 4194328
  35.4 0.8 copy-done.4
  36.1 3.7 %norm.1 = (bf16[8,256,512]{2,1,0:T(8,128)(2,1)S(1)}, bf16[8,256,512]{2,1,0:T(8,128)(2,1)}) custom-call(s32[2,8]{1,0:T(2,128)S(1)} %pad_add_fusion.slots, bf16[256,8192]{1,0:T(8,128)(2,1)S(1)} %bitcast.19, f32[1,8192]{1,0:T(1,128)S(1)} %bitcast.20), custom_call_target="tpu_custom_call" | custom-call | flops 12582912 | bytes 8388608 | tf_op jit(solution)/shard_map/norm/pallas_call | solution.py:131
  39.8 0.2 collective-permute-start.8
  40.0 0.0 collective-permute-done.6
  40.0 7.4 %collective-permute-done.5 = bf16[512,1024]{1,0:T(8,128)(2,1)} collective-permute-done((bf16[512,1024]{1,0:T(8,128)(2,1)}, bf16[512,1024]{1,0:T(8,128)(2,1)}, u32[]{:S(2)}, u32[]{:S(2)}) %collective-permute-start.5) | collective-permute-done | bytes 1048608 | tf_op jit(solution)/shard_map/ppermute | solution.py:97
  47.5 1.7 broadcast_select_fusion
  49.2 0.0 copy-start.1
  49.2 0.1 collective-permute-start.7
  49.3 9.6 %collective-permute-done.1.refs_4_ = bf16[512,1024]{1,0:T(8,128)(2,1)} collective-permute-done((bf16[512,1024]{1,0:T(8,128)(2,1)S(1)}, bf16[512,1024]{1,0:T(8,128)(2,1)}, u32[]{:S(2)}, u32[]{:S(2)}) %collective-permute-start.1) | collective-permute-done | bytes 1048608 | tf_op jit(solution)/shard_map/ppermute | solution.py:97
  58.9 1.3 broadcast_select_fusion.2
  60.2 0.1 collective-permute-start.4
  60.3 3.0 %collective-permute-start.2 = (bf16[512,1024]{1,0:T(8,128)(2,1)}, bf16[512,1024]{1,0:T(8,128)(2,1)S(1)}, u32[]{:S(2)}, u32[]{:S(2)}) collective-permute-start(bf16[512,1024]{1,0:T(8,128)(2,1)} %collective-permute-done.1.refs_4_), channel_id=1, source_target_pairs={{0,97},{1,32},{2,99},{3,34},{4,101},{5,36},{6,103},{7,38},{8,105},... | collective-permute-start | bytes 3145736 | tf_op jit(solution)/shard_map/ppermute | solution.py:97
  63.3 0.0 collective-permute-done.8.refs_0_.refs_1_.refs_2_
  63.3 0.0 copy-done.1
  63.3 2.1 %project.9.refs_6_ = f32[256,1024]{1,0:T(8,128)S(1)} custom-call(bf16[8,256,512]{2,1,0:T(8,128)(2,1)} %collective-permute-done.8.refs_0_.refs_1_.refs_2_, bf16[8,256,512]{2,1,0:T(8,128)(2,1)} %collective-permute-done.8.refs_0_.refs_1_.refs_2_, bf16[512,1024]{1,0:T(8,128)(2,1)S(1)} %copy-done.1, bf16[512,1024]{1,0:T(8,128)(2,1)S(1)} %collective-permute-done.refs_3_), custom_call_target="tpu_custom_call" | custom-call | flops 536870912 | bytes 4718592 | tf_op jit(solution)/shard_map/project/pallas_call | solution.py:171
  65.4 0.0 collective-permute-done.7.refs_3_
  65.4 2.8 %project.10.refs_6_ = f32[256,1024]{1,0:T(8,128)S(1)} custom-call(bf16[8,256,512]{2,1,0:T(8,128)(2,1)} %collective-permute-done.8.refs_0_.refs_1_.refs_2_, bf16[8,256,512]{2,1,0:T(8,128)(2,1)} %collective-permute-done.8.refs_0_.refs_1_.refs_2_, bf16[8,256,512]{2,1,0:T(8,128)(2,1)} %collective-permute-done.8.refs_0_.refs_1_.refs_2_, ...), custom_call_target="tpu_custom_call" | custom-call | flops 805306368 | bytes 6029312 | tf_op jit(solution)/shard_map/project/pallas_call | solution.py:171
  68.2 6.6 %collective-permute-done.4.refs_4_ = bf16[512,1024]{1,0:T(8,128)(2,1)S(1)} collective-permute-done((bf16[512,1024]{1,0:T(8,128)(2,1)S(1)}, bf16[512,1024]{1,0:T(8,128)(2,1)S(1)}, u32[]{:S(2)}, u32[]{:S(2)}) %collective-permute-start.4) | collective-permute-done | bytes 1048608 | tf_op jit(solution)/shard_map/ppermute | solution.py:97
  74.8 1.2 collective-permute-done.2.refs_3_
  76.0 2.5 %project.11 = f32[256,1024]{1,0:T(8,128)S(1)} custom-call(bf16[8,256,512]{2,1,0:T(8,128)(2,1)} %collective-permute-done.8.refs_0_.refs_1_.refs_2_, bf16[8,256,512]{2,1,0:T(8,128)(2,1)} %collective-permute-done.8.refs_0_.refs_1_.refs_2_, bf16[8,256,512]{2,1,0:T(8,128)(2,1)} %collective-permute-done.8.refs_0_.refs_1_.refs_2_, ...), custom_call_target="tpu_custom_call" | custom-call | flops 805306368 | bytes 6029312 | tf_op jit(solution)/shard_map/project/pallas_call | solution.py:171
  78.5 2.5 %collective-permute-start.9 = (f32[256,1024]{1,0:T(8,128)S(1)}, f32[256,1024]{1,0:T(8,128)S(1)}, u32[]{:S(2)}, u32[]{:S(2)}) collective-permute-start(f32[256,1024]{1,0:T(8,128)S(1)} %project.11), channel_id=1, source_target_pairs={{0,1},{1,0},{2,3},{3,2},{4,5},{5,4},{6,7},{7,6},{8,9},{9,8},{10,11... | collective-permute-start | bytes 3145736 | tf_op jit(solution)/shard_map/ppermute | solution.py:97
  81.0 1.1 project.6.refs_6_
  82.1 2.5 %project.7.refs_6_ = f32[256,1024]{1,0:T(8,128)S(1)} custom-call(bf16[8,256,512]{2,1,0:T(8,128)(2,1)S(1)} %get-tuple-element.4.refs_0_.refs_1_.refs_2_, bf16[8,256,512]{2,1,0:T(8,128)(2,1)S(1)} %get-tuple-element.4.refs_0_.refs_1_.refs_2_, bf16[8,256,512]{2,1,0:T(8,128)(2,1)S(1)} %get-tuple-element.4.refs_0_.refs_1_.refs_2_, ...), custom_call_target="tpu_custom_call" | custom-call | flops 805306368 | bytes 6029312 | tf_op jit(solution)/shard_map/project/pallas_call | solution.py:171
  84.6 1.5 project.8
  86.2 0.0 copy-start.7
  86.2 0.0 copy-start.3
  86.2 0.0 copy-start.5
  86.2 0.0 collective-permute-done.9
  86.2 0.2 add_convert_fusion.refs_0_.refs_8_
  86.4 2.7 %collective-permute-start.10 = (bf16[256,1024]{1,0:T(8,128)(2,1)S(1)}, bf16[256,1024]{1,0:T(8,128)(2,1)S(1)}, u32[]{:S(2)}, u32[]{:S(2)}) collective-permute-start(bf16[256,1024]{1,0:T(8,128)(2,1)S(1)} %add_convert_fusion.refs_0_.refs_8_), channel_id=1, source_target_pairs={{0,16},{1,17},{2,18},{3,19},{4,20},{5,21},{6,22},{7,23},{8,24},{9,... | collective-permute-start | bytes 1572872 | tf_op jit(solution)/shard_map/ppermute | solution.py:97
  89.2 0.0 collective-permute-start.11
  89.2 12.3 %collective-permute-done.10.refs_1_.refs_9_ = bf16[256,1024]{1,0:T(8,128)(2,1)S(1)} collective-permute-done((bf16[256,1024]{1,0:T(8,128)(2,1)S(1)}, bf16[256,1024]{1,0:T(8,128)(2,1)S(1)}, u32[]{:S(2)}, u32[]{:S(2)}) %collective-permute-start.10) | collective-permute-done | bytes 524320 | tf_op jit(solution)/shard_map/ppermute | solution.py:97
  101.4 0.0 collective-permute-start.14
  101.4 0.0 collective-permute-start.12
  101.4 2.7 %collective-permute-start.13 = (bf16[256,1024]{1,0:T(8,128)(2,1)S(1)}, bf16[256,1024]{1,0:T(8,128)(2,1)S(1)}, u32[]{:S(2)}, u32[]{:S(2)}) collective-permute-start(bf16[256,1024]{1,0:T(8,128)(2,1)S(1)} %collective-permute-done.10.refs_1_.refs_9_), channel_id=1, source_target_pairs={{0,32},{1,33},{2,34},{3,35},{4,36},{5,37},{6,38},{7,39},{8,40},{9,... | collective-permute-start | bytes 1572872 | tf_op jit(solution)/shard_map/ppermute | solution.py:97
  104.2 0.0 collective-permute-done.11.refs_2_.refs_10_
  104.2 1.4 collective-permute-start.15
  105.6 9.9 %collective-permute-done.14.refs_5_.refs_13_ = bf16[256,1024]{1,0:T(8,128)(2,1)S(1)} collective-permute-done((bf16[256,1024]{1,0:T(8,128)(2,1)S(1)}, bf16[256,1024]{1,0:T(8,128)(2,1)S(1)}, u32[]{:S(2)}, u32[]{:S(2)}) %collective-permute-start.14) | collective-permute-done | bytes 524320 | tf_op jit(solution)/shard_map/ppermute | solution.py:97
  115.5 0.0 collective-permute-start.16
  115.5 0.9 slice_bitcast_fusion
  116.5 3.1 %collective-permute-start.17 = (bf16[3,8192]{1,0:T(4,128)(2,1)S(1)}, bf16[3,8192]{1,0:T(4,128)(2,1)S(1)}, u32[]{:S(2)}, u32[]{:S(2)}) collective-permute-start(bf16[3,8192]{1,0:T(4,128)(2,1)S(1)} %slice_bitcast_fusion), channel_id=1, source_target_pairs={{0,16},{16,32},{32,48},{48,64},{64,80},{80,96},{96,112},{1,17},{17... | collective-permute-start | bytes 147464 | tf_op jit(solution)/shard_map/ppermute | solution.py:347
  119.6 0.0 copy-done.7
  119.6 0.1 pad_add_fusion.1.info
  119.7 0.1 concatenate.7.info
  119.8 7.7 %collective-permute-done.17.halo_ref = bf16[3,8192]{1,0:T(4,128)(2,1)S(1)} collective-permute-done((bf16[3,8192]{1,0:T(4,128)(2,1)S(1)}, bf16[3,8192]{1,0:T(4,128)(2,1)S(1)}, u32[]{:S(2)}, u32[]{:S(2)}) %collective-permute-start.17) | collective-permute-done | bytes 49184 | tf_op jit(solution)/shard_map/ppermute | solution.py:347
  127.5 0.0 copy-done.3
  127.5 0.0 copy-done.5
  127.5 2.2 %copy-done = bf16[1,256,8192]{2,1,0:T(8,128)(2,1)S(1)} copy-done((bf16[1,256,8192]{2,1,0:T(8,128)(2,1)S(1)}, bf16[1,256,8192]{2,1,0:T(8,128)(2,1)}, u32[]{:S(2)}) %copy-start) | copy-done | bytes 4194328
  129.7 10.4 %conv.1 = bf16[256,8192]{1,0:T(8,128)(2,1)} custom-call(s32[9]{0:T(128)S(1)} %pad_add_fusion.1.info, bf16[256,8192]{1,0:T(8,128)(2,1)S(1)} %bitcast.18, bf16[3,8192]{1,0:T(4,128)(2,1)S(1)} %collective-permute-done.17.halo_ref, f32[4,8192]{1,0:T(4,128)S(1)} %copy-done.3, f32[1,8192]{1,0:T(1,128)S(1)} %bitcast.21), custom_call_target="tpu_custom_call" | custom-call | flops 83886080 | bytes 8388608 | tf_op jit(solution)/shard_map/conv/pallas_call | solution.py:212
  140.2 0.0 collective-permute-done.12.refs_3_.refs_11_
  140.2 0.0 collective-permute-done.13.refs_4_.refs_12_
  140.2 0.0 collective-permute-done.15.refs_6_.refs_14_
  140.2 0.0 collective-permute-done.16.refs_7_.refs_15_
  140.2 38.5 %attend.1 = bf16[256,4096]{1,0:T(8,128)(2,1)} custom-call(s32[17]{0:T(128)S(1)} %concatenate.7.info, bf16[256,4096]{1,0:T(8,128)(2,1)S(1)} %bitcast.22, bf16[256,1024]{1,0:T(8,128)(2,1)S(1)} %add_convert_fusion.refs_0_.refs_8_, bf16[256,1024]{1,0:T(8,128)(2,1)S(1)} %collective-permute-done.10.refs_1_.refs_9_, ...), custom_call_target="tpu_custom_call" | custom-call | flops 8589934592 | bytes 8388608 | tf_op jit(solution)/shard_map/attend/pallas_call | solution.py:302
  (5 shorter events, 0.0 us)
Async XLA Ops:
  0.6 15.1 %collective-permute-start = (bf16[512,1024]{1,0:T(8,128)(2,1)}, bf16[512,1024]{1,0:T(8,128)(2,1)S(1)}, u32[]{:S(2)}, u32[]{:S(2)}) collective-permute-start(bf16[512,1024]{1,0:T(8,128)(2,1)} %refs_2_.3), channel_id=1, source_target_pairs={{0,12},{1,18},{2,14},{3,16},{4,0},{5,22},{6,2},{7,20},{8,4},{9,26}... | collective-permute-start | bytes 3145736 | tf_op jit(solution)/shard_map/ppermute | solution.py:97
  15.8 14.6 %collective-permute-start.3 = (bf16[512,1024]{1,0:T(8,128)(2,1)S(1)}, bf16[512,1024]{1,0:T(8,128)(2,1)}, u32[]{:S(2)}, u32[]{:S(2)}) collective-permute-start(bf16[512,1024]{1,0:T(8,128)(2,1)S(1)} %collective-permute-done.refs_3_), channel_id=1, source_target_pairs={{0,19},{1,16},{2,17},{3,18},{4,23},{5,20},{6,21},{7,22},{8,27},{9,... | collective-permute-start | bytes 3145736 | tf_op jit(solution)/shard_map/ppermute | solution.py:97
  17.3 22.7 %collective-permute-start.6 = (bf16[512,1024]{1,0:T(8,128)(2,1)}, bf16[512,1024]{1,0:T(8,128)(2,1)}, u32[]{:S(2)}, u32[]{:S(2)}) collective-permute-start(bf16[512,1024]{1,0:T(8,128)(2,1)} %refs_2_.3), channel_id=1, source_target_pairs={{0,5},{2,7},{4,9},{6,11},{8,13},{10,15},{12,1},{14,3},{17,20},{19,... | collective-permute-start | bytes 3145736 | tf_op jit(solution)/shard_map/ppermute | solution.py:97
  30.4 17.1 %collective-permute-start.5 = (bf16[512,1024]{1,0:T(8,128)(2,1)}, bf16[512,1024]{1,0:T(8,128)(2,1)}, u32[]{:S(2)}, u32[]{:S(2)}) collective-permute-start(bf16[512,1024]{1,0:T(8,128)(2,1)} %collective-permute-done.3.refs_5_), channel_id=1, source_target_pairs={{0,12},{2,14},{4,0},{6,2},{8,4},{10,6},{12,8},{14,10},{17,29},{19,... | collective-permute-start | bytes 3145736 | tf_op jit(solution)/shard_map/ppermute | solution.py:97
  32.3 26.6 %collective-permute-start.1 = (bf16[512,1024]{1,0:T(8,128)(2,1)S(1)}, bf16[512,1024]{1,0:T(8,128)(2,1)}, u32[]{:S(2)}, u32[]{:S(2)}) collective-permute-start(bf16[512,1024]{1,0:T(8,128)(2,1)S(1)} %collective-permute-done.refs_3_), channel_id=1, source_target_pairs={{0,12},{1,5},{2,14},{3,7},{4,0},{5,9},{6,2},{7,11},{8,4},{9,13},{1... | collective-permute-start | bytes 3145736 | tf_op jit(solution)/shard_map/ppermute | solution.py:97
  33.2 2.2 %copy-start.2 = (bf16[1,256,8192]{2,1,0:T(8,128)(2,1)S(1)}, bf16[1,256,8192]{2,1,0:T(8,128)(2,1)}, u32[]{:S(2)}) copy-start(bf16[1,256,8192]{2,1,0:T(8,128)(2,1)} %param.10) | copy-start | bytes 12582916
  35.4 0.8 copy-start.4
  39.8 23.5 %collective-permute-start.8 = (bf16[8,256,512]{2,1,0:T(8,128)(2,1)}, bf16[8,256,512]{2,1,0:T(8,128)(2,1)}, u32[]{:S(2)}, u32[]{:S(2)}) collective-permute-start(bf16[8,256,512]{2,1,0:T(8,128)(2,1)} %get-tuple-element.5), channel_id=1, source_target_pairs={{0,1},{1,0},{2,3},{3,2},{4,5},{5,4},{6,7},{7,6},{8,9},{9,8},{10,11... | collective-permute-start | bytes 6291464 | tf_op jit(solution)/shard_map/ppermute | solution.py:97
  49.2 14.1 %copy-start.1 = (bf16[512,1024]{1,0:T(8,128)(2,1)S(1)}, bf16[512,1024]{1,0:T(8,128)(2,1)}, u32[]{:S(2)}) copy-start(bf16[512,1024]{1,0:T(8,128)(2,1)} %refs_2_.3) | copy-start | bytes 3145732
  49.2 16.2 %collective-permute-start.7 = (bf16[512,1024]{1,0:T(8,128)(2,1)S(1)}, bf16[512,1024]{1,0:T(8,128)(2,1)S(1)}, u32[]{:S(2)}, u32[]{:S(2)}) collective-permute-start(bf16[512,1024]{1,0:T(8,128)(2,1)S(1)} %get-tuple-element.6), channel_id=1, source_target_pairs={{0,96},{1,33},{2,98},{3,35},{4,100},{5,37},{6,102},{7,39},{8,104},... | collective-permute-start | bytes 3145736 | tf_op jit(solution)/shard_map/ppermute | solution.py:97
  60.2 14.6 %collective-permute-start.4 = (bf16[512,1024]{1,0:T(8,128)(2,1)S(1)}, bf16[512,1024]{1,0:T(8,128)(2,1)S(1)}, u32[]{:S(2)}, u32[]{:S(2)}) collective-permute-start(bf16[512,1024]{1,0:T(8,128)(2,1)S(1)} %broadcast_select_fusion.2), channel_id=1, source_target_pairs={{0,16},{1,4},{2,18},{3,6},{4,20},{5,8},{6,22},{7,10},{8,24},{9,12}... | collective-permute-start | bytes 3145736 | tf_op jit(solution)/shard_map/ppermute | solution.py:97
  60.3 15.7 %collective-permute-start.2 = (bf16[512,1024]{1,0:T(8,128)(2,1)}, bf16[512,1024]{1,0:T(8,128)(2,1)S(1)}, u32[]{:S(2)}, u32[]{:S(2)}) collective-permute-start(bf16[512,1024]{1,0:T(8,128)(2,1)} %collective-permute-done.1.refs_4_), channel_id=1, source_target_pairs={{0,97},{1,32},{2,99},{3,34},{4,101},{5,36},{6,103},{7,38},{8,105},... | collective-permute-start | bytes 3145736 | tf_op jit(solution)/shard_map/ppermute | solution.py:97
  78.5 7.7 %collective-permute-start.9 = (f32[256,1024]{1,0:T(8,128)S(1)}, f32[256,1024]{1,0:T(8,128)S(1)}, u32[]{:S(2)}, u32[]{:S(2)}) collective-permute-start(f32[256,1024]{1,0:T(8,128)S(1)} %project.11), channel_id=1, source_target_pairs={{0,1},{1,0},{2,3},{3,2},{4,5},{5,4},{6,7},{7,6},{8,9},{9,8},{10,11... | collective-permute-start | bytes 3145736 | tf_op jit(solution)/shard_map/ppermute | solution.py:97
  86.2 33.4 %copy-start.7 = (s32[1,8]{1,0:T(1,128)S(1)}, s32[1,8]{1,0:T(1,128)}, u32[]{:S(2)}) copy-start(s32[1,8]{1,0:T(1,128)} %param.17) | copy-start | bytes 100
  86.2 41.3 %copy-start.3 = (f32[4,8192]{1,0:T(4,128)S(1)}, f32[4,8192]{1,0:T(4,128)}, u32[]{:S(2)}) copy-start(f32[4,8192]{1,0:T(4,128)} %w_ref.1) | copy-start | bytes 393220
  86.2 41.3 %copy-start.5 = (f32[8192]{0:T(1024)S(1)}, f32[8192]{0:T(1024)}, u32[]{:S(2)}) copy-start(f32[8192]{0:T(1024)} %param.16) | copy-start | bytes 98308
  86.4 15.0 %collective-permute-start.10 = (bf16[256,1024]{1,0:T(8,128)(2,1)S(1)}, bf16[256,1024]{1,0:T(8,128)(2,1)S(1)}, u32[]{:S(2)}, u32[]{:S(2)}) collective-permute-start(bf16[256,1024]{1,0:T(8,128)(2,1)S(1)} %add_convert_fusion.refs_0_.refs_8_), channel_id=1, source_target_pairs={{0,16},{1,17},{2,18},{3,19},{4,20},{5,21},{6,22},{7,23},{8,24},{9,... | collective-permute-start | bytes 1572872 | tf_op jit(solution)/shard_map/ppermute | solution.py:97
  89.2 15.0 %collective-permute-start.11 = (bf16[256,1024]{1,0:T(8,128)(2,1)S(1)}, bf16[256,1024]{1,0:T(8,128)(2,1)S(1)}, u32[]{:S(2)}, u32[]{:S(2)}) collective-permute-start(bf16[256,1024]{1,0:T(8,128)(2,1)S(1)} %add_convert_fusion.refs_0_.refs_8_), channel_id=1, source_target_pairs={{0,32},{1,33},{2,34},{3,35},{4,36},{5,37},{6,38},{7,39},{8,40},{9,... | collective-permute-start | bytes 1572872 | tf_op jit(solution)/shard_map/ppermute | solution.py:97
  101.4 14.1 %collective-permute-start.14 = (bf16[256,1024]{1,0:T(8,128)(2,1)S(1)}, bf16[256,1024]{1,0:T(8,128)(2,1)S(1)}, u32[]{:S(2)}, u32[]{:S(2)}) collective-permute-start(bf16[256,1024]{1,0:T(8,128)(2,1)S(1)} %collective-permute-done.10.refs_1_.refs_9_), channel_id=1, source_target_pairs={{0,96},{1,97},{2,98},{3,99},{4,100},{5,101},{6,102},{7,103},{8,104... | collective-permute-start | bytes 1572872 | tf_op jit(solution)/shard_map/ppermute | solution.py:97
  101.4 38.7 %collective-permute-start.12 = (bf16[256,1024]{1,0:T(8,128)(2,1)S(1)}, bf16[256,1024]{1,0:T(8,128)(2,1)S(1)}, u32[]{:S(2)}, u32[]{:S(2)}) collective-permute-start(bf16[256,1024]{1,0:T(8,128)(2,1)S(1)} %add_convert_fusion.refs_0_.refs_8_), channel_id=1, source_target_pairs={{0,96},{1,97},{2,98},{3,99},{4,100},{5,101},{6,102},{7,103},{8,104... | collective-permute-start | bytes 1572872 | tf_op jit(solution)/shard_map/ppermute | solution.py:97
  101.4 38.7 %collective-permute-start.13 = (bf16[256,1024]{1,0:T(8,128)(2,1)S(1)}, bf16[256,1024]{1,0:T(8,128)(2,1)S(1)}, u32[]{:S(2)}, u32[]{:S(2)}) collective-permute-start(bf16[256,1024]{1,0:T(8,128)(2,1)S(1)} %collective-permute-done.10.refs_1_.refs_9_), channel_id=1, source_target_pairs={{0,32},{1,33},{2,34},{3,35},{4,36},{5,37},{6,38},{7,39},{8,40},{9,... | collective-permute-start | bytes 1572872 | tf_op jit(solution)/shard_map/ppermute | solution.py:97
  104.2 36.0 %collective-permute-start.15 = (bf16[256,1024]{1,0:T(8,128)(2,1)S(1)}, bf16[256,1024]{1,0:T(8,128)(2,1)}, u32[]{:S(2)}, u32[]{:S(2)}) collective-permute-start(bf16[256,1024]{1,0:T(8,128)(2,1)S(1)} %collective-permute-done.11.refs_2_.refs_10_), channel_id=1, source_target_pairs={{0,32},{1,33},{2,34},{3,35},{4,36},{5,37},{6,38},{7,39},{8,40},{9,... | collective-permute-start | bytes 1572872 | tf_op jit(solution)/shard_map/ppermute | solution.py:97
  115.5 24.7 %collective-permute-start.16 = (bf16[256,1024]{1,0:T(8,128)(2,1)S(1)}, bf16[256,1024]{1,0:T(8,128)(2,1)}, u32[]{:S(2)}, u32[]{:S(2)}) collective-permute-start(bf16[256,1024]{1,0:T(8,128)(2,1)S(1)} %collective-permute-done.14.refs_5_.refs_13_), channel_id=1, source_target_pairs={{0,96},{1,97},{2,98},{3,99},{4,100},{5,101},{6,102},{7,103},{8,104... | collective-permute-start | bytes 1572872 | tf_op jit(solution)/shard_map/ppermute | solution.py:97
  116.5 11.1 %collective-permute-start.17 = (bf16[3,8192]{1,0:T(4,128)(2,1)S(1)}, bf16[3,8192]{1,0:T(4,128)(2,1)S(1)}, u32[]{:S(2)}, u32[]{:S(2)}) collective-permute-start(bf16[3,8192]{1,0:T(4,128)(2,1)S(1)} %slice_bitcast_fusion), channel_id=1, source_target_pairs={{0,16},{16,32},{32,48},{48,64},{64,80},{80,96},{96,112},{1,17},{17... | collective-permute-start | bytes 147464 | tf_op jit(solution)/shard_map/ppermute | solution.py:347
  127.5 2.2 %copy-start = (bf16[1,256,8192]{2,1,0:T(8,128)(2,1)S(1)}, bf16[1,256,8192]{2,1,0:T(8,128)(2,1)}, u32[]{:S(2)}) copy-start(bf16[1,256,8192]{2,1,0:T(8,128)(2,1)} %param.12) | copy-start | bytes 12582916
  129.7 10.5 %copy-start.6 = (bf16[1,256,4096]{2,1,0:T(8,128)(2,1)S(1)}, bf16[1,256,4096]{2,1,0:T(8,128)(2,1)}, u32[]{:S(2)}) copy-start(bf16[1,256,4096]{2,1,0:T(8,128)(2,1)} %param.11) | copy-start | bytes 6291460

commit v2 on v1

v2 whole, which is shorter than its diff:
```python
import functools
import math

import jax
import jax.numpy as jnp
import numpy as np
from jax import lax
from jax.experimental import pallas as pl
from jax.experimental.pallas import tpu as pltpu
from jax.sharding import PartitionSpec as P

HEAD = 128
TAPS = 4
EPISODES = 8
AXES = ("ctx", "fsdp")
CTX, FSDP = 8, 16
DEVICES = CTX * FSDP
MIB = 1 << 20


def place(i):
    c, f = divmod(i, FSDP)
    x, zl = divmod(c, 2)
    y, r = divmod(f, 4)
    zh, k = divmod(r, 2)
    return x, y, zh, zl, k


def device(x, y, zh, zl, k):
    return ((x % 4) * 2 + zl) * FSDP + ((y % 4) * 2 + zh) * 2 + k


def lead_core(x, zl):
    return (x + zl) % 2


def neighbour(x, y, zh, zl, way):
    return {
        "x+": (x + 1, y, zh, zl),
        "x-": (x - 1, y, zh, zl),
        "y+": (x, y + 1, zh, zl),
        "y-": (x, y - 1, zh, zl),
        "zlo": (x, y, zh, 1 - zl),
        "zhi": (x, y, 1 - zh, 1 - zl),
    }[way]


STEPS = (
    ((0, "y-", 0), (1, "zhi", 1)),
    ((0, "y+", 1),),
    ((0, "x-", 1), (1, "zlo", 0)),
    ((0, "y-", 0), (1, "y+", 1)),
    ((0, "zhi", 0), (1, "x+", 1)),
    ((0, "x-", 0), (1, "x+", 1)),
    ((0, "y-", 1), (1, "y+", 0)),
    ((0, "zlo", 0),),
)
SENT = ((0, 0), (0, 0), (1, 1), (1, 1), (1, 2), (4, 4), (5, 4), (5, 5))
SLOT_STEPS = ((0, 0), (1, 1), (3, 3), (4, 4), (5, 5), (6, 6), (7, 7), (8, 2))


def role_of(i):
    x, _, _, zl, k = place(i)
    return 0 if k == lead_core(x, zl) else 1


def weight_plan():
    pairs, held = [], [[i % FSDP for i in range(DEVICES)]]
    for step, sent in zip(STEPS, SENT):
        now, got = [], [-1] * DEVICES
        for i in range(DEVICES):
            for sender, way, receiver in step:
                if sender == role_of(i):
                    nx, ny, nzh, nzl = neighbour(*place(i)[:4], way)
                    lead = lead_core(nx, nzl)
                    to = device(nx, ny, nzh, nzl, lead if receiver == 0 else 1 - lead)
                    now.append((i, to))
                    got[to] = held[sent[role_of(i)]][i]
        pairs.append(now)
        held.append(got)
    slots = [[held[step[role_of(i)]][i] for step in SLOT_STEPS] for i in range(DEVICES)]
    return pairs, np.asarray(slots, np.int32)


WEIGHT_PAIRS, SLOTS = weight_plan()


def moved(way, wanted):
    pairs = [(i, device(*neighbour(*place(i)[:4], way), place(i)[4])) for i in range(DEVICES)]
    return [(i, to) for i, to in pairs if wanted(place(to)[0], place(to)[3])]


SWAP = [(i, i ^ 1) for i in range(DEVICES)]


def send(x, pairs):
    return lax.ppermute(x, AXES, pairs)


def together(*values):
    return lax.optimization_barrier(values)


def params(mib, **kw):
    return pltpu.CompilerParams(vmem_limit_bytes=mib * MIB, **kw)


WHOLE = pl.BlockSpec(memory_space=pltpu.VMEM)
SCALARS = pl.BlockSpec(memory_space=pltpu.SMEM)
BLOCKS = 8
LEAD = 1 + EPISODES + BLOCKS


def hand_on(scalars, token):
    for i in range(LEAD + 1):
        token[i] = scalars[i]


def cost(flops, moved_bytes, trans=0):
    return pl.CostEstimate(
        flops=int(flops), bytes_accessed=int(moved_bytes), transcendentals=int(trans)
    )


def norm_kernel(slots, h_ref, g_ref, mine_ref, other_ref, *, width, chunk, count):
    rows = h_ref.shape[0]
    here = pl.ds(pl.multiple_of(pl.program_id(0) * rows, rows), rows)
    total = jnp.zeros((rows, chunk), jnp.float32)
    for c in range(width // chunk):
        f = h_ref[:, c * chunk : (c + 1) * chunk].astype(jnp.float32)
        total = total + f * f
    mean = jnp.sum(total, axis=-1, keepdims=True) * (1.0 / width)
    factor = lax.rsqrt(mean + 1e-06)
    for which, out in ((1, other_ref), (0, mine_ref)):
        for s in range(count):
            at = pl.multiple_of(slots[which, s] * chunk, chunk)
            f = h_ref[:, pl.ds(at, chunk)].astype(jnp.float32)
            out[s, here, :] = (f * factor * g_ref[:, pl.ds(at, chunk)]).astype(jnp.bfloat16)


def norm(slots, hidden, gain, chunk):
    rows, width = hidden.shape
    count = slots.shape[1]
    tile = 64
    shape = pltpu.VMEM((count, rows, chunk), jnp.bfloat16)
    return pl.pallas_call(
        functools.partial(norm_kernel, width=width, chunk=chunk, count=count),
        grid=(rows // tile,),
        in_specs=[
            pl.BlockSpec(memory_space=pltpu.SMEM),
            pl.BlockSpec((tile, width), lambda i: (i, 0)),
            pl.BlockSpec((1, width), lambda i: (0, 0)),
        ],
        out_specs=[WHOLE, WHOLE],
        out_shape=[shape, shape],
        compiler_params=params(16),
        cost_estimate=cost(rows * width * 6, rows * width * 2),
        name="norm",
    )(slots, hidden, gain)


def project_kernel(scalars, *refs, sides, slots, counts, carried):
    xs, ws = refs[:sides], refs[sides : sides + sum(counts)]
    olds = refs[sides + sum(counts) :][:carried]
    outs, token = refs[-1 - sides : -1], refs[-1]
    hand_on(scalars, token)
    tile = 256
    at = 0
    for s, n in enumerate(counts):
        for c in range(0, ws[at].shape[1], tile):
            cols = slice(c, c + tile)
            w = ws[at][:, cols]
            if n == 2:
                w = jnp.where(scalars[LEAD] > 0, w, ws[at + 1][:, cols])
            for side in range(sides):
                part = jnp.dot(xs[side][slots[s]], w, preferred_element_type=jnp.float32)
                if s:
                    part = outs[side][:, cols] + part
                elif carried:
                    part = olds[side][:, cols] + part
                outs[side][:, cols] = part
        at += n


def project(scalars, xs, slots, weights, carried=()):
    _, rows, depth = xs[0].shape
    weights = [w if isinstance(w, tuple) else (w,) for w in weights]
    counts = tuple(len(w) for w in weights)
    flat = [v for w in weights for v in w]
    columns = flat[0].shape[1]
    sides, count = len(xs), len(slots)
    inside = [pltpu.with_memory_space_constraint(v, pltpu.VMEM) for v in (*xs, *flat, *carried)]
    return pl.pallas_call(
        functools.partial(
            project_kernel, sides=sides, slots=slots, counts=counts, carried=len(carried)
        ),
        in_specs=[SCALARS] + [WHOLE] * len(inside),
        out_specs=[WHOLE] * sides + [SCALARS],
        out_shape=[pltpu.VMEM((rows, columns), jnp.float32)] * sides
        + [jax.ShapeDtypeStruct(scalars.shape, scalars.dtype)],
        compiler_params=params(8),
        cost_estimate=cost(2 * sides * count * rows * depth * columns, rows * columns * 4),
        name="project",
    )(scalars, *inside)


def pick_kernel(scalars, a_ref, b_ref, o_ref, token):
    hand_on(scalars, token)

    @pl.when(scalars[LEAD] > 0)
    def _():
        o_ref[...] = a_ref[...]

    @pl.when(scalars[LEAD] <= 0)
    def _():
        o_ref[...] = b_ref[...]


def pick(scalars, a, b):
    inside = [pltpu.with_memory_space_constraint(v, pltpu.VMEM) for v in (a, b)]
    return pl.pallas_call(
        pick_kernel,
        in_specs=[SCALARS, WHOLE, WHOLE],
        out_specs=[WHOLE, SCALARS],
        out_shape=[
            pltpu.VMEM(a.shape, a.dtype),
            jax.ShapeDtypeStruct(scalars.shape, scalars.dtype),
        ],
        compiler_params=params(8),
        cost_estimate=cost(a.size, a.size),
        name="pick",
    )(scalars, *inside)


def add_kernel(a_ref, b_ref, o_ref):
    o_ref[...] = (a_ref[...] + b_ref[...]).astype(o_ref.dtype)


def add(a, b):
    inside = [pltpu.with_memory_space_constraint(v, pltpu.VMEM) for v in (a, b)]
    return pl.pallas_call(
        add_kernel,
        in_specs=[WHOLE, WHOLE],
        out_specs=WHOLE,
        out_shape=pltpu.VMEM(a.shape, jnp.bfloat16),
        compiler_params=params(8),
        cost_estimate=cost(a.size, a.size),
        name="add",
    )(*inside)


def conv_kernel(info, x_ref, halo_ref, w_ref, b_ref, o_ref, token, pick, before):
    rows, width = x_ref.shape
    ahead = halo_ref.shape[0]
    hand_on(info, token)

    @pl.when(pl.program_id(0) == 0)
    def _():
        before[...] = halo_ref[...]

    shape = (rows, ahead + rows)
    pos = info[0] + pl.program_id(0) * rows + lax.broadcasted_iota(jnp.int32, shape, 0)
    begin = jnp.zeros(shape, jnp.int32)
    for e in range(EPISODES):
        begin = jnp.where(info[1 + e] <= pos, jnp.maximum(begin, info[1 + e]), begin)
    apart = lax.broadcasted_iota(jnp.int32, shape, 0) + ahead - lax.broadcasted_iota(jnp.int32, shape, 1)
    for tap in range(TAPS):
        behind = TAPS - 1 - tap
        taken = (apart == behind) & (pos - behind >= begin)
        pick[tap * rows : (tap + 1) * rows, :] = jnp.where(taken, 1.0, 0.0).astype(pick.dtype)

    lanes = 256
    for c in range(0, width, lanes):
        cols = slice(c, c + lanes)
        source = jnp.concatenate([before[:, cols], x_ref[:, cols]], axis=0)
        taps = jnp.dot(pick[...], source, preferred_element_type=jnp.float32)
        mixing = b_ref[:, cols] + taps[:rows] * w_ref[0:1, cols]
        for tap in range(1, TAPS):
            mixing = mixing + taps[tap * rows : (tap + 1) * rows] * w_ref[tap : tap + 1, cols]
        by_half = 0.5 * mixing
        o_ref[:, cols] = (by_half + by_half * jnp.tanh(by_half)).astype(o_ref.dtype)
    before[...] = x_ref[rows - ahead :, :]


def conv(info, x, halo, weight, bias):
    rows, width = x.shape
    tile = 64
    ahead = halo.shape[0]
    full = lambda n: pl.BlockSpec((n, width), lambda i: (0, 0))
    return pl.pallas_call(
        conv_kernel,
        grid=(rows // tile,),
        in_specs=[
            SCALARS,
            pl.BlockSpec((tile, width), lambda i: (i, 0)),
            full(ahead),
            full(TAPS),
            full(1),
        ],
        out_specs=[pl.BlockSpec((tile, width), lambda i: (i, 0)), SCALARS],
        out_shape=[
            jax.ShapeDtypeStruct((rows, width), x.dtype),
            jax.ShapeDtypeStruct(info.shape, info.dtype),
        ],
        scratch_shapes=[
            pltpu.VMEM((TAPS * tile, ahead + tile), jnp.bfloat16),
            pltpu.VMEM((ahead, width), x.dtype),
        ],
        compiler_params=params(16),
        cost_estimate=cost(rows * width * 40, rows * width * 4, rows * width),
        name="conv",
    )(info, x, halo, weight, bias)


def attend_kernel(info, q_ref, *refs, pieces, per_group, stage, at):
    count = len(pieces)

    ks, vs = refs[: sum(pieces)], refs[sum(pieces) : 2 * sum(pieces)]
    rest = refs[2 * sum(pieces) :]
    if stage == "first":
        m_ref, a_ref, token, mask_ref = rest
        m_in, a_in = m_ref, a_ref
        hand_on(info, token)
    elif stage == "middle":
        m_in, a_in, m_ref, a_ref, token, mask_ref = rest
        hand_on(info, token)
    else:
        m_in, a_in, o_ref, mask_ref = rest
    rows = q_ref.shape[0]
    keys = mask_ref.shape[1]
    factor = math.log2(math.e) / math.sqrt(HEAD)
    first = info[0]
    lowest = jnp.int32(0)
    for e in range(EPISODES):
        start = info[1 + e]
        lowest = jnp.where(start <= first, jnp.maximum(lowest, start), lowest)
    head = pl.program_id(0) * per_group

    def loaded(parts, b):
        at = sum(pieces[:b])
        values = [r[...] for r in parts[at : at + pieces[b]]]
        return values[0] if len(values) == 1 else jnp.concatenate(values, axis=0)

    def divided(h, a):
        o_ref[:, h * HEAD : (h + 1) * HEAD] = (a[:, :HEAD] / a[:, HEAD:]).astype(o_ref.dtype)

    def block(b):
        pos = first + lax.broadcasted_iota(jnp.int32, (rows, keys), 0)
        key_pos = info[1 + EPISODES + at + b] + lax.broadcasted_iota(jnp.int32, (rows, keys), 1)
        begin = jnp.zeros((rows, keys), jnp.int32)
        for e in range(EPISODES):
            begin = jnp.where(info[1 + e] <= pos, jnp.maximum(begin, info[1 + e]), begin)
        allowed = (key_pos >= begin) & (key_pos <= pos)
        mask_ref[...] = jnp.where(allowed, 0.0, -1e30)
        k, v = loaded(ks, b), loaded(vs, b)
        v = jnp.concatenate([v, jnp.ones_like(v)], axis=1)
        for h in range(per_group):
            q = q_ref[:, h * HEAD : (h + 1) * HEAD]
            s = lax.dot_general(
                q, k, (((1,), (1,)), ((), ())), preferred_element_type=jnp.float32
            )
            s = s + mask_ref[...]
            top = jnp.max(s, axis=1, keepdims=True)
            if stage == "first":
                new = jnp.broadcast_to(top, (rows, HEAD))
            else:
                old = m_in[head + h]
                new = jnp.maximum(old, top)
            w = jnp.exp2((s - jnp.concatenate([new] * (keys // HEAD), axis=1)) * factor)
            a = jnp.dot(w.astype(jnp.bfloat16), v, preferred_element_type=jnp.float32)
            if stage != "first":
                shrink = jnp.exp2((old - new) * factor)
                a = a_in[head + h] * jnp.concatenate([shrink, shrink], axis=1) + a
            if stage == "last":
                divided(h, a)
            else:
                a_ref[head + h] = a
                m_ref[head + h] = new

    for b in range(count):
        if stage == "first":
            block(b)
            continue
        base = info[1 + EPISODES + at + b]
        live = (base < first) & (base + keys > lowest)
        pl.when(live)(functools.partial(block, b))
        if stage == "last":

            @pl.when(jnp.logical_not(live))
            def _():
                for h in range(per_group):
                    divided(h, a_in[head + h])


def attend(stage, scalars, at, queries, blocks, state=()):
    rows, width = queries.shape
    blocks = [b if isinstance(b, tuple) else (b,) for b in blocks]
    flat = [v for b in blocks for v in b]
    pieces = [len(b) for b in blocks]
    columns = flat[0].shape[1]
    kv_heads = columns // (2 * HEAD)
    group = width // kv_heads
    heads = width // HEAD
    keys = sum(v.shape[0] for v in blocks[0])
    assert stage != "last" or len(blocks) == 1
    q_spec = pl.BlockSpec((rows, group), lambda g: (0, g))
    if stage == "last":
        out_shape = jax.ShapeDtypeStruct((rows, width), queries.dtype)
        out_specs = q_spec
    else:
        out_shape = [
            pltpu.VMEM((heads, rows, HEAD), jnp.float32),
            pltpu.VMEM((heads, rows, 2 * HEAD), jnp.float32),
            jax.ShapeDtypeStruct(scalars.shape, scalars.dtype),
        ]
        out_specs = [WHOLE, WHOLE, SCALARS]
    in_specs = [pl.BlockSpec(memory_space=pltpu.SMEM), q_spec]
    in_specs += [pl.BlockSpec((v.shape[0], HEAD), lambda g: (0, g)) for v in flat]
    in_specs += [pl.BlockSpec((v.shape[0], HEAD), lambda g: (0, kv_heads + g)) for v in flat]
    in_specs += [WHOLE] * len(state)
    aliases = {} if stage != "middle" else {len(in_specs) - 2: 0, len(in_specs) - 1: 1}
    state = [pltpu.with_memory_space_constraint(v, pltpu.VMEM) for v in state]
    return pl.pallas_call(
        functools.partial(
            attend_kernel, pieces=pieces, per_group=group // HEAD, stage=stage, at=at
        ),
        grid=(kv_heads,),
        in_specs=in_specs,
        out_specs=out_specs,
        out_shape=out_shape,
        input_output_aliases=aliases,
        scratch_shapes=[pltpu.VMEM((rows, keys), jnp.float32)],
        compiler_params=params(12),
        cost_estimate=cost(
            4 * rows * width * keys * len(blocks),
            rows * width * 2 + keys * columns * 2 * len(blocks),
            rows * keys * len(blocks) * heads,
        ),
        name="attend_" + stage,
    )(scalars, queries, *flat, *flat, *state)


def body(
    hidden, queries, conv_input, norm_gain, kv_weight, conv_weight, conv_bias, starts, segment_ids
):
    del segment_ids
    rows = hidden.shape[1]
    ctx = lax.axis_index("ctx")
    me = ctx * FSDP + lax.axis_index("fsdp")
    x, zl = ctx // 2, ctx % 2
    depth = kv_weight.shape[0]
    leads = lax.axis_index("fsdp") % 2 == lead_core(x, zl)
    table = jnp.asarray(SLOTS)
    slots = jnp.stack([table[me], table[me ^ 1]])

    def base(dx, dz):
        return (((x + dx) % 4) * 2 + (zl + dz) % 2) * rows

    bases = [base(0, 0), base(0, 1), base(-1, 0), base(1, 0), base(-1, 1), base(2, 0), base(1, 1), base(2, 1)]
    scalars = jnp.concatenate(
        [(ctx * rows)[None], starts[0], jnp.stack(bases), leads.astype(jnp.int32)[None]]
    )
    signal = conv_input[0]
    tail = signal[rows - 16 :]
    scalars, slots, tail = together(scalars, slots, tail)

    w0 = kv_weight
    w1 = send(w0, WEIGHT_PAIRS[0])
    w2 = send(w0, WEIGHT_PAIRS[1])
    halo = lax.ppermute(tail, "ctx", [(i, i + 1) for i in range(CTX - 1)])
    mine, other = norm(slots, hidden[0], norm_gain[None], depth)
    w1, w2, halo, mine, other = together(w1, w2, halo, mine, other)

    w4 = send(w1, WEIGHT_PAIRS[3])
    theirs = send(other, SWAP)
    picked, scalars = pick(scalars, w1, w2)
    w5 = send(picked, WEIGHT_PAIRS[4])
    w1_later, scalars = together(w1, scalars)
    w3 = send(w1_later, WEIGHT_PAIRS[2])
    *sums, scalars = project(scalars, (theirs, mine), (0, 1), (w0, w1))

    w4, w5, scalars = together(w4, w5, scalars)
    w6 = send(w4, WEIGHT_PAIRS[5])
    picked, scalars = pick(scalars, w5, w4)
    w7 = send(picked, WEIGHT_PAIRS[6])
    w8 = send(w5, WEIGHT_PAIRS[7])
    conv_out, scalars = conv(scalars, signal, halo, conv_weight, conv_bias[None])
    *sums, scalars = project(scalars, (theirs, mine), (2, 3, 4), (w3, w4, w5), sums)

    last = ((5, 6, 7), (w6, w7, (w8, w2)))
    their_sum, _ = project(scalars, (theirs,), *last, (sums[0],))
    back = send(their_sum, SWAP)
    my_sum, _ = project(scalars, (mine,), *last, (sums[1],))
    kv = add(my_sum, back)

    half = rows // 2
    right_end = (0, 3)
    q = queries[0]
    from_right = send(kv, moved("x-", lambda x, z: x in right_end))
    from_pair = send(kv, moved("zlo", lambda x, z: x < 3 or z == 1))
    from_left = send(kv, moved("x+", lambda x, z: x > 0))
    *state, scalars = attend("first", scalars, 0, q, [kv])
    from_right, from_pair, scalars = together(from_right, from_pair, scalars)
    left_pair = send(from_pair, moved("x+", lambda x, z: x > 0))
    right_pair = send(from_right, moved("zlo", lambda x, z: x in right_end))
    far = send(from_right, moved("x-", lambda x, z: x > 1))
    *state, scalars = attend(
        "middle",
        scalars,
        1,
        q,
        [from_pair, from_left, from_right],
        state,
    )
    left_pair, right_pair, scalars = together(left_pair, right_pair, scalars)
    far_top = send(left_pair[:half], moved("x+", lambda x, z: x > 1))
    far_bottom = send(right_pair[half:], moved("x-", lambda x, z: x > 1))
    *state, scalars = attend(
        "middle",
        scalars,
        4,
        q,
        [left_pair, far, right_pair],
        state,
    )
    attended = attend("last", scalars, 7, q, [(far_top, far_bottom)], state)
    return attended[None], conv_out[None]


def solution(mesh):
    return jax.shard_map(
        body,
        mesh=mesh,
        in_specs=(
            P("fsdp", "ctx", None),
            P("fsdp", "ctx", None),
            P("fsdp", "ctx", None),
            P(),
            P("fsdp", None),
            P(),
            P(),
            P("fsdp", None),
            P("fsdp", "ctx"),
        ),
        out_specs=(P("fsdp", "ctx", None), P("fsdp", "ctx", None)),
        check_vma=False,
    )
```

time: 180 us -> 129 us (0.72)
  the two profiles are of different devices: /device:TPU:95 before, /device:TPU:47 now
where the time goes in v2:
time: 129 us; the launch traced here: 128 us
  Pallas kernels  60 us (47%)
  starting transfers between devices  33.6 us (26%)
  waiting for transfers between devices  27.7 us (21%)
  local copies, waits for them, and re-layouts  5.48 us (4%)
    pallas_call x4, Pallas kernels, attend(): pl.pallas_call(functools.partial(attend_kernel, pieces=pieces, per_group=...  39.2 us
    ppermute x18, starting transfers between devices, send(): return lax.ppermute(x, AXES, pairs)  32.3 us
    ppermute x18, waiting for transfers between devices, send(): return lax.ppermute(x, AXES, pairs)  22.7 us
    pallas_call x4, Pallas kernels, project(): pl.pallas_call(functools.partial(project_kernel, sides=sides, slots=slots...  8.69 us
    pallas_call x1, Pallas kernels, conv(): pl.pallas_call(conv_kernel, grid=(rows // tile,), in_specs=[SCALARS, pl.B...  7.07 us
    ppermute x1, waiting for transfers between devices, body(): halo = lax.ppermute(tail, 'ctx', [(i, i + 1) for i in range(CTX - 1)])  5.08 us
    unnamed x14, local copies, waits for them, and re-layouts  2.96 us
  transfers between devices with their start and end apart: 19, of which 8 were waited for; matrix products, arithmetic and copies ran while one was open for 2% of the time, Pallas kernels for 40%

profile of v2, /device:TPU:47, one launch (start us, length us, event | category | flops | bytes accessed | tf_op | source)
XLA Modules:
  0.0 127.9 jit_solution(12372094780353122608)
XLA Ops:
  0.6 2.3 %collective-permute-start = (bf16[512,1024]{1,0:T(8,128)(2,1)}, bf16[512,1024]{1,0:T(8,128)(2,1)S(1)}, u32[]{:S(2)}, u32[]{:S(2)}) collective-permute-start(bf16[512,1024]{1,0:T(8,128)(2,1)} %refs_2_.1), channel_id=1, source_target_pairs={{0,12},{1,18},{2,14},{3,16},{4,0},{5,22},{6,2},{7,20},{8,4},{9,26}... | collective-permute-start | bytes 3145736 | tf_op jit(solution)/shard_map/ppermute | solution.py:97
  2.9 1.3 %collective-permute-start.1 = (bf16[512,1024]{1,0:T(8,128)(2,1)}, bf16[512,1024]{1,0:T(8,128)(2,1)S(1)}, u32[]{:S(2)}, u32[]{:S(2)}) collective-permute-start(bf16[512,1024]{1,0:T(8,128)(2,1)} %refs_2_.1), channel_id=1, source_target_pairs={{0,5},{2,7},{4,9},{6,11},{8,13},{10,15},{12,1},{14,3},{17,20},{19,... | collective-permute-start | bytes 3145736 | tf_op jit(solution)/shard_map/ppermute | solution.py:97
  4.2 1.0 slice_bitcast_fusion
  5.3 0.7 concatenate.3.scalars
  6.0 0.8 constant_dynamic-slice_fusion.1
  6.8 1.3 %collective-permute-start.2 = (bf16[16,8192]{1,0:T(8,128)(2,1)S(1)}, bf16[16,8192]{1,0:T(8,128)(2,1)S(1)}, u32[]{:S(2)}, u32[]{:S(2)}) collective-permute-start(bf16[16,8192]{1,0:T(8,128)(2,1)S(1)} %slice_bitcast_fusion), channel_id=1, source_target_pairs={{0,16},{16,32},{32,48},{48,64},{64,80},{80,96},{96,112},{1,17},{17... | collective-permute-start | bytes 786440 | tf_op jit(solution)/shard_map/ppermute | solution.py:470
  8.1 0.0 copy-start.2
  8.1 2.2 %copy-done.2 = bf16[1,256,8192]{2,1,0:T(8,128)(2,1)S(1)} copy-done((bf16[1,256,8192]{2,1,0:T(8,128)(2,1)S(1)}, bf16[1,256,8192]{2,1,0:T(8,128)(2,1)}, u32[]{:S(2)}) %copy-start.2) | copy-done | bytes 4194328
  10.3 0.0 copy-start.5
  10.3 0.8 copy-done.5
  11.1 0.0 copy-start.3
  11.1 2.5 %norm.1 = (bf16[8,256,512]{2,1,0:T(8,128)(2,1)S(1)}, bf16[8,256,512]{2,1,0:T(8,128)(2,1)S(1)}) custom-call(s32[2,8]{1,0:T(2,128)S(1)} %pad_add_fusion.slots, bf16[256,8192]{1,0:T(8,128)(2,1)S(1)} %bitcast.25, f32[1,8192]{1,0:T(1,128)S(1)} %bitcast.26), custom_call_target="tpu_custom_call" | custom-call | flops 12582912 | bytes 4194304 | tf_op jit(solution)/shard_map/norm/pallas_call | solution.py:146
  13.6 5.1 %collective-permute-done.2.halo_ref = bf16[16,8192]{1,0:T(8,128)(2,1)S(1)} collective-permute-done((bf16[16,8192]{1,0:T(8,128)(2,1)S(1)}, bf16[16,8192]{1,0:T(8,128)(2,1)S(1)}, u32[]{:S(2)}, u32[]{:S(2)}) %collective-permute-start.2) | collective-permute-done | bytes 262176 | tf_op jit(solution)/shard_map/ppermute | solution.py:470
  18.7 0.0 collective-permute-done.a_ref.refs_3_
  18.7 0.6 collective-permute-done.1.b_ref.refs_4_
  19.2 0.4 collective-permute-start.5
  19.6 1.2 pick.2
  20.9 0.1 collective-permute-start.4
  20.9 1.1 collective-permute-start.3
  22.0 2.1 %collective-permute-start.6 = (bf16[512,1024]{1,0:T(8,128)(2,1)S(1)}, bf16[512,1024]{1,0:T(8,128)(2,1)S(1)}, u32[]{:S(2)}, u32[]{:S(2)}) collective-permute-start(bf16[512,1024]{1,0:T(8,128)(2,1)S(1)} %collective-permute-done.a_ref.refs_3_), channel_id=1, source_target_pairs={{0,96},{1,17},{2,98},{3,19},{4,100},{5,21},{6,102},{7,23},{8,104},... | collective-permute-start | bytes 3145736 | tf_op jit(solution)/shard_map/ppermute | solution.py:97
  24.1 0.0 collective-permute-done.5.refs_0_
  24.1 0.0 copy-done.3
  24.2 2.3 %project.4 = (f32[256,1024]{1,0:T(8,128)S(1)}, f32[256,1024]{1,0:T(8,128)S(1)}, s32[18]{0:T(128)S(1)}) custom-call(s32[18]{0:T(128)S(1)} %get-tuple-element.55.scalars, bf16[8,256,512]{2,1,0:T(8,128)(2,1)S(1)} %collective-permute-done.5.refs_0_, bf16[8,256,512]{2,1,0:T(8,128)(2,1)S(1)} %get-tuple-element.57.refs_1_.refs_0_, bf16[512,1024]{1,0:T(8,128)(2,1)S(1)} %copy-done.3, ...), custom_call_target="tpu_custom_call" | custom-call | flops 1073741824 | bytes 1048576 | tf_op jit(solution)/shard_map/project/pallas_call | solution.py:193
  26.4 9.0 %collective-permute-done.4.a_ref.refs_4_ = bf16[512,1024]{1,0:T(8,128)(2,1)S(1)} collective-permute-done((bf16[512,1024]{1,0:T(8,128)(2,1)S(1)}, bf16[512,1024]{1,0:T(8,128)(2,1)S(1)}, u32[]{:S(2)}, u32[]{:S(2)}) %collective-permute-start.4) | collective-permute-done | bytes 1048608 | tf_op jit(solution)/shard_map/ppermute | solution.py:97
  35.5 0.0 collective-permute-done.3.b_ref.refs_3_
  35.5 1.2 pick.3
  36.7 1.7 %collective-permute-start.8 = (bf16[512,1024]{1,0:T(8,128)(2,1)S(1)}, bf16[512,1024]{1,0:T(8,128)(2,1)S(1)}, u32[]{:S(2)}, u32[]{:S(2)}) collective-permute-start(bf16[512,1024]{1,0:T(8,128)(2,1)S(1)} %get-tuple-element.69), channel_id=1, source_target_pairs={{0,13},{1,4},{2,15},{3,6},{4,1},{5,8},{6,3},{7,10},{8,5},{9,12},{1... | collective-permute-start | bytes 3145736 | tf_op jit(solution)/shard_map/ppermute | solution.py:97
  38.4 0.7 collective-permute-start.9
  39.1 0.6 collective-permute-start.7
  39.7 0.0 copy-done.1
  39.7 0.0 copy-done.4
  39.7 0.0 copy-done.6
  39.8 7.1 %conv.1 = (bf16[256,8192]{1,0:T(8,128)(2,1)}, s32[18]{0:T(128)S(1)}) custom-call(s32[18]{0:T(128)S(1)} %get-tuple-element.62.info, bf16[256,8192]{1,0:T(8,128)(2,1)S(1)} %bitcast.24, bf16[16,8192]{1,0:T(8,128)(2,1)S(1)} %collective-permute-done.2.halo_ref, f32[4,8192]{1,0:T(4,128)S(1)} %copy-done.4, f32[1,8192]{1,0:T(1,128)S(1)} %bitcast.27), custom_call_target="tpu_custom_call" | custom-call | flops 83886080 | bytes 8388608 | tf_op jit(solution)/shard_map/conv/pallas_call | solution.py:290
  46.8 0.0 collective-permute-done.6.refs_2_
  46.8 2.7 %project.5 = (f32[256,1024]{1,0:T(8,128)S(1)}, f32[256,1024]{1,0:T(8,128)S(1)}, s32[18]{0:T(128)S(1)}) custom-call(s32[18]{0:T(128)S(1)} %get-tuple-element.64.scalars, bf16[8,256,512]{2,1,0:T(8,128)(2,1)S(1)} %collective-permute-done.5.refs_0_, bf16[8,256,512]{2,1,0:T(8,128)(2,1)S(1)} %get-tuple-element.57.refs_1_.refs_0_, ...), custom_call_target="tpu_custom_call" | custom-call | flops 1610612736 | bytes 1048576 | tf_op jit(solution)/shard_map/project/pallas_call | solution.py:193
  49.5 1.7 %collective-permute-done.8.refs_2_ = bf16[512,1024]{1,0:T(8,128)(2,1)S(1)} collective-permute-done((bf16[512,1024]{1,0:T(8,128)(2,1)S(1)}, bf16[512,1024]{1,0:T(8,128)(2,1)S(1)}, u32[]{:S(2)}, u32[]{:S(2)}) %collective-permute-start.8) | collective-permute-done | bytes 1048608 | tf_op jit(solution)/shard_map/ppermute | solution.py:97
  51.3 0.0 collective-permute-done.9.refs_3_
  51.3 2.4 %collective-permute-done.7.refs_1_ = bf16[512,1024]{1,0:T(8,128)(2,1)S(1)} collective-permute-done((bf16[512,1024]{1,0:T(8,128)(2,1)S(1)}, bf16[512,1024]{1,0:T(8,128)(2,1)S(1)}, u32[]{:S(2)}, u32[]{:S(2)}) %collective-permute-start.7) | collective-permute-done | bytes 1048608 | tf_op jit(solution)/shard_map/ppermute | solution.py:97
  53.7 1.9 %project.7 = (f32[256,1024]{1,0:T(8,128)S(1)}, s32[18]{0:T(128)}) custom-call(s32[18]{0:T(128)S(1)} %get-tuple-element.68.scalars.info, bf16[8,256,512]{2,1,0:T(8,128)(2,1)S(1)} %collective-permute-done.5.refs_0_, bf16[512,1024]{1,0:T(8,128)(2,1)S(1)} %collective-permute-done.7.refs_1_, bf16[512,1024]{1,0:T(8,128)(2,1)S(1)} %collective-permute-done.8.refs_2_, ...), custom_call_target="tpu_custom_call" | custom-call | flops 805306368 | bytes 1048576 | tf_op jit(solution)/shard_map/project/pallas_call | solution.py:193
  55.6 5.8 %collective-permute-start.10 = (f32[256,1024]{1,0:T(8,128)S(1)}, f32[256,1024]{1,0:T(8,128)S(1)}, u32[]{:S(2)}, u32[]{:S(2)}) collective-permute-start(f32[256,1024]{1,0:T(8,128)S(1)} %get-tuple-element.73), channel_id=1, source_target_pairs={{0,1},{1,0},{2,3},{3,2},{4,5},{5,4},{6,7},{7,6},{8,9},{9,8},{10,11... | collective-permute-start | bytes 3145736 | tf_op jit(solution)/shard_map/ppermute | solution.py:97
  61.4 1.8 %project.6 = (f32[256,1024]{1,0:T(8,128)S(1)}, s32[18]{0:T(128)}) custom-call(s32[18]{0:T(128)S(1)} %get-tuple-element.68.scalars.info, bf16[8,256,512]{2,1,0:T(8,128)(2,1)S(1)} %get-tuple-element.57.refs_1_.refs_0_, bf16[512,1024]{1,0:T(8,128)(2,1)S(1)} %collective-permute-done.7.refs_1_, bf16[512,1024]{1,0:T(8,128)(2,1)S(1)} %collective-permute-done.8.refs_2_, ...), custom_call_target="tpu_custom_call" | custom-call | flops 805306368 | bytes 1048576 | tf_op jit(solution)/shard_map/project/pallas_call | solution.py:193
  63.2 0.4 collective-permute-done.10.b_ref
  63.7 0.2 add.121.refs_0_.refs_1_
  63.9 1.3 %collective-permute-start.12 = (bf16[256,1024]{1,0:T(8,128)(2,1)S(1)}, bf16[256,1024]{1,0:T(8,128)(2,1)S(1)}, u32[]{:S(2)}, u32[]{:S(2)}) collective-permute-start(bf16[256,1024]{1,0:T(8,128)(2,1)S(1)} %add.121.refs_0_.refs_1_), channel_id=1, source_target_pairs={{0,16},{1,17},{2,18},{3,19},{4,20},{5,21},{6,22},{7,23},{8,24},{9,... | collective-permute-start | bytes 1572872 | tf_op jit(solution)/shard_map/ppermute | solution.py:97
  65.2 1.3 %collective-permute-start.11 = (bf16[256,1024]{1,0:T(8,128)(2,1)S(1)}, bf16[256,1024]{1,0:T(8,128)(2,1)S(1)}, u32[]{:S(2)}, u32[]{:S(2)}) collective-permute-start(bf16[256,1024]{1,0:T(8,128)(2,1)S(1)} %add.121.refs_0_.refs_1_), channel_id=1, source_target_pairs={{0,96},{1,97},{2,98},{3,99},{4,100},{5,101},{6,102},{7,103},{8,104... | collective-permute-start | bytes 1572872 | tf_op jit(solution)/shard_map/ppermute | solution.py:97
  66.5 1.3 %collective-permute-start.15 = (bf16[256,1024]{1,0:T(8,128)(2,1)S(1)}, bf16[256,1024]{1,0:T(8,128)(2,1)S(1)}, u32[]{:S(2)}, u32[]{:S(2)}) collective-permute-start(bf16[256,1024]{1,0:T(8,128)(2,1)S(1)} %add.121.refs_0_.refs_1_), channel_id=1, source_target_pairs={{0,32},{1,33},{2,34},{3,35},{4,36},{5,37},{6,38},{7,39},{8,40},{9,... | collective-permute-start | bytes 1572872 | tf_op jit(solution)/shard_map/ppermute | solution.py:97
  67.8 0.0 copy-done
  67.8 5.2 %attend_first.1 = (f32[32,256,128]{2,1,0:T(8,128)S(1)}, f32[32,256,256]{2,1,0:T(8,128)S(1)}, s32[18]{0:T(128)S(1)}) custom-call(s32[18]{0:T(128)S(1)} %get-tuple-element.68.scalars.info, bf16[256,4096]{1,0:T(8,128)(2,1)S(1)} %bitcast.20, bf16[256,1024]{1,0:T(8,128)(2,1)S(1)} %add.121.refs_0_.refs_1_, bf16[256,1024]{1,0:T(8,128)(2,1)S(1)} %add.121.refs_0_.refs_1_), custom_call_target="tpu_custom_call" | custom-call | flops 1073741824 | bytes 2621440 | tf_op jit(solution)/shard_map/attend_first/pallas_call | solution.py:423
  73.0 5.9 %collective-permute-done.12.refs_0_.refs_3_ = bf16[256,1024]{1,0:T(8,128)(2,1)S(1)} collective-permute-done((bf16[256,1024]{1,0:T(8,128)(2,1)S(1)}, bf16[256,1024]{1,0:T(8,128)(2,1)S(1)}, u32[]{:S(2)}, u32[]{:S(2)}) %collective-permute-start.12) | collective-permute-done | bytes 524320 | tf_op jit(solution)/shard_map/ppermute | solution.py:97
  78.9 2.5 %collective-permute-done.11.refs_2_.refs_5_ = bf16[256,1024]{1,0:T(8,128)(2,1)S(1)} collective-permute-done((bf16[256,1024]{1,0:T(8,128)(2,1)S(1)}, bf16[256,1024]{1,0:T(8,128)(2,1)S(1)}, u32[]{:S(2)}, u32[]{:S(2)}) %collective-permute-start.11) | collective-permute-done | bytes 524320 | tf_op jit(solution)/shard_map/ppermute | solution.py:97
  81.4 1.3 %collective-permute-start.13 = (bf16[256,1024]{1,0:T(8,128)(2,1)S(1)}, bf16[256,1024]{1,0:T(8,128)(2,1)S(1)}, u32[]{:S(2)}, u32[]{:S(2)}) collective-permute-start(bf16[256,1024]{1,0:T(8,128)(2,1)S(1)} %collective-permute-done.12.refs_0_.refs_3_), channel_id=1, source_target_pairs={{0,32},{1,33},{2,34},{3,35},{4,36},{5,37},{6,38},{7,39},{8,40},{9,... | collective-permute-start | bytes 1572872 | tf_op jit(solution)/shard_map/ppermute | solution.py:97
  82.7 3.7 %collective-permute-start.14 = (bf16[256,1024]{1,0:T(8,128)(2,1)S(1)}, bf16[256,1024]{1,0:T(8,128)(2,1)S(1)}, u32[]{:S(2)}, u32[]{:S(2)}) collective-permute-start(bf16[256,1024]{1,0:T(8,128)(2,1)S(1)} %collective-permute-done.11.refs_2_.refs_5_), channel_id=1, source_target_pairs={{0,16},{1,17},{2,18},{3,19},{4,20},{5,21},{6,22},{7,23},{8,24},{9,... | collective-permute-start | bytes 1572872 | tf_op jit(solution)/shard_map/ppermute | solution.py:97
  86.4 2.1 %collective-permute-start.16 = (bf16[256,1024]{1,0:T(8,128)(2,1)S(1)}, bf16[256,1024]{1,0:T(8,128)(2,1)S(1)}, u32[]{:S(2)}, u32[]{:S(2)}) collective-permute-start(bf16[256,1024]{1,0:T(8,128)(2,1)S(1)} %collective-permute-done.11.refs_2_.refs_5_), channel_id=1, source_target_pairs={{0,96},{1,97},{2,98},{3,99},{4,100},{5,101},{6,102},{7,103},{8,104... | collective-permute-start | bytes 1572872 | tf_op jit(solution)/shard_map/ppermute | solution.py:97
  88.5 0.0 collective-permute-done.15.refs_1_.refs_4_
  88.5 16.1 %attend_middle.2 = (f32[32,256,128]{2,1,0:T(8,128)S(1)}, f32[32,256,256]{2,1,0:T(8,128)S(1)}, s32[18]{0:T(128)S(1)}) custom-call(s32[18]{0:T(128)S(1)} %get-tuple-element.77.info, bf16[256,4096]{1,0:T(8,128)(2,1)S(1)} %bitcast.21, bf16[256,1024]{1,0:T(8,128)(2,1)S(1)} %collective-permute-done.12.refs_0_.refs_3_, ...), custom_call_target="tpu_custom_call", output_to_operand_aliasing={{0}: (8, {}), {1}: (9, {})} | custom-call | flops 3221225472 | bytes 3670016 | tf_op jit(solution)/shard_map/attend_middle/pallas_call | solution.py:423
  104.6 0.0 collective-permute-done.13.refs_0_.refs_3_
  104.6 0.0 collective-permute-done.14.refs_2_.refs_5_
  104.7 1.3 %collective-permute-start.17 = (bf16[128,1024]{1,0:T(8,128)(2,1)S(1)}, bf16[128,1024]{1,0:T(8,128)(2,1)S(1)}, u32[]{:S(2)}, u32[]{:S(2)}) collective-permute-start(bf16[128,1024]{1,0:T(8,128)(2,1)S(1)} %slice.14), channel_id=1, source_target_pairs={{32,64},{33,65},{34,66},{35,67},{36,68},{37,69},{38,70},{39,71},{4... | collective-permute-start | bytes 786440 | tf_op jit(solution)/shard_map/ppermute | solution.py:97
  106.0 4.0 %collective-permute-start.18 = (bf16[128,1024]{1,0:T(8,128)(2,1)S(1)}, bf16[128,1024]{1,0:T(8,128)(2,1)S(1)}, u32[]{:S(2)}, u32[]{:S(2)}) collective-permute-start(bf16[128,1024]{1,0:T(8,128)(2,1)S(1)} %slice.15), channel_id=1, source_target_pairs={{0,96},{1,97},{2,98},{3,99},{4,100},{5,101},{6,102},{7,103},{8,104... | collective-permute-start | bytes 786440 | tf_op jit(solution)/shard_map/ppermute | solution.py:97
  110.0 0.0 collective-permute-done.16.refs_1_.refs_4_
  110.0 11.4 %attend_middle.3 = (f32[32,256,128]{2,1,0:T(8,128)S(1)}, f32[32,256,256]{2,1,0:T(8,128)S(1)}, s32[18]{0:T(128)S(1)}) custom-call(s32[18]{0:T(128)S(1)} %get-tuple-element.81.info, bf16[256,4096]{1,0:T(8,128)(2,1)S(1)} %bitcast.22, bf16[256,1024]{1,0:T(8,128)(2,1)S(1)} %collective-permute-done.13.refs_0_.refs_3_, ...), custom_call_target="tpu_custom_call", output_to_operand_aliasing={{0}: (8, {}), {1}: (9, {})} | custom-call | flops 3221225472 | bytes 3670016 | tf_op jit(solution)/shard_map/attend_middle/pallas_call | solution.py:423
  121.4 0.0 collective-permute-done.17.refs_0_.refs_2_
  121.4 0.0 collective-permute-done.18.refs_1_.refs_3_
  121.4 6.5 %attend_last.1 = bf16[256,4096]{1,0:T(8,128)(2,1)} custom-call(s32[18]{0:T(128)S(1)} %get-tuple-element.86.info, bf16[256,4096]{1,0:T(8,128)(2,1)S(1)} %bitcast.23, bf16[128,1024]{1,0:T(8,128)(2,1)S(1)} %collective-permute-done.17.refs_0_.refs_2_, bf16[128,1024]{1,0:T(8,128)(2,1)S(1)} %collective-permute-done.18.refs_1_.refs_3_, ...), custom_call_target="tpu_custom_call" | custom-call | flops 1073741824 | bytes 2621440 | tf_op jit(solution)/shard_map/attend_last/pallas_call | solution.py:423
  (7 shorter events, 0.1 us)
Async XLA Ops:
  0.6 18.0 %collective-permute-start = (bf16[512,1024]{1,0:T(8,128)(2,1)}, bf16[512,1024]{1,0:T(8,128)(2,1)S(1)}, u32[]{:S(2)}, u32[]{:S(2)}) collective-permute-start(bf16[512,1024]{1,0:T(8,128)(2,1)} %refs_2_.1), channel_id=1, source_target_pairs={{0,12},{1,18},{2,14},{3,16},{4,0},{5,22},{6,2},{7,20},{8,4},{9,26}... | collective-permute-start | bytes 3145736 | tf_op jit(solution)/shard_map/ppermute | solution.py:97
  2.9 16.3 %collective-permute-start.1 = (bf16[512,1024]{1,0:T(8,128)(2,1)}, bf16[512,1024]{1,0:T(8,128)(2,1)S(1)}, u32[]{:S(2)}, u32[]{:S(2)}) collective-permute-start(bf16[512,1024]{1,0:T(8,128)(2,1)} %refs_2_.1), channel_id=1, source_target_pairs={{0,5},{2,7},{4,9},{6,11},{8,13},{10,15},{12,1},{14,3},{17,20},{19,... | collective-permute-start | bytes 3145736 | tf_op jit(solution)/shard_map/ppermute | solution.py:97
  6.8 11.8 %collective-permute-start.2 = (bf16[16,8192]{1,0:T(8,128)(2,1)S(1)}, bf16[16,8192]{1,0:T(8,128)(2,1)S(1)}, u32[]{:S(2)}, u32[]{:S(2)}) collective-permute-start(bf16[16,8192]{1,0:T(8,128)(2,1)S(1)} %slice_bitcast_fusion), channel_id=1, source_target_pairs={{0,16},{16,32},{32,48},{48,64},{64,80},{80,96},{96,112},{1,17},{17... | collective-permute-start | bytes 786440 | tf_op jit(solution)/shard_map/ppermute | solution.py:470
  8.1 2.2 %copy-start.2 = (bf16[1,256,8192]{2,1,0:T(8,128)(2,1)S(1)}, bf16[1,256,8192]{2,1,0:T(8,128)(2,1)}, u32[]{:S(2)}) copy-start(bf16[1,256,8192]{2,1,0:T(8,128)(2,1)} %param.10) | copy-start | bytes 12582916
  10.3 0.8 copy-start.5
  11.1 13.1 %copy-start.3 = (bf16[512,1024]{1,0:T(8,128)(2,1)S(1)}, bf16[512,1024]{1,0:T(8,128)(2,1)}, u32[]{:S(2)}) copy-start(bf16[512,1024]{1,0:T(8,128)(2,1)} %refs_2_.1) | copy-start | bytes 3145732
  19.2 4.9 %collective-permute-start.5 = (bf16[8,256,512]{2,1,0:T(8,128)(2,1)S(1)}, bf16[8,256,512]{2,1,0:T(8,128)(2,1)S(1)}, u32[]{:S(2)}, u32[]{:S(2)}) collective-permute-start(bf16[8,256,512]{2,1,0:T(8,128)(2,1)S(1)} %get-tuple-element.56), channel_id=1, source_target_pairs={{0,1},{1,0},{2,3},{3,2},{4,5},{5,4},{6,7},{7,6},{8,9},{9,8},{10,11... | collective-permute-start | bytes 6291464 | tf_op jit(solution)/shard_map/ppermute | solution.py:97
  20.9 14.6 %collective-permute-start.4 = (bf16[512,1024]{1,0:T(8,128)(2,1)S(1)}, bf16[512,1024]{1,0:T(8,128)(2,1)S(1)}, u32[]{:S(2)}, u32[]{:S(2)}) collective-permute-start(bf16[512,1024]{1,0:T(8,128)(2,1)S(1)} %get-tuple-element.53), channel_id=1, source_target_pairs={{0,19},{1,32},{2,17},{3,34},{4,23},{5,36},{6,21},{7,38},{8,27},{9,... | collective-permute-start | bytes 3145736 | tf_op jit(solution)/shard_map/ppermute | solution.py:97
  20.9 14.5 %collective-permute-start.3 = (bf16[512,1024]{1,0:T(8,128)(2,1)S(1)}, bf16[512,1024]{1,0:T(8,128)(2,1)S(1)}, u32[]{:S(2)}, u32[]{:S(2)}) collective-permute-start(bf16[512,1024]{1,0:T(8,128)(2,1)S(1)} %collective-permute-done.a_ref.refs_3_), channel_id=1, source_target_pairs={{0,12},{1,5},{2,14},{3,7},{4,0},{5,9},{6,2},{7,11},{8,4},{9,13},{1... | collective-permute-start | bytes 3145736 | tf_op jit(solution)/shard_map/ppermute | solution.py:97
  22.0 17.7 %copy-start.1 = (bf16[1,256,8192]{2,1,0:T(8,128)(2,1)S(1)}, bf16[1,256,8192]{2,1,0:T(8,128)(2,1)}, u32[]{:S(2)}) copy-start(bf16[1,256,8192]{2,1,0:T(8,128)(2,1)} %param.12) | copy-start | bytes 12582916
  22.0 17.7 %copy-start.4 = (f32[4,8192]{1,0:T(4,128)S(1)}, f32[4,8192]{1,0:T(4,128)}, u32[]{:S(2)}) copy-start(f32[4,8192]{1,0:T(4,128)} %w_ref.1) | copy-start | bytes 393220
  22.0 17.7 %copy-start.6 = (f32[8192]{0:T(1024)S(1)}, f32[8192]{0:T(1024)}, u32[]{:S(2)}) copy-start(f32[8192]{0:T(1024)} %param.16) | copy-start | bytes 98308
  22.0 24.8 %collective-permute-start.6 = (bf16[512,1024]{1,0:T(8,128)(2,1)S(1)}, bf16[512,1024]{1,0:T(8,128)(2,1)S(1)}, u32[]{:S(2)}, u32[]{:S(2)}) collective-permute-start(bf16[512,1024]{1,0:T(8,128)(2,1)S(1)} %collective-permute-done.a_ref.refs_3_), channel_id=1, source_target_pairs={{0,96},{1,17},{2,98},{3,19},{4,100},{5,21},{6,102},{7,23},{8,104},... | collective-permute-start | bytes 3145736 | tf_op jit(solution)/shard_map/ppermute | solution.py:97
  36.7 14.6 %collective-permute-start.8 = (bf16[512,1024]{1,0:T(8,128)(2,1)S(1)}, bf16[512,1024]{1,0:T(8,128)(2,1)S(1)}, u32[]{:S(2)}, u32[]{:S(2)}) collective-permute-start(bf16[512,1024]{1,0:T(8,128)(2,1)S(1)} %get-tuple-element.69), channel_id=1, source_target_pairs={{0,13},{1,4},{2,15},{3,6},{4,1},{5,8},{6,3},{7,10},{8,5},{9,12},{1... | collective-permute-start | bytes 3145736 | tf_op jit(solution)/shard_map/ppermute | solution.py:97
  38.4 12.9 %collective-permute-start.9 = (bf16[512,1024]{1,0:T(8,128)(2,1)S(1)}, bf16[512,1024]{1,0:T(8,128)(2,1)S(1)}, u32[]{:S(2)}, u32[]{:S(2)}) collective-permute-start(bf16[512,1024]{1,0:T(8,128)(2,1)S(1)} %collective-permute-done.4.a_ref.refs_4_), channel_id=1, source_target_pairs={{0,17},{2,19},{4,21},{6,23},{8,25},{10,27},{12,29},{14,31},{17,0},... | collective-permute-start | bytes 3145736 | tf_op jit(solution)/shard_map/ppermute | solution.py:97
  39.1 14.6 %collective-permute-start.7 = (bf16[512,1024]{1,0:T(8,128)(2,1)S(1)}, bf16[512,1024]{1,0:T(8,128)(2,1)S(1)}, u32[]{:S(2)}, u32[]{:S(2)}) collective-permute-start(bf16[512,1024]{1,0:T(8,128)(2,1)S(1)} %collective-permute-done.3.b_ref.refs_3_), channel_id=1, source_target_pairs={{0,97},{1,32},{2,99},{3,34},{4,101},{5,36},{6,103},{7,38},{8,105},... | collective-permute-start | bytes 3145736 | tf_op jit(solution)/shard_map/ppermute | solution.py:97
  55.6 8.1 %collective-permute-start.10 = (f32[256,1024]{1,0:T(8,128)S(1)}, f32[256,1024]{1,0:T(8,128)S(1)}, u32[]{:S(2)}, u32[]{:S(2)}) collective-permute-start(f32[256,1024]{1,0:T(8,128)S(1)} %get-tuple-element.73), channel_id=1, source_target_pairs={{0,1},{1,0},{2,3},{3,2},{4,5},{5,4},{6,7},{7,6},{8,9},{9,8},{10,11... | collective-permute-start | bytes 3145736 | tf_op jit(solution)/shard_map/ppermute | solution.py:97
  61.4 6.4 %copy-start = (bf16[1,256,4096]{2,1,0:T(8,128)(2,1)S(1)}, bf16[1,256,4096]{2,1,0:T(8,128)(2,1)}, u32[]{:S(2)}) copy-start(bf16[1,256,4096]{2,1,0:T(8,128)(2,1)} %param.11) | copy-start | bytes 6291460
  63.9 15.0 %collective-permute-start.12 = (bf16[256,1024]{1,0:T(8,128)(2,1)S(1)}, bf16[256,1024]{1,0:T(8,128)(2,1)S(1)}, u32[]{:S(2)}, u32[]{:S(2)}) collective-permute-start(bf16[256,1024]{1,0:T(8,128)(2,1)S(1)} %add.121.refs_0_.refs_1_), channel_id=1, source_target_pairs={{0,16},{1,17},{2,18},{3,19},{4,20},{5,21},{6,22},{7,23},{8,24},{9,... | collective-permute-start | bytes 1572872 | tf_op jit(solution)/shard_map/ppermute | solution.py:97
  65.2 16.2 %collective-permute-start.11 = (bf16[256,1024]{1,0:T(8,128)(2,1)S(1)}, bf16[256,1024]{1,0:T(8,128)(2,1)S(1)}, u32[]{:S(2)}, u32[]{:S(2)}) collective-permute-start(bf16[256,1024]{1,0:T(8,128)(2,1)S(1)} %add.121.refs_0_.refs_1_), channel_id=1, source_target_pairs={{0,96},{1,97},{2,98},{3,99},{4,100},{5,101},{6,102},{7,103},{8,104... | collective-permute-start | bytes 1572872 | tf_op jit(solution)/shard_map/ppermute | solution.py:97
  66.5 22.0 %collective-permute-start.15 = (bf16[256,1024]{1,0:T(8,128)(2,1)S(1)}, bf16[256,1024]{1,0:T(8,128)(2,1)S(1)}, u32[]{:S(2)}, u32[]{:S(2)}) collective-permute-start(bf16[256,1024]{1,0:T(8,128)(2,1)S(1)} %add.121.refs_0_.refs_1_), channel_id=1, source_target_pairs={{0,32},{1,33},{2,34},{3,35},{4,36},{5,37},{6,38},{7,39},{8,40},{9,... | collective-permute-start | bytes 1572872 | tf_op jit(solution)/shard_map/ppermute | solution.py:97
  81.4 23.2 %collective-permute-start.13 = (bf16[256,1024]{1,0:T(8,128)(2,1)S(1)}, bf16[256,1024]{1,0:T(8,128)(2,1)S(1)}, u32[]{:S(2)}, u32[]{:S(2)}) collective-permute-start(bf16[256,1024]{1,0:T(8,128)(2,1)S(1)} %collective-permute-done.12.refs_0_.refs_3_), channel_id=1, source_target_pairs={{0,32},{1,33},{2,34},{3,35},{4,36},{5,37},{6,38},{7,39},{8,40},{9,... | collective-permute-start | bytes 1572872 | tf_op jit(solution)/shard_map/ppermute | solution.py:97
  82.7 21.9 %collective-permute-start.14 = (bf16[256,1024]{1,0:T(8,128)(2,1)S(1)}, bf16[256,1024]{1,0:T(8,128)(2,1)S(1)}, u32[]{:S(2)}, u32[]{:S(2)}) collective-permute-start(bf16[256,1024]{1,0:T(8,128)(2,1)S(1)} %collective-permute-done.11.refs_2_.refs_5_), channel_id=1, source_target_pairs={{0,16},{1,17},{2,18},{3,19},{4,20},{5,21},{6,22},{7,23},{8,24},{9,... | collective-permute-start | bytes 1572872 | tf_op jit(solution)/shard_map/ppermute | solution.py:97
  86.4 23.6 %collective-permute-start.16 = (bf16[256,1024]{1,0:T(8,128)(2,1)S(1)}, bf16[256,1024]{1,0:T(8,128)(2,1)S(1)}, u32[]{:S(2)}, u32[]{:S(2)}) collective-permute-start(bf16[256,1024]{1,0:T(8,128)(2,1)S(1)} %collective-permute-done.11.refs_2_.refs_5_), channel_id=1, source_target_pairs={{0,96},{1,97},{2,98},{3,99},{4,100},{5,101},{6,102},{7,103},{8,104... | collective-permute-start | bytes 1572872 | tf_op jit(solution)/shard_map/ppermute | solution.py:97
  104.7 16.7 %collective-permute-start.17 = (bf16[128,1024]{1,0:T(8,128)(2,1)S(1)}, bf16[128,1024]{1,0:T(8,128)(2,1)S(1)}, u32[]{:S(2)}, u32[]{:S(2)}) collective-permute-start(bf16[128,1024]{1,0:T(8,128)(2,1)S(1)} %slice.14), channel_id=1, source_target_pairs={{32,64},{33,65},{34,66},{35,67},{36,68},{37,69},{38,70},{39,71},{4... | collective-permute-start | bytes 786440 | tf_op jit(solution)/shard_map/ppermute | solution.py:97
  106.0 15.4 %collective-permute-start.18 = (bf16[128,1024]{1,0:T(8,128)(2,1)S(1)}, bf16[128,1024]{1,0:T(8,128)(2,1)S(1)}, u32[]{:S(2)}, u32[]{:S(2)}) collective-permute-start(bf16[128,1024]{1,0:T(8,128)(2,1)S(1)} %slice.15), channel_id=1, source_target_pairs={{0,96},{1,97},{2,98},{3,99},{4,100},{5,101},{6,102},{7,103},{8,104... | collective-permute-start | bytes 786440 | tf_op jit(solution)/shard_map/ppermute | solution.py:97

commit v3 on v2

v3 whole, which is shorter than its diff:
```python
import functools
import math

import jax
import jax.numpy as jnp
import numpy as np
from jax import lax
from jax.experimental import pallas as pl
from jax.experimental.pallas import tpu as pltpu
from jax.sharding import PartitionSpec as P

HEAD = 128
TAPS = 4
EPISODES = 8
AXES = ("ctx", "fsdp")
CTX, FSDP = 8, 16
DEVICES = CTX * FSDP
MIB = 1 << 20


def place(i):
    c, f = divmod(i, FSDP)
    x, zl = divmod(c, 2)
    y, r = divmod(f, 4)
    zh, k = divmod(r, 2)
    return x, y, zh, zl, k


def device(x, y, zh, zl, k):
    return ((x % 4) * 2 + zl) * FSDP + ((y % 4) * 2 + zh) * 2 + k


def lead_core(x, zl):
    return (x + zl) % 2


def neighbour(x, y, zh, zl, way):
    return {
        "x+": (x + 1, y, zh, zl),
        "x-": (x - 1, y, zh, zl),
        "y+": (x, y + 1, zh, zl),
        "y-": (x, y - 1, zh, zl),
        "zlo": (x, y, zh, 1 - zl),
        "zhi": (x, y, 1 - zh, 1 - zl),
    }[way]


STEPS = (
    ((0, "y-", 0), (1, "zhi", 1)),
    ((0, "y+", 1),),
    ((0, "x-", 1), (1, "zlo", 0)),
    ((0, "y-", 0), (1, "y+", 1)),
    ((0, "zhi", 0), (1, "x+", 1)),
    ((0, "x-", 0), (1, "x+", 1)),
    ((0, "y-", 1), (1, "y+", 0)),
    ((0, "zlo", 0),),
)
SENT = ((0, 0), (0, 0), (1, 1), (1, 1), (1, 2), (4, 4), (5, 4), (5, 5))
SLOT_STEPS = ((0, 0), (1, 1), (3, 3), (4, 4), (5, 5), (6, 6), (7, 7), (8, 2))


def role_of(i):
    x, _, _, zl, k = place(i)
    return 0 if k == lead_core(x, zl) else 1


def weight_plan():
    pairs, held = [], [[i % FSDP for i in range(DEVICES)]]
    for step, sent in zip(STEPS, SENT):
        now, got = [], [-1] * DEVICES
        for i in range(DEVICES):
            for sender, way, receiver in step:
                if sender == role_of(i):
                    nx, ny, nzh, nzl = neighbour(*place(i)[:4], way)
                    lead = lead_core(nx, nzl)
                    to = device(nx, ny, nzh, nzl, lead if receiver == 0 else 1 - lead)
                    now.append((i, to))
                    got[to] = held[sent[role_of(i)]][i]
        pairs.append(now)
        held.append(got)
    slots = [[held[step[role_of(i)]][i] for step in SLOT_STEPS] for i in range(DEVICES)]
    return pairs, np.asarray(slots, np.int32)


WEIGHT_PAIRS, SLOTS = weight_plan()


def moved(way, wanted):
    pairs = [(i, device(*neighbour(*place(i)[:4], way), place(i)[4])) for i in range(DEVICES)]
    return [(i, to) for i, to in pairs if wanted(place(to)[0], place(to)[3])]


SWAP = [(i, i ^ 1) for i in range(DEVICES)]


def send(x, pairs):
    return lax.ppermute(x, AXES, pairs)


def together(*values):
    return lax.optimization_barrier(values)


def params(mib, **kw):
    return pltpu.CompilerParams(vmem_limit_bytes=mib * MIB, **kw)


WHOLE = pl.BlockSpec(memory_space=pltpu.VMEM)
SCALARS = pl.BlockSpec(memory_space=pltpu.SMEM)
ANYWHERE = pl.BlockSpec(memory_space=pl.ANY)
ROWS_HERE = 2
BLOCKS = 8
BASES = 1 + ROWS_HERE * EPISODES
LEAD = BASES + BLOCKS
CORE = LEAD + 1


def in_smem(scalars):
    return pltpu.with_memory_space_constraint(scalars, pltpu.SMEM)


SHORT = pl.CostEstimate(flops=1024, bytes_accessed=1024, transcendentals=0)


def norm_kernel(slots, h_ref, g_ref, mine_ref, other_ref, *, width, chunk, count):
    rows = h_ref.shape[0]
    here = pl.ds(pl.multiple_of(pl.program_id(0) * rows, rows), rows)
    total = jnp.zeros((rows, chunk), jnp.float32)
    for c in range(width // chunk):
        f = h_ref[:, c * chunk : (c + 1) * chunk].astype(jnp.float32)
        total = total + f * f
    mean = jnp.sum(total, axis=-1, keepdims=True) * (1.0 / width)
    factor = lax.rsqrt(mean + 1e-06)
    for which, out in ((1, other_ref), (0, mine_ref)):
        for s in range(count):
            at = pl.multiple_of(slots[which, s] * chunk, chunk)
            f = h_ref[:, pl.ds(at, chunk)].astype(jnp.float32)
            out[s, here, :] = (f * factor * g_ref[:, pl.ds(at, chunk)]).astype(jnp.bfloat16)


def norm(slots, hidden, gain, chunk):
    rows, width = hidden.shape
    count = slots.shape[1]
    tile = 64
    shape = pltpu.VMEM((count, rows, chunk), jnp.bfloat16)
    return pl.pallas_call(
        functools.partial(norm_kernel, width=width, chunk=chunk, count=count),
        grid=(rows // tile,),
        in_specs=[
            pl.BlockSpec(memory_space=pltpu.SMEM),
            pl.BlockSpec((tile, width), lambda i: (i, 0)),
            pl.BlockSpec((1, width), lambda i: (0, 0)),
        ],
        out_specs=[WHOLE, WHOLE],
        out_shape=[shape, shape],
        compiler_params=params(16),
        cost_estimate=SHORT,
        name="norm",
    )(slots, pltpu.with_memory_space_constraint(hidden, pltpu.HBM), gain)


def project_kernel(*refs, sides, slots, carried, after):
    del after
    count = len(slots)
    xs, ws = refs[:sides], refs[sides : sides + count]
    olds, outs = refs[sides + count :][:carried], refs[-sides:]
    tile = 256
    for s in range(count):
        for c in range(0, ws[s].shape[1], tile):
            cols = slice(c, c + tile)
            w = ws[s][:, cols]
            for side in range(sides):
                part = jnp.dot(xs[side][slots[s]], w, preferred_element_type=jnp.float32)
                if s:
                    part = outs[side][:, cols] + part
                elif carried:
                    part = olds[side][:, cols] + part
                outs[side][:, cols] = part


def project(xs, slots, weights, carried=(), after=()):
    _, rows, depth = xs[0].shape
    columns = weights[0].shape[1]
    sides = len(xs)
    inside = [
        pltpu.with_memory_space_constraint(v, pltpu.VMEM) for v in (*xs, *weights, *carried, *after)
    ]
    return pl.pallas_call(
        functools.partial(
            project_kernel, sides=sides, slots=slots, carried=len(carried), after=len(after)
        ),
        in_specs=[WHOLE] * len(inside),
        out_specs=[WHOLE] * sides,
        out_shape=[pltpu.VMEM((rows, columns), jnp.float32)] * sides,
        compiler_params=params(8),
        cost_estimate=SHORT,
        name="project",
    )(*inside)


def pick_kernel(flag_ref, a_ref, b_ref, o_ref):
    o_ref[...] = jnp.where(flag_ref[0:1, :] > 0, a_ref[...], b_ref[...])


def pick(flag, a, b):
    inside = [pltpu.with_memory_space_constraint(v, pltpu.VMEM) for v in (flag, a, b)]
    return pl.pallas_call(
        pick_kernel,
        in_specs=[WHOLE] * 3,
        out_specs=WHOLE,
        out_shape=pltpu.VMEM(a.shape, a.dtype),
        compiler_params=params(8),
        cost_estimate=SHORT,
        name="pick",
    )(*inside)


def finish_kernel(scalars, x0, x1, old0, old1, *refs, slots, counts, own):
    ws, out = refs[:-1], refs[-1]
    rows, tile = old0.shape[0], out.shape[1] // 2
    core = scalars[CORE] if own else 1 - scalars[CORE]
    for part in range(2):
        cols = pl.ds(pl.multiple_of((2 * part + core) * tile, tile), tile)
        for side, (x, old) in enumerate(((x0, old0), (x1, old1))):
            total = old[:, cols]
            at = 0
            for s, n in enumerate(counts):
                w = ws[at][:, cols]
                if n == 2:
                    w = jnp.where(scalars[LEAD] > 0, w, ws[at + 1][:, cols])
                total = total + jnp.dot(x[slots[s]], w, preferred_element_type=jnp.float32)
                at += n
            out[side * rows : (side + 1) * rows, part * tile : (part + 1) * tile] = total


def finish(scalars, xs, olds, slots, weights, own):
    weights = [w if isinstance(w, tuple) else (w,) for w in weights]
    counts = tuple(len(w) for w in weights)
    flat = [v for w in weights for v in w]
    rows, columns = olds[0].shape
    inside = [pltpu.with_memory_space_constraint(v, pltpu.VMEM) for v in (*xs, *olds, *flat)]
    depth = xs[0].shape[2]
    return pl.pallas_call(
        functools.partial(finish_kernel, slots=slots, counts=counts, own=own),
        in_specs=[SCALARS] + [WHOLE] * len(inside),
        out_specs=WHOLE,
        out_shape=pltpu.VMEM((2 * rows, columns // 2), jnp.float32),
        compiler_params=params(8),
        cost_estimate=SHORT,
        name="finish",
    )(in_smem(scalars), *inside)


def add_kernel(a_ref, b_ref, o_ref):
    o_ref[...] = (a_ref[...] + b_ref[...]).astype(o_ref.dtype)


def add(a, b):
    inside = [pltpu.with_memory_space_constraint(v, pltpu.VMEM) for v in (a, b)]
    return pl.pallas_call(
        add_kernel,
        in_specs=[WHOLE, WHOLE],
        out_specs=WHOLE,
        out_shape=pltpu.VMEM(a.shape, jnp.bfloat16),
        compiler_params=params(8),
        cost_estimate=SHORT,
        name="add",
    )(*inside)


PIECES = 8


def copies_of(pairs, sems):
    copies = []
    for i, (source, target, rows) in enumerate(pairs):
        step = rows // PIECES
        for p in range(PIECES):
            here = pl.ds(p * step, step)
            copies.append(pltpu.make_async_copy(source(here), target(here), sems.at[i, p]))
    return copies


def split_kernel(scalars, q_ref, out_ref, sems):
    rows, width = out_ref.shape
    cols = pl.ds(pl.multiple_of((1 - scalars[CORE]) * width, width), width)
    copies = copies_of([(lambda r: q_ref.at[r, cols], lambda r: out_ref.at[r, :], rows)], sems)
    for c in copies:
        c.start()
    for c in copies:
        c.wait()


def split(scalars, queries):
    rows, width = queries.shape
    return pl.pallas_call(
        split_kernel,
        in_specs=[SCALARS, ANYWHERE],
        out_specs=WHOLE,
        out_shape=pltpu.VMEM((rows, width // 2), queries.dtype),
        scratch_shapes=[pltpu.SemaphoreType.DMA((1, PIECES))],
        compiler_params=params(8),
        cost_estimate=SHORT,
        name="split",
    )(in_smem(scalars), pltpu.with_memory_space_constraint(queries, pltpu.HBM))


def merge_kernel(scalars, part_ref, all_in, all_ref, sems):
    del all_in
    rows, width = part_ref.shape
    cols = pl.ds(pl.multiple_of((1 - scalars[CORE]) * width, width), width)
    copies = copies_of(
        [(lambda r: part_ref.at[r, :], lambda r: all_ref.at[r, cols], rows)], sems
    )
    for c in copies:
        c.start()
    for c in copies:
        c.wait()


def merge(scalars, part, whole):
    return pl.pallas_call(
        merge_kernel,
        in_specs=[SCALARS, WHOLE, ANYWHERE],
        out_specs=ANYWHERE,
        out_shape=jax.ShapeDtypeStruct(whole.shape, whole.dtype),
        input_output_aliases={2: 0},
        scratch_shapes=[pltpu.SemaphoreType.DMA((1, PIECES))],
        compiler_params=params(8),
        cost_estimate=SHORT,
        name="merge",
    )(in_smem(scalars), pltpu.with_memory_space_constraint(part, pltpu.VMEM), whole)


def conv_kernel(info, x_ref, halo_ref, w_ref, b_ref, o_ref, token, pick, before):
    rows, width = x_ref.shape
    ahead = halo_ref.shape[0]
    token[...] = jnp.zeros_like(token)

    @pl.when(pl.program_id(0) == 0)
    def _():
        before[...] = halo_ref[...]

    shape = (rows, ahead + rows)
    pos = info[0] + pl.program_id(0) * rows + lax.broadcasted_iota(jnp.int32, shape, 0)
    begin = jnp.zeros(shape, jnp.int32)
    for e in range(EPISODES):
        begin = jnp.where(info[1 + e] <= pos, jnp.maximum(begin, info[1 + e]), begin)
    apart = lax.broadcasted_iota(jnp.int32, shape, 0) + ahead - lax.broadcasted_iota(jnp.int32, shape, 1)
    for tap in range(TAPS):
        behind = TAPS - 1 - tap
        taken = (apart == behind) & (pos - behind >= begin)
        pick[tap * rows : (tap + 1) * rows, :] = jnp.where(taken, 1.0, 0.0).astype(pick.dtype)

    lanes = 256
    for c in range(0, width, lanes):
        cols = slice(c, c + lanes)
        source = jnp.concatenate([before[:, cols], x_ref[:, cols]], axis=0)
        taps = jnp.dot(pick[...], source, preferred_element_type=jnp.float32)
        mixing = b_ref[:, cols] + taps[:rows] * w_ref[0:1, cols]
        for tap in range(1, TAPS):
            mixing = mixing + taps[tap * rows : (tap + 1) * rows] * w_ref[tap : tap + 1, cols]
        by_half = 0.5 * mixing
        o_ref[:, cols] = (by_half + by_half * jnp.tanh(by_half)).astype(o_ref.dtype)
    before[...] = x_ref[rows - ahead :, :]


def conv(info, x, halo, weight, bias):
    rows, width = x.shape
    tile = 64
    ahead = halo.shape[0]
    full = lambda n: pl.BlockSpec((n, width), lambda i: (0, 0))
    return pl.pallas_call(
        conv_kernel,
        grid=(rows // tile,),
        in_specs=[
            SCALARS,
            pl.BlockSpec((tile, width), lambda i: (i, 0)),
            full(ahead),
            full(TAPS),
            full(1),
        ],
        out_specs=[pl.BlockSpec((tile, width), lambda i: (i, 0)), WHOLE],
        out_shape=[
            jax.ShapeDtypeStruct((rows, width), x.dtype),
            pltpu.VMEM((8, 128), jnp.float32),
        ],
        scratch_shapes=[
            pltpu.VMEM((TAPS * tile, ahead + tile), jnp.bfloat16),
            pltpu.VMEM((ahead, width), x.dtype),
        ],
        compiler_params=params(16),
        cost_estimate=SHORT,
        name="conv",
    )(in_smem(info), x, halo, weight, bias)


def attend_kernel(info, *refs, count, per_group, stage, at, row):
    if stage == "first":
        q1_ref, *refs = refs
    else:
        q0_ref, q1_ref, *refs = refs
    ks, vs = refs[:count], refs[count : 2 * count]
    rest = refs[2 * count :]
    if stage == "first":
        q_hbm, m_ref, a_ref, own_ref, q_ref, mask_ref, q_sems = rest
        m_in, a_in = m_ref, a_ref
    elif stage == "middle":
        m_in, a_in, m_ref, a_ref, q_ref, mask_ref = rest
    elif row:
        m_in, a_in, o_ref, q_ref, mask_ref = rest
    else:
        m_in, a_in, o_hbm, q_ref, mask_ref, o_buf, sems = rest
    rows, keys = mask_ref.shape[1:]
    factor = math.log2(math.e) / math.sqrt(HEAD)
    first = info[0]
    if stage == "last":
        here, group = row, pl.program_id(0)
        q_ref = q1_ref if row else q0_ref
    else:
        here, group = 1 - pl.program_id(0) // 2, pl.program_id(0) % 2
    if stage == "middle":
        q_ref[...] = jnp.where(here == 0, q0_ref[...], q1_ref[...])
    if stage == "first":
        width = own_ref.shape[1]
        cols = pl.ds(pl.multiple_of(info[CORE] * width, width), width)
        copies = copies_of(
            [(lambda r: q_hbm.at[r, cols], lambda r: own_ref.at[r, :], own_ref.shape[0])], q_sems
        )

        @pl.when(pl.program_id(0) == 0)
        def _():
            for c in copies:
                c.start()

        @pl.when(pl.program_id(0) == 2)
        def _():
            for c in copies:
                c.wait()

        @pl.when(here == 0)
        def _():
            part = q_ref.shape[1]
            q_ref[...] = own_ref[:, pl.ds(pl.multiple_of(group * part, part), part)]

        @pl.when(here == 1)
        def _():
            q_ref[...] = q1_ref[...]

    if stage == "last" and not row:
        o_ref = o_buf.at[group]

    def start(e):
        return info[1 + here * EPISODES + e]

    lowest = jnp.int32(0)
    for e in range(EPISODES):
        lowest = jnp.where(start(e) <= first, jnp.maximum(lowest, start(e)), lowest)
    head = (here * 2 + group) * per_group

    def divided(h, a):
        value = (a[:, :HEAD] / a[:, HEAD:]).astype(jnp.bfloat16)
        if row:
            part = per_group * HEAD
            at_column = pl.multiple_of(group * part, part) + h * HEAD
            o_ref[:, pl.ds(pl.multiple_of(at_column, HEAD), HEAD)] = value
        else:
            o_ref[:, h * HEAD : (h + 1) * HEAD] = value

    def work(some):
        pos = first + lax.broadcasted_iota(jnp.int32, (rows, keys), 0)
        begin = jnp.zeros((rows, keys), jnp.int32)
        for e in range(EPISODES):
            begin = jnp.where(start(e) <= pos, jnp.maximum(begin, start(e)), begin)
        for b in some:
            key_pos = info[BASES + at + b] + lax.broadcasted_iota(jnp.int32, (rows, keys), 1)
            allowed = (key_pos >= begin) & (key_pos <= pos)
            mask_ref[b] = jnp.where(allowed, 0.0, -1e30)
        k = [ks[b][...] for b in some]
        v = [jnp.concatenate([vs[b][...], jnp.ones((keys, HEAD), jnp.bfloat16)], axis=1) for b in some]
        for h in range(per_group):
            q = q_ref[:, h * HEAD : (h + 1) * HEAD]
            scores = [
                lax.dot_general(q, k_b, (((1,), (1,)), ((), ())), preferred_element_type=jnp.float32)
                + mask_ref[b]
                for b, k_b in zip(some, k)
            ]
            top = scores[0]
            for s in scores[1:]:
                top = jnp.maximum(top, s)
            top = jnp.max(top, axis=1, keepdims=True)
            if stage == "first":
                new = jnp.broadcast_to(top, (rows, HEAD))
                a = None
            else:
                old = m_in[head + h]
                new = jnp.maximum(old, top)
                shrink = jnp.exp2((old - new) * factor)
                a = a_in[head + h] * jnp.concatenate([shrink, shrink], axis=1)
            wide = jnp.concatenate([new] * (keys // HEAD), axis=1)
            for s, v_b in zip(scores, v):
                w = jnp.exp2((s - wide) * factor).astype(jnp.bfloat16)
                part = jnp.dot(w, v_b, preferred_element_type=jnp.float32)
                a = part if a is None else a + part
            if stage == "last":
                divided(h, a)
            else:
                a_ref[head + h] = a
                m_ref[head + h] = new

    if stage == "first":
        work([0])
    else:
        lives = []
        for b in range(count):
            base = info[BASES + at + b]
            lives.append((base < first) & (base + keys > lowest))
        done = functools.reduce(jnp.logical_and, lives)
        pl.when(done)(functools.partial(work, list(range(count))))
        if count > 2:
            pair = lives[0] & lives[1] & jnp.logical_not(done)
            pl.when(pair)(functools.partial(work, [0, 1]))
            done = done | pair
        if count > 1:
            for b in range(count):
                pl.when(lives[b] & jnp.logical_not(done))(functools.partial(work, [b]))
        if stage == "last":

            @pl.when(jnp.logical_not(done))
            def _():
                for h in range(per_group):
                    divided(h, a_in[head + h])

    if stage == "last" and not row:
        width = o_buf.shape[2]

        def out_copy(j):
            cols = pl.ds(pl.multiple_of((info[CORE] * 2 + j) * width, width), width)
            return pltpu.make_async_copy(o_buf.at[j], o_hbm.at[:, cols], sems.at[j])

        out_copy(group).start()

        @pl.when(group == 1)
        def _():
            out_copy(0).wait()
            out_copy(1).wait()


def attend(stage, scalars, at, queries, blocks, state=(), row=None, whole=None):
    rows, width = queries[0].shape
    columns = blocks[0].shape[1]
    keys = blocks[0].shape[0] // (1 if stage == "last" else ROWS_HERE)
    count = len(blocks)
    group = width // 2
    heads = ROWS_HERE * width // HEAD
    scratch = [pltpu.VMEM((rows, group), jnp.bfloat16), pltpu.VMEM((count, rows, keys), jnp.float32)]
    half_columns = columns // (2 * HEAD)
    if stage == "last":
        grid = (2,)
        q_specs = [pl.BlockSpec((rows, group), lambda g: (0, g))] * 2
        k_spec = pl.BlockSpec((keys, HEAD), lambda g: (0, g))
        v_spec = pl.BlockSpec((keys, HEAD), lambda g: (0, half_columns + g))
        if row:
            out_shape = pltpu.VMEM((rows, width), jnp.bfloat16)
            out_specs = WHOLE
        else:
            out_shape = jax.ShapeDtypeStruct((rows, 2 * width), jnp.bfloat16)
            out_specs = ANYWHERE
            scratch += [pltpu.VMEM((2, rows, group), jnp.bfloat16), pltpu.SemaphoreType.DMA((2,))]
    else:
        grid = (4,)
        q_specs = [pl.BlockSpec((rows, group), lambda g: (0, g % 2))] * 2
        k_spec = pl.BlockSpec((keys, HEAD), lambda g: (1 - g // 2, g % 2))
        v_spec = pl.BlockSpec((keys, HEAD), lambda g: (1 - g // 2, half_columns + g % 2))
        out_shape = [
            pltpu.VMEM((heads, rows, HEAD), jnp.float32),
            pltpu.VMEM((heads, rows, 2 * HEAD), jnp.float32),
        ]
        out_specs = [WHOLE, WHOLE]
        if stage == "first":
            out_shape.append(pltpu.VMEM((rows, width), jnp.bfloat16))
            out_specs.append(WHOLE)
            scratch.append(pltpu.SemaphoreType.DMA((1, PIECES)))
            q_specs = q_specs[1:]
    in_specs = [SCALARS] + q_specs + [k_spec] * count + [v_spec] * count + [WHOLE] * len(state)
    extra = []
    if stage == "first":
        in_specs.append(ANYWHERE)
        extra = [pltpu.with_memory_space_constraint(whole, pltpu.HBM)]
    aliases = {} if stage != "middle" else {len(in_specs) - 2: 0, len(in_specs) - 1: 1}
    state = [pltpu.with_memory_space_constraint(v, pltpu.VMEM) for v in state]
    return pl.pallas_call(
        functools.partial(
            attend_kernel, count=count, per_group=group // HEAD, stage=stage, at=at, row=row
        ),
        grid=grid,
        in_specs=in_specs,
        out_specs=out_specs,
        out_shape=out_shape,
        input_output_aliases=aliases,
        scratch_shapes=scratch,
        compiler_params=params(14),
        cost_estimate=SHORT,
        name="attend_" + stage,
    )(in_smem(scalars), *queries, *blocks, *blocks, *state, *extra)


def body(
    hidden, queries, conv_input, norm_gain, kv_weight, conv_weight, conv_bias, starts, segment_ids
):
    del segment_ids
    rows = hidden.shape[1]
    ctx = lax.axis_index("ctx")
    me = ctx * FSDP + lax.axis_index("fsdp")
    x, zl = ctx // 2, ctx % 2
    depth = kv_weight.shape[0]
    leads = lax.axis_index("fsdp") % 2 == lead_core(x, zl)
    table = jnp.asarray(SLOTS)
    slots = jnp.stack([table[me], table[me ^ 1]])

    def base(dx, dz):
        return (((x + dx) % 4) * 2 + (zl + dz) % 2) * rows

    bases = [base(0, 0), base(0, 1), base(-1, 0), base(1, 0), base(-1, 1), base(2, 0), base(1, 1), base(2, 1)]
    core = lax.axis_index("fsdp") % 2
    flags = jnp.stack([leads.astype(jnp.int32), core])
    scalars = jnp.concatenate(
        [(ctx * rows)[None], starts[0], send(starts, SWAP)[0], jnp.stack(bases), flags]
    )
    signal = conv_input[0]
    tail = signal[rows - 16 :]
    flag = jnp.full((8, kv_weight.shape[1]), leads.astype(jnp.int32))
    slots, tail, scalars, flag = together(slots, tail, scalars, flag)

    w0 = kv_weight
    w1 = send(w0, WEIGHT_PAIRS[0])
    w2 = send(w0, WEIGHT_PAIRS[1])
    halo = lax.ppermute(tail, "ctx", [(i, i + 1) for i in range(CTX - 1)])
    mine, other = norm(slots, hidden[0], norm_gain[None], depth)
    w1, w2, halo, mine, other, scalars, flag = together(w1, w2, halo, mine, other, scalars, flag)

    w4 = send(w1, WEIGHT_PAIRS[3])
    theirs = send(other, SWAP)
    w5 = send(pick(flag, w1, w2), WEIGHT_PAIRS[4])
    theirs, scalars_later, w1_later = together(theirs, scalars, w1)
    w3 = send(w1_later, WEIGHT_PAIRS[2])
    q_theirs = send(split(scalars_later, queries[0]), SWAP)
    sums = project((mine, theirs), (0, 1), (w0, w1))

    w4, w5, q_theirs, *sums = together(w4, w5, q_theirs, *sums)
    w6 = send(w4, WEIGHT_PAIRS[5])
    w7 = send(pick(flag, w5, w4), WEIGHT_PAIRS[6])
    w8 = send(w5, WEIGHT_PAIRS[7])
    conv_out, token = conv(scalars, signal, halo, conv_weight, conv_bias[None])
    sums = project((mine, theirs), (2, 3, 4), (w3, w4, w5), sums, (token,))

    last = ((5, 6, 7), (w6, w7, (w8, w2)))
    their_sum = finish(scalars, (theirs, mine), sums[::-1], *last, False)
    back = send(their_sum, SWAP)
    my_sum = finish(scalars, (mine, theirs), sums, *last, True)
    kv = add(my_sum, back)

    right_end = (0, 3)
    from_right = send(kv, moved("x-", lambda x, z: x in right_end))
    from_pair = send(kv, moved("zlo", lambda x, z: x < 3 or z == 1))
    from_left = send(kv, moved("x+", lambda x, z: x > 0))
    *state, q_mine = attend("first", scalars, 0, (q_theirs,), [kv], whole=queries[0])
    q = (q_mine, q_theirs)
    from_right, from_pair, *state = together(from_right, from_pair, *state)
    left_pair = send(from_pair, moved("x+", lambda x, z: x > 0))
    right_pair = send(from_right, moved("zlo", lambda x, z: x in right_end))
    far = send(from_right, moved("x-", lambda x, z: x > 1))
    state = attend("middle", scalars, 1, q, [from_pair, from_left, from_right], state)
    left_pair, right_pair, *state = together(left_pair, right_pair, *state)
    far_own = send(left_pair[:rows], moved("x+", lambda x, z: x > 1))
    far_other = send(right_pair[rows:], moved("x-", lambda x, z: x > 1))
    state = attend("middle", scalars, 4, q, [left_pair, far, right_pair], state)
    far_own, far_other, *state = together(far_own, far_other, *state)
    for_other = attend("last", scalars, 7, q, [far_other], state, row=1)
    from_other = send(for_other, SWAP)
    attended = attend("last", scalars, 7, q, [far_own], state, row=0)
    attended = merge(scalars, from_other, attended)
    return attended[None], conv_out[None]


def solution(mesh):
    return jax.shard_map(
        body,
        mesh=mesh,
        in_specs=(
            P("fsdp", "ctx", None),
            P("fsdp", "ctx", None),
            P("fsdp", "ctx", None),
            P(),
            P("fsdp", None),
            P(),
            P(),
            P("fsdp", None),
            P("fsdp", "ctx"),
        ),
        out_specs=(P("fsdp", "ctx", None), P("fsdp", "ctx", None)),
        check_vma=False,
    )
```

time: 129 us -> 124 us (0.961)
  the two profiles are of different devices: /device:TPU:47 before, /device:TPU:7 now
where the time goes in v3:
time: 124 us; the launch traced here: 122 us
  Pallas kernels  49.7 us (40%)
  starting transfers between devices  37 us (30%)
  waiting for transfers between devices  31.1 us (25%)
  local copies, waits for them, and re-layouts  3.31 us (3%)
  between operations  1.32 us (1%)
    ppermute x21, starting transfers between devices, send(): return lax.ppermute(x, AXES, pairs)  35 us
    pallas_call x5, Pallas kernels, attend(): pl.pallas_call(functools.partial(attend_kernel, count=count, per_group=gr...  28.8 us
    ppermute x21, waiting for transfers between devices, send(): return lax.ppermute(x, AXES, pairs)  27.8 us
    pallas_call x1, Pallas kernels, conv(): pl.pallas_call(conv_kernel, grid=(rows // tile,), in_specs=[SCALARS, pl.B...  6.99 us
    pallas_call x1, Pallas kernels, norm(): pl.pallas_call(functools.partial(norm_kernel, width=width, chunk=chunk, c...  3.99 us
    ppermute x1, waiting for transfers between devices, body(): halo = lax.ppermute(tail, 'ctx', [(i, i + 1) for i in range(CTX - 1)])  3.31 us
    pallas_call x2, Pallas kernels, finish(): pl.pallas_call(functools.partial(finish_kernel, slots=slots, counts=count...  3.09 us
    pallas_call x2, Pallas kernels, project(): pl.pallas_call(functools.partial(project_kernel, sides=sides, slots=slots...  3.03 us
  transfers between devices with their start and end apart: 22, of which 11 were waited for; matrix products, arithmetic and copies ran while one was open for 2% of the time, Pallas kernels for 35%

profile of v3, /device:TPU:7, one launch (start us, length us, event | category | flops | bytes accessed | tf_op | source)
XLA Modules:
  0.0 122.5 jit_solution(9509472402609536872)
XLA Ops:
  0.6 2.8 %collective-permute-start = (bf16[512,1024]{1,0:T(8,128)(2,1)}, bf16[512,1024]{1,0:T(8,128)(2,1)S(1)}, u32[]{:S(2)}, u32[]{:S(2)}) collective-permute-start(bf16[512,1024]{1,0:T(8,128)(2,1)} %refs_2_.1), channel_id=1, source_target_pairs={{0,12},{1,18},{2,14},{3,16},{4,0},{5,22},{6,2},{7,20},{8,4},{9,26}... | collective-permute-start | bytes 3145736 | tf_op jit(solution)/shard_map/ppermute | solution.py:97
  3.4 4.6 %collective-permute-start.1 = (bf16[512,1024]{1,0:T(8,128)(2,1)}, bf16[512,1024]{1,0:T(8,128)(2,1)S(1)}, u32[]{:S(2)}, u32[]{:S(2)}) collective-permute-start(bf16[512,1024]{1,0:T(8,128)(2,1)} %refs_2_.1), channel_id=1, source_target_pairs={{0,5},{2,7},{4,9},{6,11},{8,13},{10,15},{12,1},{14,3},{17,20},{19,... | collective-permute-start | bytes 3145736 | tf_op jit(solution)/shard_map/ppermute | solution.py:97
  8.0 0.1 collective-permute-start.2
  8.1 1.0 slice_bitcast_fusion
  9.2 0.8 constant_dynamic-slice_fusion.1
  10.0 0.0 collective-permute-done.2
  10.0 0.7 concatenate.3.scalars.info
  10.8 2.1 %collective-permute-start.3 = (bf16[16,8192]{1,0:T(8,128)(2,1)S(1)}, bf16[16,8192]{1,0:T(8,128)(2,1)S(1)}, u32[]{:S(2)}, u32[]{:S(2)}) collective-permute-start(bf16[16,8192]{1,0:T(8,128)(2,1)S(1)} %slice_bitcast_fusion), channel_id=1, source_target_pairs={{0,16},{16,32},{32,48},{48,64},{64,80},{80,96},{96,112},{1,17},{17... | collective-permute-start | bytes 786440 | tf_op jit(solution)/shard_map/ppermute | solution.py:638
  12.9 0.0 copy-start.3
  12.9 0.7 copy-done.3
  13.6 4.0 %norm.1 = (bf16[8,256,512]{2,1,0:T(8,128)(2,1)S(1)}, bf16[8,256,512]{2,1,0:T(8,128)(2,1)S(1)}) custom-call(s32[2,8]{1,0:T(2,128)S(1)} %pad_add_fusion.slots, bf16[256,8192]{1,0:T(8,128)(2,1)} %bitcast.28, f32[1,8192]{1,0:T(1,128)S(1)} %bitcast.23), custom_call_target="tpu_custom_call" | custom-call | flops 1024 | bytes 1024 | tf_op jit(solution)/shard_map/norm/pallas_call | solution.py:146
  17.6 0.0 copy-start.1
  17.6 3.3 %collective-permute-done.3.halo_ref = bf16[16,8192]{1,0:T(8,128)(2,1)S(1)} collective-permute-done((bf16[16,8192]{1,0:T(8,128)(2,1)S(1)}, bf16[16,8192]{1,0:T(8,128)(2,1)S(1)}, u32[]{:S(2)}, u32[]{:S(2)}) %collective-permute-start.3) | collective-permute-done | bytes 262176 | tf_op jit(solution)/shard_map/ppermute | solution.py:638
  21.0 0.0 collective-permute-done.a_ref.refs_3_
  21.0 0.0 collective-permute-done.1.b_ref.refs_3_
  21.0 1.4 %collective-permute-start.6 = (bf16[8,256,512]{2,1,0:T(8,128)(2,1)S(1)}, bf16[8,256,512]{2,1,0:T(8,128)(2,1)S(1)}, u32[]{:S(2)}, u32[]{:S(2)}) collective-permute-start(bf16[8,256,512]{2,1,0:T(8,128)(2,1)S(1)} %get-tuple-element.58), channel_id=1, source_target_pairs={{0,1},{1,0},{2,3},{3,2},{4,5},{5,4},{6,7},{7,6},{8,9},{9,8},{10,11... | collective-permute-start | bytes 6291464 | tf_op jit(solution)/shard_map/ppermute | solution.py:97
  22.4 1.5 %collective-permute-start.4 = (bf16[512,1024]{1,0:T(8,128)(2,1)S(1)}, bf16[512,1024]{1,0:T(8,128)(2,1)S(1)}, u32[]{:S(2)}, u32[]{:S(2)}) collective-permute-start(bf16[512,1024]{1,0:T(8,128)(2,1)S(1)} %collective-permute-done.a_ref.refs_3_), channel_id=1, source_target_pairs={{0,12},{1,5},{2,14},{3,7},{4,0},{5,9},{6,2},{7,11},{8,4},{9,13},{1... | collective-permute-start | bytes 3145736 | tf_op jit(solution)/shard_map/ppermute | solution.py:97
  23.9 0.1 pick.2
  24.0 0.5 collective-permute-start.5
  24.6 1.6 %collective-permute-done.6.refs_1_.x1.x0 = bf16[8,256,512]{2,1,0:T(8,128)(2,1)S(1)} collective-permute-done((bf16[8,256,512]{2,1,0:T(8,128)(2,1)S(1)}, bf16[8,256,512]{2,1,0:T(8,128)(2,1)S(1)}, u32[]{:S(2)}, u32[]{:S(2)}) %collective-permute-start.6) | collective-permute-done | bytes 2097184 | tf_op jit(solution)/shard_map/ppermute | solution.py:97
  26.2 1.9 %split.1 = bf16[256,2048]{1,0:T(8,128)(2,1)S(1)} custom-call(s32[27]{0:T(128)S(1)} %concatenate.3.scalars.info, bf16[256,4096]{1,0:T(8,128)(2,1)} %bitcast.26), custom_call_target="tpu_custom_call" | custom-call | flops 1024 | bytes 1024 | tf_op jit(solution)/shard_map/split/pallas_call | solution.py:296
  28.1 0.0 copy-start
  28.1 0.0 copy-start.2
  28.1 0.0 copy-start.4
  28.1 0.5 collective-permute-start.7
  28.6 1.1 collective-permute-start.8
  29.7 1.2 %project.2 = (f32[256,1024]{1,0:T(8,128)S(1)}, f32[256,1024]{1,0:T(8,128)S(1)}) custom-call(bf16[8,256,512]{2,1,0:T(8,128)(2,1)S(1)} %get-tuple-element.60.refs_0_.x0.x1, bf16[8,256,512]{2,1,0:T(8,128)(2,1)S(1)} %collective-permute-done.6.refs_1_.x1.x0, bf16[512,1024]{1,0:T(8,128)(2,1)S(1)} %copy-done.1, bf16[512,1024]{1,0:T(8,128)(2,1)S(1)} %collective-permute-done.a_ref.refs_3_), custom_call_target="tpu_custom_call" | custom-call | flops 1024 | bytes 1024 | tf_op jit(solution)/shard_map/project/pallas_call | solution.py:188
  30.9 8.9 %collective-permute-done.5.refs_4_.a_ref = bf16[512,1024]{1,0:T(8,128)(2,1)S(1)} collective-permute-done((bf16[512,1024]{1,0:T(8,128)(2,1)S(1)}, bf16[512,1024]{1,0:T(8,128)(2,1)S(1)}, u32[]{:S(2)}, u32[]{:S(2)}) %collective-permute-start.5) | collective-permute-done | bytes 1048608 | tf_op jit(solution)/shard_map/ppermute | solution.py:97
  39.8 0.0 collective-permute-done.4.refs_3_.b_ref
  39.8 0.0 collective-permute-done.7.refs_0_.refs_1_
  39.8 0.1 pick.3
  39.9 0.1 collective-permute-start.10
  40.0 1.3 %collective-permute-start.9 = (bf16[512,1024]{1,0:T(8,128)(2,1)S(1)}, bf16[512,1024]{1,0:T(8,128)(2,1)S(1)}, u32[]{:S(2)}, u32[]{:S(2)}) collective-permute-start(bf16[512,1024]{1,0:T(8,128)(2,1)S(1)} %collective-permute-done.4.refs_3_.b_ref), channel_id=1, source_target_pairs={{0,97},{1,32},{2,99},{3,34},{4,101},{5,36},{6,103},{7,38},{8,105},... | collective-permute-start | bytes 3145736 | tf_op jit(solution)/shard_map/ppermute | solution.py:97
  41.4 1.9 %collective-permute-start.11 = (bf16[512,1024]{1,0:T(8,128)(2,1)S(1)}, bf16[512,1024]{1,0:T(8,128)(2,1)S(1)}, u32[]{:S(2)}, u32[]{:S(2)}) collective-permute-start(bf16[512,1024]{1,0:T(8,128)(2,1)S(1)} %collective-permute-done.5.refs_4_.a_ref), channel_id=1, source_target_pairs={{0,17},{2,19},{4,21},{6,23},{8,25},{10,27},{12,29},{14,31},{17,0},... | collective-permute-start | bytes 3145736 | tf_op jit(solution)/shard_map/ppermute | solution.py:97
  43.3 7.0 %conv.1 = (bf16[256,8192]{1,0:T(8,128)(2,1)}, f32[8,128]{1,0:T(8,128)S(1)}) custom-call(s32[27]{0:T(128)S(1)} %concatenate.3.scalars.info, bf16[256,8192]{1,0:T(8,128)(2,1)S(1)} %bitcast.22, bf16[16,8192]{1,0:T(8,128)(2,1)S(1)} %collective-permute-done.3.halo_ref, f32[4,8192]{1,0:T(4,128)S(1)} %copy-done.2, f32[1,8192]{1,0:T(1,128)S(1)} %bitcast.24), custom_call_target="tpu_custom_call" | custom-call | flops 1024 | bytes 1024 | tf_op jit(solution)/shard_map/conv/pallas_call | solution.py:373
  50.3 1.8 %project.3 = (f32[256,1024]{1,0:T(8,128)S(1)}, f32[256,1024]{1,0:T(8,128)S(1)}) custom-call(bf16[8,256,512]{2,1,0:T(8,128)(2,1)S(1)} %get-tuple-element.60.refs_0_.x0.x1, bf16[8,256,512]{2,1,0:T(8,128)(2,1)S(1)} %collective-permute-done.6.refs_1_.x1.x0, bf16[512,1024]{1,0:T(8,128)(2,1)S(1)} %collective-permute-done.8.refs_2_, ...), custom_call_target="tpu_custom_call" | custom-call | flops 1024 | bytes 1024 | tf_op jit(solution)/shard_map/project/pallas_call | solution.py:188
  52.1 3.4 %collective-permute-done.10.refs_1_ = bf16[512,1024]{1,0:T(8,128)(2,1)S(1)} collective-permute-done((bf16[512,1024]{1,0:T(8,128)(2,1)S(1)}, bf16[512,1024]{1,0:T(8,128)(2,1)S(1)}, u32[]{:S(2)}, u32[]{:S(2)}) %collective-permute-start.10) | collective-permute-done | bytes 1048608 | tf_op jit(solution)/shard_map/ppermute | solution.py:97
  55.5 0.1 collective-permute-done.9.refs_0_
  55.5 1.9 %collective-permute-done.11.refs_2_ = bf16[512,1024]{1,0:T(8,128)(2,1)S(1)} collective-permute-done((bf16[512,1024]{1,0:T(8,128)(2,1)S(1)}, bf16[512,1024]{1,0:T(8,128)(2,1)S(1)}, u32[]{:S(2)}, u32[]{:S(2)}) %collective-permute-start.11) | collective-permute-done | bytes 1048608 | tf_op jit(solution)/shard_map/ppermute | solution.py:97
  57.5 1.5 %finish.3 = f32[512,512]{1,0:T(8,128)S(1)} custom-call(s32[27]{0:T(128)S(1)} %concatenate.3.scalars.info, bf16[8,256,512]{2,1,0:T(8,128)(2,1)S(1)} %collective-permute-done.6.refs_1_.x1.x0, bf16[8,256,512]{2,1,0:T(8,128)(2,1)S(1)} %get-tuple-element.60.refs_0_.x0.x1, f32[256,1024]{1,0:T(8,128)S(1)} %get-tuple-element.73.old1.old0, ...), custom_call_target="tpu_custom_call" | custom-call | flops 1024 | bytes 1024 | tf_op jit(solution)/shard_map/finish/pallas_call | solution.py:243
  59.0 0.1 collective-permute-start.12
  59.1 1.6 %finish.2.a_ref = f32[512,512]{1,0:T(8,128)S(1)} custom-call(s32[27]{0:T(128)S(1)} %concatenate.3.scalars.info, bf16[8,256,512]{2,1,0:T(8,128)(2,1)S(1)} %get-tuple-element.60.refs_0_.x0.x1, bf16[8,256,512]{2,1,0:T(8,128)(2,1)S(1)} %collective-permute-done.6.refs_1_.x1.x0, f32[256,1024]{1,0:T(8,128)S(1)} %get-tuple-element.72.old0.old1, ...), custom_call_target="tpu_custom_call" | custom-call | flops 1024 | bytes 1024 | tf_op jit(solution)/shard_map/finish/pallas_call | solution.py:243
  60.7 1.1 collective-permute-done.12.b_ref
  61.8 0.1 add.122.refs_1_.refs_2_
  61.9 1.7 %collective-permute-start.14 = (bf16[512,512]{1,0:T(8,128)(2,1)S(1)}, bf16[512,512]{1,0:T(8,128)(2,1)S(1)}, u32[]{:S(2)}, u32[]{:S(2)}) collective-permute-start(bf16[512,512]{1,0:T(8,128)(2,1)S(1)} %add.122.refs_1_.refs_2_), channel_id=1, source_target_pairs={{0,16},{1,17},{2,18},{3,19},{4,20},{5,21},{6,22},{7,23},{8,24},{9,... | collective-permute-start | bytes 1572872 | tf_op jit(solution)/shard_map/ppermute | solution.py:97
  63.6 1.3 %collective-permute-start.13 = (bf16[512,512]{1,0:T(8,128)(2,1)S(1)}, bf16[512,512]{1,0:T(8,128)(2,1)S(1)}, u32[]{:S(2)}, u32[]{:S(2)}) collective-permute-start(bf16[512,512]{1,0:T(8,128)(2,1)S(1)} %add.122.refs_1_.refs_2_), channel_id=1, source_target_pairs={{0,96},{1,97},{2,98},{3,99},{4,100},{5,101},{6,102},{7,103},{8,104... | collective-permute-start | bytes 1572872 | tf_op jit(solution)/shard_map/ppermute | solution.py:97
  64.9 1.3 %collective-permute-start.17 = (bf16[512,512]{1,0:T(8,128)(2,1)S(1)}, bf16[512,512]{1,0:T(8,128)(2,1)S(1)}, u32[]{:S(2)}, u32[]{:S(2)}) collective-permute-start(bf16[512,512]{1,0:T(8,128)(2,1)S(1)} %add.122.refs_1_.refs_2_), channel_id=1, source_target_pairs={{0,32},{1,33},{2,34},{3,35},{4,36},{5,37},{6,38},{7,39},{8,40},{9,... | collective-permute-start | bytes 1572872 | tf_op jit(solution)/shard_map/ppermute | solution.py:97
  66.2 5.1 %attend_first.1 = (f32[32,256,128]{2,1,0:T(8,128)S(1)}, f32[32,256,256]{2,1,0:T(8,128)S(1)}, bf16[256,2048]{1,0:T(8,128)(2,1)S(1)}) custom-call(s32[27]{0:T(128)S(1)} %concatenate.3.scalars.info, bf16[256,2048]{1,0:T(8,128)(2,1)S(1)} %collective-permute-done.7.refs_0_.refs_1_, bf16[512,512]{1,0:T(8,128)(2,1)S(1)} %add.122.refs_1_.refs_2_, ...), custom_call_target="tpu_custom_call" | custom-call | flops 1024 | bytes 1024 | tf_op jit(solution)/shard_map/attend_first/pallas_call | solution.py:592
  71.3 3.2 %collective-permute-done.14.refs_2_.refs_5_ = bf16[512,512]{1,0:T(8,128)(2,1)S(1)} collective-permute-done((bf16[512,512]{1,0:T(8,128)(2,1)S(1)}, bf16[512,512]{1,0:T(8,128)(2,1)S(1)}, u32[]{:S(2)}, u32[]{:S(2)}) %collective-permute-start.14) | collective-permute-done | bytes 524320 | tf_op jit(solution)/shard_map/ppermute | solution.py:97
  74.5 5.0 %collective-permute-done.13.refs_4_.refs_7_ = bf16[512,512]{1,0:T(8,128)(2,1)S(1)} collective-permute-done((bf16[512,512]{1,0:T(8,128)(2,1)S(1)}, bf16[512,512]{1,0:T(8,128)(2,1)S(1)}, u32[]{:S(2)}, u32[]{:S(2)}) %collective-permute-start.13) | collective-permute-done | bytes 524320 | tf_op jit(solution)/shard_map/ppermute | solution.py:97
  79.5 1.3 %collective-permute-start.15 = (bf16[512,512]{1,0:T(8,128)(2,1)S(1)}, bf16[512,512]{1,0:T(8,128)(2,1)S(1)}, u32[]{:S(2)}, u32[]{:S(2)}) collective-permute-start(bf16[512,512]{1,0:T(8,128)(2,1)S(1)} %collective-permute-done.14.refs_2_.refs_5_), channel_id=1, source_target_pairs={{0,32},{1,33},{2,34},{3,35},{4,36},{5,37},{6,38},{7,39},{8,40},{9,... | collective-permute-start | bytes 1572872 | tf_op jit(solution)/shard_map/ppermute | solution.py:97
  80.8 2.7 %collective-permute-start.16 = (bf16[512,512]{1,0:T(8,128)(2,1)S(1)}, bf16[512,512]{1,0:T(8,128)(2,1)S(1)}, u32[]{:S(2)}, u32[]{:S(2)}) collective-permute-start(bf16[512,512]{1,0:T(8,128)(2,1)S(1)} %collective-permute-done.13.refs_4_.refs_7_), channel_id=1, source_target_pairs={{0,16},{1,17},{2,18},{3,19},{4,20},{5,21},{6,22},{7,23},{8,24},{9,... | collective-permute-start | bytes 1572872 | tf_op jit(solution)/shard_map/ppermute | solution.py:97
  83.5 2.2 %collective-permute-start.20 = (bf16[512,512]{1,0:T(8,128)(2,1)S(1)}, bf16[512,512]{1,0:T(8,128)(2,1)S(1)}, u32[]{:S(2)}, u32[]{:S(2)}) collective-permute-start(bf16[512,512]{1,0:T(8,128)(2,1)S(1)} %collective-permute-done.13.refs_4_.refs_7_), channel_id=1, source_target_pairs={{0,96},{1,97},{2,98},{3,99},{4,100},{5,101},{6,102},{7,103},{8,104... | collective-permute-start | bytes 1572872 | tf_op jit(solution)/shard_map/ppermute | solution.py:97
  85.7 0.0 collective-permute-done.17.refs_3_.refs_6_
  85.7 6.2 %attend_middle.2 = (f32[32,256,128]{2,1,0:T(8,128)S(1)}, f32[32,256,256]{2,1,0:T(8,128)S(1)}) custom-call(s32[27]{0:T(128)S(1)} %concatenate.3.scalars.info, bf16[256,2048]{1,0:T(8,128)(2,1)S(1)} %get-tuple-element.74.refs_0_, bf16[256,2048]{1,0:T(8,128)(2,1)S(1)} %collective-permute-done.7.refs_0_.refs_1_, ...), custom_call_target="tpu_custom_call", output_to_operand_aliasing={{0}: (9, {}), {1}: (10, {})} | custom-call | flops 1024 | bytes 1024 | tf_op jit(solution)/shard_map/attend_middle/pallas_call | solution.py:592
  91.9 1.3 %collective-permute-done.15.refs_2_.refs_5_ = bf16[512,512]{1,0:T(8,128)(2,1)S(1)} collective-permute-done((bf16[512,512]{1,0:T(8,128)(2,1)S(1)}, bf16[512,512]{1,0:T(8,128)(2,1)S(1)}, u32[]{:S(2)}, u32[]{:S(2)}) %collective-permute-start.15) | collective-permute-done | bytes 524320 | tf_op jit(solution)/shard_map/ppermute | solution.py:97
  93.3 1.3 %collective-permute-done.16.refs_4_.refs_7_ = bf16[512,512]{1,0:T(8,128)(2,1)S(1)} collective-permute-done((bf16[512,512]{1,0:T(8,128)(2,1)S(1)}, bf16[512,512]{1,0:T(8,128)(2,1)S(1)}, u32[]{:S(2)}, u32[]{:S(2)}) %collective-permute-start.16) | collective-permute-done | bytes 524320 | tf_op jit(solution)/shard_map/ppermute | solution.py:97
  94.6 1.3 %collective-permute-start.18 = (bf16[256,512]{1,0:T(8,128)(2,1)S(1)}, bf16[256,512]{1,0:T(8,128)(2,1)S(1)}, u32[]{:S(2)}, u32[]{:S(2)}) collective-permute-start(bf16[256,512]{1,0:T(8,128)(2,1)S(1)} %slice.14), channel_id=1, source_target_pairs={{32,64},{33,65},{34,66},{35,67},{36,68},{37,69},{38,70},{39,71},{4... | collective-permute-start | bytes 786440 | tf_op jit(solution)/shard_map/ppermute | solution.py:97
  95.9 4.2 %collective-permute-start.19 = (bf16[256,512]{1,0:T(8,128)(2,1)S(1)}, bf16[256,512]{1,0:T(8,128)(2,1)S(1)}, u32[]{:S(2)}, u32[]{:S(2)}) collective-permute-start(bf16[256,512]{1,0:T(8,128)(2,1)S(1)} %slice.15), channel_id=1, source_target_pairs={{0,96},{1,97},{2,98},{3,99},{4,100},{5,101},{6,102},{7,103},{8,104... | collective-permute-start | bytes 786440 | tf_op jit(solution)/shard_map/ppermute | solution.py:97
  100.1 10.4 %attend_middle.3 = (f32[32,256,128]{2,1,0:T(8,128)S(1)}, f32[32,256,256]{2,1,0:T(8,128)S(1)}) custom-call(s32[27]{0:T(128)S(1)} %concatenate.3.scalars.info, bf16[256,2048]{1,0:T(8,128)(2,1)S(1)} %get-tuple-element.74.refs_0_, bf16[256,2048]{1,0:T(8,128)(2,1)S(1)} %collective-permute-done.7.refs_0_.refs_1_, ...), custom_call_target="tpu_custom_call", output_to_operand_aliasing={{0}: (9, {}), {1}: (10, {})} | custom-call | flops 1024 | bytes 1024 | tf_op jit(solution)/shard_map/attend_middle/pallas_call | solution.py:592
  110.6 3.1 %attend_last.2 = bf16[256,2048]{1,0:T(8,128)(2,1)S(1)} custom-call(s32[27]{0:T(128)S(1)} %concatenate.3.scalars.info, bf16[256,2048]{1,0:T(8,128)(2,1)S(1)} %get-tuple-element.74.refs_0_, bf16[256,2048]{1,0:T(8,128)(2,1)S(1)} %collective-permute-done.7.refs_0_.refs_1_, bf16[256,512]{1,0:T(8,128)(2,1)S(1)} %collective-permute-done.19.refs_2_.refs_3_, ...), custom_call_target="tpu_custom_call" | custom-call | flops 1024 | bytes 1024 | tf_op jit(solution)/shard_map/attend_last/pallas_call | solution.py:592
  113.7 3.1 %collective-permute-start.21 = (bf16[256,2048]{1,0:T(8,128)(2,1)S(1)}, bf16[256,2048]{1,0:T(8,128)(2,1)S(1)}, u32[]{:S(2)}, u32[]{:S(2)}) collective-permute-start(bf16[256,2048]{1,0:T(8,128)(2,1)S(1)} %attend_last.2), channel_id=1, source_target_pairs={{0,1},{1,0},{2,3},{3,2},{4,5},{5,4},{6,7},{7,6},{8,9},{9,8},{10,11... | collective-permute-start | bytes 3145736 | tf_op jit(solution)/shard_map/ppermute | solution.py:97
  116.8 3.9 %attend_last.3.all_in = bf16[256,4096]{1,0:T(8,128)(2,1)} custom-call(s32[27]{0:T(128)S(1)} %concatenate.3.scalars.info, bf16[256,2048]{1,0:T(8,128)(2,1)S(1)} %get-tuple-element.74.refs_0_, bf16[256,2048]{1,0:T(8,128)(2,1)S(1)} %collective-permute-done.7.refs_0_.refs_1_, bf16[256,512]{1,0:T(8,128)(2,1)S(1)} %collective-permute-done.18.refs_2_.refs_3_, ...), custom_call_target="tpu_custom_call" | custom-call | flops 1024 | bytes 1024 | tf_op jit(solution)/shard_map/attend_last/pallas_call | solution.py:592
  120.7 1.6 %merge.1 = bf16[256,4096]{1,0:T(8,128)(2,1)} custom-call(s32[27]{0:T(128)S(1)} %concatenate.3.scalars.info, bf16[256,2048]{1,0:T(8,128)(2,1)S(1)} %collective-permute-done.21.part_ref, bf16[256,4096]{1,0:T(8,128)(2,1)} %attend_last.3.all_in), custom_call_target="tpu_custom_call", output_to_operand_aliasing={{}: (2, {})} | custom-call | flops 1024 | bytes 1024 | tf_op jit(solution)/shard_map/merge/pallas_call | solution.py:322
  (13 shorter events, 0.1 us)
Async XLA Ops:
  0.6 20.3 %collective-permute-start = (bf16[512,1024]{1,0:T(8,128)(2,1)}, bf16[512,1024]{1,0:T(8,128)(2,1)S(1)}, u32[]{:S(2)}, u32[]{:S(2)}) collective-permute-start(bf16[512,1024]{1,0:T(8,128)(2,1)} %refs_2_.1), channel_id=1, source_target_pairs={{0,12},{1,18},{2,14},{3,16},{4,0},{5,22},{6,2},{7,20},{8,4},{9,26}... | collective-permute-start | bytes 3145736 | tf_op jit(solution)/shard_map/ppermute | solution.py:97
  3.4 17.5 %collective-permute-start.1 = (bf16[512,1024]{1,0:T(8,128)(2,1)}, bf16[512,1024]{1,0:T(8,128)(2,1)S(1)}, u32[]{:S(2)}, u32[]{:S(2)}) collective-permute-start(bf16[512,1024]{1,0:T(8,128)(2,1)} %refs_2_.1), channel_id=1, source_target_pairs={{0,5},{2,7},{4,9},{6,11},{8,13},{10,15},{12,1},{14,3},{17,20},{19,... | collective-permute-start | bytes 3145736 | tf_op jit(solution)/shard_map/ppermute | solution.py:97
  8.0 2.0 %collective-permute-start.2 = (s32[1,8]{1,0:T(1,128)}, s32[1,8]{1,0:T(1,128)S(1)}, u32[]{:S(2)}, u32[]{:S(2)}) collective-permute-start(s32[1,8]{1,0:T(1,128)} %param.17), channel_id=1, source_target_pairs={{0,1},{1,0},{2,3},{3,2},{4,5},{5,4},{6,7},{7,6},{8,9},{9,8},{10,11... | collective-permute-start | bytes 104 | tf_op jit(solution)/shard_map/ppermute | solution.py:97
  10.8 10.2 %collective-permute-start.3 = (bf16[16,8192]{1,0:T(8,128)(2,1)S(1)}, bf16[16,8192]{1,0:T(8,128)(2,1)S(1)}, u32[]{:S(2)}, u32[]{:S(2)}) collective-permute-start(bf16[16,8192]{1,0:T(8,128)(2,1)S(1)} %slice_bitcast_fusion), channel_id=1, source_target_pairs={{0,16},{16,32},{32,48},{48,64},{64,80},{80,96},{96,112},{1,17},{17... | collective-permute-start | bytes 786440 | tf_op jit(solution)/shard_map/ppermute | solution.py:638
  12.9 0.8 copy-start.3
  17.6 12.1 %copy-start.1 = (bf16[512,1024]{1,0:T(8,128)(2,1)S(1)}, bf16[512,1024]{1,0:T(8,128)(2,1)}, u32[]{:S(2)}) copy-start(bf16[512,1024]{1,0:T(8,128)(2,1)} %refs_2_.1) | copy-start | bytes 3145732
  21.0 5.2 %collective-permute-start.6 = (bf16[8,256,512]{2,1,0:T(8,128)(2,1)S(1)}, bf16[8,256,512]{2,1,0:T(8,128)(2,1)S(1)}, u32[]{:S(2)}, u32[]{:S(2)}) collective-permute-start(bf16[8,256,512]{2,1,0:T(8,128)(2,1)S(1)} %get-tuple-element.58), channel_id=1, source_target_pairs={{0,1},{1,0},{2,3},{3,2},{4,5},{5,4},{6,7},{7,6},{8,9},{9,8},{10,11... | collective-permute-start | bytes 6291464 | tf_op jit(solution)/shard_map/ppermute | solution.py:97
  22.4 17.4 %collective-permute-start.4 = (bf16[512,1024]{1,0:T(8,128)(2,1)S(1)}, bf16[512,1024]{1,0:T(8,128)(2,1)S(1)}, u32[]{:S(2)}, u32[]{:S(2)}) collective-permute-start(bf16[512,1024]{1,0:T(8,128)(2,1)S(1)} %collective-permute-done.a_ref.refs_3_), channel_id=1, source_target_pairs={{0,12},{1,5},{2,14},{3,7},{4,0},{5,9},{6,2},{7,11},{8,4},{9,13},{1... | collective-permute-start | bytes 3145736 | tf_op jit(solution)/shard_map/ppermute | solution.py:97
  24.0 15.8 %collective-permute-start.5 = (bf16[512,1024]{1,0:T(8,128)(2,1)S(1)}, bf16[512,1024]{1,0:T(8,128)(2,1)S(1)}, u32[]{:S(2)}, u32[]{:S(2)}) collective-permute-start(bf16[512,1024]{1,0:T(8,128)(2,1)S(1)} %pick.2), channel_id=1, source_target_pairs={{0,19},{1,32},{2,17},{3,34},{4,23},{5,36},{6,21},{7,38},{8,27},{9,... | collective-permute-start | bytes 3145736 | tf_op jit(solution)/shard_map/ppermute | solution.py:97
  28.1 15.2 %copy-start = (bf16[1,256,8192]{2,1,0:T(8,128)(2,1)S(1)}, bf16[1,256,8192]{2,1,0:T(8,128)(2,1)}, u32[]{:S(2)}) copy-start(bf16[1,256,8192]{2,1,0:T(8,128)(2,1)} %param.12) | copy-start | bytes 12582916
  28.1 15.2 %copy-start.2 = (f32[4,8192]{1,0:T(4,128)S(1)}, f32[4,8192]{1,0:T(4,128)}, u32[]{:S(2)}) copy-start(f32[4,8192]{1,0:T(4,128)} %w_ref.1) | copy-start | bytes 393220
  28.1 15.2 %copy-start.4 = (f32[8192]{0:T(1024)S(1)}, f32[8192]{0:T(1024)}, u32[]{:S(2)}) copy-start(f32[8192]{0:T(1024)} %param.16) | copy-start | bytes 98308
  28.1 11.7 %collective-permute-start.7 = (bf16[256,2048]{1,0:T(8,128)(2,1)S(1)}, bf16[256,2048]{1,0:T(8,128)(2,1)S(1)}, u32[]{:S(2)}, u32[]{:S(2)}) collective-permute-start(bf16[256,2048]{1,0:T(8,128)(2,1)S(1)} %split.1), channel_id=1, source_target_pairs={{0,1},{1,0},{2,3},{3,2},{4,5},{5,4},{6,7},{7,6},{8,9},{9,8},{10,11... | collective-permute-start | bytes 3145736 | tf_op jit(solution)/shard_map/ppermute | solution.py:97
  28.6 21.7 %collective-permute-start.8 = (bf16[512,1024]{1,0:T(8,128)(2,1)S(1)}, bf16[512,1024]{1,0:T(8,128)(2,1)S(1)}, u32[]{:S(2)}, u32[]{:S(2)}) collective-permute-start(bf16[512,1024]{1,0:T(8,128)(2,1)S(1)} %collective-permute-done.a_ref.refs_3_), channel_id=1, source_target_pairs={{0,96},{1,17},{2,98},{3,19},{4,100},{5,21},{6,102},{7,23},{8,104},... | collective-permute-start | bytes 3145736 | tf_op jit(solution)/shard_map/ppermute | solution.py:97
  39.9 15.5 %collective-permute-start.10 = (bf16[512,1024]{1,0:T(8,128)(2,1)S(1)}, bf16[512,1024]{1,0:T(8,128)(2,1)S(1)}, u32[]{:S(2)}, u32[]{:S(2)}) collective-permute-start(bf16[512,1024]{1,0:T(8,128)(2,1)S(1)} %pick.3), channel_id=1, source_target_pairs={{0,13},{1,4},{2,15},{3,6},{4,1},{5,8},{6,3},{7,10},{8,5},{9,12},{1... | collective-permute-start | bytes 3145736 | tf_op jit(solution)/shard_map/ppermute | solution.py:97
  40.0 15.5 %collective-permute-start.9 = (bf16[512,1024]{1,0:T(8,128)(2,1)S(1)}, bf16[512,1024]{1,0:T(8,128)(2,1)S(1)}, u32[]{:S(2)}, u32[]{:S(2)}) collective-permute-start(bf16[512,1024]{1,0:T(8,128)(2,1)S(1)} %collective-permute-done.4.refs_3_.b_ref), channel_id=1, source_target_pairs={{0,97},{1,32},{2,99},{3,34},{4,101},{5,36},{6,103},{7,38},{8,105},... | collective-permute-start | bytes 3145736 | tf_op jit(solution)/shard_map/ppermute | solution.py:97
  41.4 16.1 %collective-permute-start.11 = (bf16[512,1024]{1,0:T(8,128)(2,1)S(1)}, bf16[512,1024]{1,0:T(8,128)(2,1)S(1)}, u32[]{:S(2)}, u32[]{:S(2)}) collective-permute-start(bf16[512,1024]{1,0:T(8,128)(2,1)S(1)} %collective-permute-done.5.refs_4_.a_ref), channel_id=1, source_target_pairs={{0,17},{2,19},{4,21},{6,23},{8,25},{10,27},{12,29},{14,31},{17,0},... | collective-permute-start | bytes 3145736 | tf_op jit(solution)/shard_map/ppermute | solution.py:97
  59.0 2.7 %collective-permute-start.12 = (f32[512,512]{1,0:T(8,128)S(1)}, f32[512,512]{1,0:T(8,128)S(1)}, u32[]{:S(2)}, u32[]{:S(2)}) collective-permute-start(f32[512,512]{1,0:T(8,128)S(1)} %finish.3), channel_id=1, source_target_pairs={{0,1},{1,0},{2,3},{3,2},{4,5},{5,4},{6,7},{7,6},{8,9},{9,8},{10,11... | collective-permute-start | bytes 3145736 | tf_op jit(solution)/shard_map/ppermute | solution.py:97
  61.9 12.6 %collective-permute-start.14 = (bf16[512,512]{1,0:T(8,128)(2,1)S(1)}, bf16[512,512]{1,0:T(8,128)(2,1)S(1)}, u32[]{:S(2)}, u32[]{:S(2)}) collective-permute-start(bf16[512,512]{1,0:T(8,128)(2,1)S(1)} %add.122.refs_1_.refs_2_), channel_id=1, source_target_pairs={{0,16},{1,17},{2,18},{3,19},{4,20},{5,21},{6,22},{7,23},{8,24},{9,... | collective-permute-start | bytes 1572872 | tf_op jit(solution)/shard_map/ppermute | solution.py:97
  63.6 15.9 %collective-permute-start.13 = (bf16[512,512]{1,0:T(8,128)(2,1)S(1)}, bf16[512,512]{1,0:T(8,128)(2,1)S(1)}, u32[]{:S(2)}, u32[]{:S(2)}) collective-permute-start(bf16[512,512]{1,0:T(8,128)(2,1)S(1)} %add.122.refs_1_.refs_2_), channel_id=1, source_target_pairs={{0,96},{1,97},{2,98},{3,99},{4,100},{5,101},{6,102},{7,103},{8,104... | collective-permute-start | bytes 1572872 | tf_op jit(solution)/shard_map/ppermute | solution.py:97
  64.9 20.8 %collective-permute-start.17 = (bf16[512,512]{1,0:T(8,128)(2,1)S(1)}, bf16[512,512]{1,0:T(8,128)(2,1)S(1)}, u32[]{:S(2)}, u32[]{:S(2)}) collective-permute-start(bf16[512,512]{1,0:T(8,128)(2,1)S(1)} %add.122.refs_1_.refs_2_), channel_id=1, source_target_pairs={{0,32},{1,33},{2,34},{3,35},{4,36},{5,37},{6,38},{7,39},{8,40},{9,... | collective-permute-start | bytes 1572872 | tf_op jit(solution)/shard_map/ppermute | solution.py:97
  79.5 13.8 %collective-permute-start.15 = (bf16[512,512]{1,0:T(8,128)(2,1)S(1)}, bf16[512,512]{1,0:T(8,128)(2,1)S(1)}, u32[]{:S(2)}, u32[]{:S(2)}) collective-permute-start(bf16[512,512]{1,0:T(8,128)(2,1)S(1)} %collective-permute-done.14.refs_2_.refs_5_), channel_id=1, source_target_pairs={{0,32},{1,33},{2,34},{3,35},{4,36},{5,37},{6,38},{7,39},{8,40},{9,... | collective-permute-start | bytes 1572872 | tf_op jit(solution)/shard_map/ppermute | solution.py:97
  80.8 13.8 %collective-permute-start.16 = (bf16[512,512]{1,0:T(8,128)(2,1)S(1)}, bf16[512,512]{1,0:T(8,128)(2,1)S(1)}, u32[]{:S(2)}, u32[]{:S(2)}) collective-permute-start(bf16[512,512]{1,0:T(8,128)(2,1)S(1)} %collective-permute-done.13.refs_4_.refs_7_), channel_id=1, source_target_pairs={{0,16},{1,17},{2,18},{3,19},{4,20},{5,21},{6,22},{7,23},{8,24},{9,... | collective-permute-start | bytes 1572872 | tf_op jit(solution)/shard_map/ppermute | solution.py:97
  83.5 16.7 %collective-permute-start.20 = (bf16[512,512]{1,0:T(8,128)(2,1)S(1)}, bf16[512,512]{1,0:T(8,128)(2,1)S(1)}, u32[]{:S(2)}, u32[]{:S(2)}) collective-permute-start(bf16[512,512]{1,0:T(8,128)(2,1)S(1)} %collective-permute-done.13.refs_4_.refs_7_), channel_id=1, source_target_pairs={{0,96},{1,97},{2,98},{3,99},{4,100},{5,101},{6,102},{7,103},{8,104... | collective-permute-start | bytes 1572872 | tf_op jit(solution)/shard_map/ppermute | solution.py:97
  94.6 16.0 %collective-permute-start.18 = (bf16[256,512]{1,0:T(8,128)(2,1)S(1)}, bf16[256,512]{1,0:T(8,128)(2,1)S(1)}, u32[]{:S(2)}, u32[]{:S(2)}) collective-permute-start(bf16[256,512]{1,0:T(8,128)(2,1)S(1)} %slice.14), channel_id=1, source_target_pairs={{32,64},{33,65},{34,66},{35,67},{36,68},{37,69},{38,70},{39,71},{4... | collective-permute-start | bytes 786440 | tf_op jit(solution)/shard_map/ppermute | solution.py:97
  95.9 14.7 %collective-permute-start.19 = (bf16[256,512]{1,0:T(8,128)(2,1)S(1)}, bf16[256,512]{1,0:T(8,128)(2,1)S(1)}, u32[]{:S(2)}, u32[]{:S(2)}) collective-permute-start(bf16[256,512]{1,0:T(8,128)(2,1)S(1)} %slice.15), channel_id=1, source_target_pairs={{0,96},{1,97},{2,98},{3,99},{4,100},{5,101},{6,102},{7,103},{8,104... | collective-permute-start | bytes 786440 | tf_op jit(solution)/shard_map/ppermute | solution.py:97
  113.7 7.0 %collective-permute-start.21 = (bf16[256,2048]{1,0:T(8,128)(2,1)S(1)}, bf16[256,2048]{1,0:T(8,128)(2,1)S(1)}, u32[]{:S(2)}, u32[]{:S(2)}) collective-permute-start(bf16[256,2048]{1,0:T(8,128)(2,1)S(1)} %attend_last.2), channel_id=1, source_target_pairs={{0,1},{1,0},{2,3},{3,2},{4,5},{5,4},{6,7},{7,6},{8,9},{9,8},{10,11... | collective-permute-start | bytes 3145736 | tf_op jit(solution)/shard_map/ppermute | solution.py:97
